TPU v7x, 32 devices: a whole 2x2x4 slice. The times are simulated.
32 devices in a mesh: layer: 4 (over z), plane: 8 (over y, x, core).
Axes of the slice: x: 2, y: 2, z: 4, core: 2. Of those that a mesh axis runs over, the one named last changes fastest.
Arguments:
- leaf_rhs: bfloat16 [256, 128, 512], P(('layer', 'plane')), may hold values from -6 to 6
- leaf_inverse: bfloat16 [256, 128, 128], P(('layer', 'plane')), may hold values from -0.5 to 0.5
- leaf_couple: bfloat16 [256, 2, 1024, 128], P(('layer', 'plane')), may hold values from -0.09375 to 0.09375
- couple_mask: int32 [256, 2], P(('layer', 'plane')), may hold values 0 or 1
- leaf_diag: float32 [256, 128], P(('layer', 'plane')), may hold values from 0.5 to 2
- sep_rhs: bfloat16 [3, 1024, 512], P(None, 'plane'), may hold values from -6 to 6
- sep_inverse: bfloat16 [3, 1024, 1024], P(None, 'plane'), may hold values from -0.1875 to 0.1875
- sep_couple: bfloat16 [3, 1, 1024, 1024], P(None, None, 'plane'), may hold values from -0.125 to 0.125
- sep_diag: float32 [3, 1024], P(None, 'plane'), may hold values from 0.5 to 2
Outputs:
- leaf_solution: bfloat16 [256, 128, 512], P(('layer', 'plane'))
- sep_solution: bfloat16 [4, 2, 1024, 512], P('layer', None, 'plane')
All inputs are finite; a program needn't handle non-finite values. No bound on the sum of `couple_mask` on one device may be relied on, other than what follows from the above.
Results may differ from a plain program's by a relative error of at most 0.02.
Values may be sent and summed in bfloat16 or wider, within the bound.
No kernel may reach another device: no remote copies, remote signals or barrier semaphores. Data moves between devices by JAX's collectives and lax.ppermute only.
A program may use at most 128 MiB of HBM per device.

v0:
```python
import jax
import jax.numpy as jnp
from jax import lax
from jax.sharding import PartitionSpec as P


def from_partner(value, axis, stride):
    mask = 2**stride
    pairs = [(source, source ^ mask) for source in range(lax.axis_size(axis))]
    return lax.ppermute(value, axis, pairs)


def lower_unit(block, first_row):
    row_count = block.shape[-2]
    col_count = block.shape[-1]
    row_ids = first_row + lax.broadcasted_iota(jnp.int32, (row_count, col_count), 0)
    col_ids = lax.broadcasted_iota(jnp.int32, (row_count, col_count), 1)
    below = jnp.where(col_ids < row_ids, block, jnp.zeros_like(block))
    return jnp.where(col_ids == row_ids, jnp.ones_like(block), below)


def body(
    leaf_rhs,
    leaf_inverse,
    leaf_couple,
    couple_mask,
    leaf_diag,
    sep_rhs,
    sep_inverse,
    sep_couple,
    sep_diag,
):
    levels = leaf_couple.shape[1]
    layers = lax.axis_size("layer")
    own_rows = sep_rhs.shape[1]
    layer_id = lax.axis_index("layer")
    plane_id = lax.axis_index("plane")
    first_row = plane_id * own_rows
    leaf_lower = lower_unit(leaf_inverse, 0)
    leaf_y = jnp.einsum(
        "bij,bjr->bir", leaf_lower, leaf_rhs, preferred_element_type=jnp.float32
    ).astype(jnp.bfloat16)
    masked = leaf_couple * couple_mask.astype(jnp.bfloat16)[:, :, None, None]
    totals = lax.psum_scatter(
        jnp.einsum("bksc,bcr->skr", masked, leaf_y, preferred_element_type=jnp.float32),
        "plane",
        scatter_dimension=0,
        tiled=True,
    )
    sep_ids = [
        layers - (layers >> level - 1) + jnp.right_shift(layer_id, level)
        for level in range(1, levels + 1)
    ]

    def select_sep(array, level):
        return lax.dynamic_index_in_dim(array, sep_ids[level - 1], 0, keepdims=False)

    inverses = [
        lower_unit(select_sep(sep_inverse, level), first_row) for level in range(1, levels + 1)
    ]
    sep_z = []
    for level in range(1, levels + 1):
        partner = from_partner(totals[:, level - 1 :], "layer", level - 1)
        totals = jnp.concatenate([totals[:, : level - 1], totals[:, level - 1 :] + partner], axis=1)
        residual = (select_sep(sep_rhs, level).astype(jnp.float32) - totals[:, level - 1]).astype(
            jnp.bfloat16
        )
        residual_full = lax.all_gather(residual, "plane", axis=0, tiled=True)
        solved = jnp.dot(
            inverses[level - 1], residual_full, preferred_element_type=jnp.float32
        ).astype(jnp.bfloat16)
        if level < levels:
            solved_full = lax.all_gather(solved, "plane", axis=0, tiled=True)
        if level < levels:
            blocks = select_sep(sep_couple, level)[: levels - level]
            coupling = jnp.einsum(
                "jos,sr->ojr", blocks, solved_full, preferred_element_type=jnp.float32
            )
            totals = jnp.concatenate([totals[:, :level], totals[:, level:] + coupling], axis=1)
        sep_z.append(solved.astype(jnp.float32) / select_sep(sep_diag, level)[:, None])
    answers = [None] * levels
    for level in range(levels, 0, -1):
        if level < levels:
            blocks = select_sep(sep_couple, level)[: levels - level]
            upper_rows = jnp.stack(answers[level:])

            def couple_back(offset_row, row_count, blocks=blocks, upper_rows=upper_rows):
                return jnp.einsum(
                    "jos,jor->sr", blocks, upper_rows, preferred_element_type=jnp.float32
                )

            carried = lax.psum_scatter(
                couple_back(jnp.int32(0), lax.axis_size("plane") * own_rows),
                "plane",
                scatter_dimension=0,
                tiled=True,
            )
            target_now = (sep_z[level - 1] - carried).astype(jnp.bfloat16)
        else:
            target_now = sep_z[level - 1].astype(jnp.bfloat16)
        lower_part = inverses[level - 1]

        def transpose_solve(offset_row, row_count, lower_part=lower_part, target_now=target_now):
            return lax.dot_general(
                lower_part, target_now, (((0,), (0,)), ((), ())), preferred_element_type=jnp.float32
            )

        answers[level - 1] = lax.psum_scatter(
            transpose_solve(jnp.int32(0), lax.axis_size("plane") * own_rows),
            "plane",
            scatter_dimension=0,
            tiled=True,
        ).astype(jnp.bfloat16)
    above = lax.all_gather(jnp.stack(answers), "plane", axis=1, tiled=True)
    back_terms = jnp.einsum("bksc,ksr->bcr", masked, above, preferred_element_type=jnp.float32)
    leaf_target = (leaf_y.astype(jnp.float32) / leaf_diag[:, :, None] - back_terms).astype(
        jnp.bfloat16
    )
    leaf_solution = jnp.einsum(
        "bjc,bjr->bcr", leaf_lower, leaf_target, preferred_element_type=jnp.float32
    ).astype(jnp.bfloat16)
    sep_solution = jnp.stack(answers)[None]
    return (leaf_solution, sep_solution)


def solution(mesh):
    in_specs = (
        P(("layer", "plane"), None, None),
        P(("layer", "plane"), None, None),
        P(("layer", "plane"), None, None, None),
        P(("layer", "plane"), None),
        P(("layer", "plane"), None),
        P(None, "plane", None),
        P(None, "plane", None),
        P(None, None, "plane", None),
        P(None, "plane"),
    )
    out_specs = (P(("layer", "plane"), None, None), P("layer", None, "plane", None))
    return jax.shard_map(body, mesh=mesh, in_specs=in_specs, out_specs=out_specs, check_vma=False)
```

profile of v0, /device:TPU:0, one launch (start us, length us, event | category | flops | bytes accessed | tf_op | source)
XLA Modules:
  0.0 355.6 jit_solution(10957012939890570942)
XLA Ops:
  7.3 0.8 convert_element_type.59
  8.4 1.4 convolution_convert_fusion.1
  9.8 6.6 %fusion.4 = f32[1024,2,512]{0,2,1:T(8,128)} fusion(bf16[8,2,1024,128]{3,2,1,0:T(8,128)(2,1)} %param.11, bf16[8,2]{1,0:T(8,128)(2,1)S(1)} %copy.11, bf16[8,128,512]{2,1,0:T(8,128)(2,1)S(1)} %convolution_convert_fusion.1), kind=kOutput, calls=%fused_computation.4 | convolution fusion | flops 2155872256 | bytes 9437216 | tf_op jit(solution)/shard_map/bksc,bcr->skr/dot_general | solution.py:45
  16.5 54.1 %reduce-scatter.5.cloned.1.call-done = f32[128,2,512]{0,2,1:T(8,128)} async-done(((f32[1024,2,512]{0,2,1:T(8,128)}), f32[128,2,512]{0,2,1:T(8,128)}) %reduce-scatter.5.cloned.1.call-update) | async-done | bytes 524304 | tf_op jit(solution)/shard_map/reduce_scatter | solution.py:44
  70.6 1.5 collective-permute-start
  72.2 12.2 %collective-permute-done = f32[128,2,512]{0,2,1:T(8,128)S(1)} collective-permute-done((f32[128,2,512]{0,2,1:T(8,128)}, f32[128,2,512]{0,2,1:T(8,128)S(1)}, u32[]{:S(2)}, u32[]{:S(2)}) %collective-permute-start) | collective-permute-done | bytes 524320 | tf_op jit(solution)/shard_map/ppermute | solution.py:10
  84.4 1.1 add.50
  86.3 23.7 %all-gather.5.cloned.1.call-done = bf16[1024,512]{0,1:T(8,128)(2,1)} async-done(((bf16[128,512]{0,1:T(8,128)(2,1)}), bf16[1024,512]{0,1:T(8,128)(2,1)}) %all-gather.5.cloned.1.call-update) | async-done | bytes 1048592 | tf_op jit(solution)/shard_map/all_gather | solution.py:68
  110.0 2.5 convolution_convert_fusion.3
  112.5 23.6 %all-gather.7.cloned.1.call-done = bf16[1024,512]{1,0:T(8,128)(2,1)} async-done(((bf16[128,512]{1,0:T(8,128)(2,1)}), bf16[1024,512]{1,0:T(8,128)(2,1)}) %all-gather.7.cloned.1.call-update) | async-done | bytes 1048592 | tf_op jit(solution)/shard_map/all_gather | solution.py:73
  136.1 1.7 slice_add_fusion
  137.9 2.5 collective-permute-start.1
  140.5 12.5 %collective-permute-done.1 = f32[128,1,512]{0,2,1:T(8,128)S(1)} collective-permute-done((f32[128,1,512]{0,2,1:T(8,128)S(1)}, f32[128,1,512]{0,2,1:T(8,128)S(1)}, u32[]{:S(2)}, u32[]{:S(2)}) %collective-permute-start.1) | collective-permute-done | bytes 262176 | tf_op jit(solution)/shard_map/ppermute | solution.py:10
  153.7 23.6 %all-gather.9.cloned.1.call-done = bf16[1024,512]{0,1:T(8,128)(2,1)} async-done(((bf16[128,512]{0,1:T(8,128)(2,1)}), bf16[1024,512]{0,1:T(8,128)(2,1)}) %all-gather.9.cloned.1.call-update) | async-done | bytes 1048592 | tf_op jit(solution)/shard_map/all_gather | solution.py:68
  177.4 3.7 %fusion.22 = f32[1024,512]{1,0:T(8,128)} fusion(bf16[1024,512]{0,1:T(8,128)(2,1)} %all-gather.9.cloned.1.call-done, bf16[3,128,1024]{2,1,0:T(8,128)(2,1)} %param.15, s32[]{:T(128)S(6)} %select_n.41, s32[128]{0:T(128)S(1)} %iota_add_fusion, f32[128]{0:T(128)S(1)} %get-tuple-element.7), kind=kOutput, calls=%fused_computation.18 | convolution fusion | flops 269746176 | bytes 3672576 | tf_op jit(solution)/shard_map/dot_general | solution.py:104
  181.1 41.3 %reduce-scatter.7.cloned.1.call-done = f32[128,512]{1,0:T(8,128)} async-done(((f32[1024,512]{1,0:T(8,128)}), f32[128,512]{1,0:T(8,128)}) %reduce-scatter.7.cloned.1.call-update) | async-done | bytes 262160 | tf_op jit(solution)/shard_map/reduce_scatter | solution.py:108
  222.4 2.8 fusion.38
  225.3 41.5 %reduce-scatter.9.cloned.1.call-done = f32[128,512]{1,0:T(8,128)} async-done(((f32[1024,512]{1,0:T(8,128)}), f32[128,512]{1,0:T(8,128)}) %reduce-scatter.9.cloned.1.call-update) | async-done | bytes 262160 | tf_op jit(solution)/shard_map/reduce_scatter | solution.py:92
  266.8 3.0 fusion.49
  269.9 41.8 %reduce-scatter.11.cloned.1.call-done = f32[128,512]{1,0:T(8,128)} async-done(((f32[1024,512]{1,0:T(8,128)}), f32[128,512]{1,0:T(8,128)}) %reduce-scatter.11.cloned.1.call-update) | async-done | bytes 262160 | tf_op jit(solution)/shard_map/reduce_scatter | solution.py:108
  311.7 1.0 convert_bitcast_fusion
  312.7 0.8 fusion.77
  313.5 28.6 %all-gather.11.cloned.1.call-done = bf16[2,1024,512]{2,1,0:T(8,128)(2,1)} async-done(((bf16[2,128,512]{2,1,0:T(8,128)(2,1)}), bf16[2,1024,512]{2,1,0:T(8,128)(2,1)}) %all-gather.11.cloned.1.call-update) | async-done | bytes 2097168 | tf_op jit(solution)/shard_map/all_gather | solution.py:114
  342.1 6.7 %convolution_convert_fusion = bf16[8,128,512]{2,1,0:T(8,128)(2,1)} fusion(bf16[8,128,512]{2,1,0:T(8,128)(2,1)S(1)} %convolution_convert_fusion.1, bf16[2,1024,512]{2,1,0:T(8,128)(2,1)} %all-gather.11.cloned.1.call-done, bf16[8,2,1024,128]{3,2,1,0:T(8,128)(2,1)} %param.11, bf16[8,2]{1,0:T(8,128)(2,1)S(1)} %copy.11, f32[8,128]{1,0:T(8,128)S(1)} %copy-done.6, ...), kind=kOutput, calls=%fused_computation.10 | convolution fusion | flops 2286682112 | bytes 8687648 | tf_op jit(solution)/shard_map/bjc,bjr->bcr/dot_general | solution.py:119
  (40 shorter events, 2.6 us)
Async XLA Ops:
  7.2 1.2 copy-start
  7.2 63.4 %reduce-scatter.5.cloned.1.call-start = ((), (), s32[]{:S(2)}) async-start(), calls=%async_computation.4 | async-start | bytes 4718592 | tf_op jit(solution)/shard_map/reduce_scatter | solution.py:44
  16.4 55.7 %copy-start.4 = (bf16[3,128,512]{2,1,0:T(8,128)(2,1)S(1)}, bf16[3,128,512]{2,1,0:T(8,128)(2,1)}, u32[]{:S(2)}) copy-start(bf16[3,128,512]{2,1,0:T(8,128)(2,1)} %param.14) | copy-start | bytes 1179652
  16.4 93.6 %all-gather.5.cloned.1.call-start = ((), (), s32[]{:S(2)}) async-start(), calls=%async_computation.5 | async-start | bytes 1179648 | tf_op jit(solution)/shard_map/all_gather | solution.py:68
  70.6 13.9 %collective-permute-start = (f32[128,2,512]{0,2,1:T(8,128)}, f32[128,2,512]{0,2,1:T(8,128)S(1)}, u32[]{:S(2)}, u32[]{:S(2)}) collective-permute-start(f32[128,2,512]{0,2,1:T(8,128)} %reduce-scatter.5.cloned.1.call-done), channel_id=1, source_target_pairs={{0,8},{8,0},{16,24},{24,16},{1,9},{9,1},{17,25},{25,17},{2,10},{10... | collective-permute-start | bytes 1572872 | tf_op jit(solution)/shard_map/ppermute | solution.py:10
  86.2 49.9 %all-gather.7.cloned.1.call-start = ((), (), s32[]{:S(2)}) async-start(), calls=%async_computation.6 | async-start | bytes 1179648 | tf_op jit(solution)/shard_map/all_gather | solution.py:73
  86.3 67.4 %copy-start.5 = (f32[3,128]{1,0:T(4,128)S(1)}, f32[3,128]{1,0:T(4,128)}, u32[]{:S(2)}) copy-start(f32[3,128]{1,0:T(4,128)} %param.17) | copy-start | bytes 4612
  112.5 64.9 %all-gather.9.cloned.1.call-start = ((), (), s32[]{:S(2)}) async-start(), calls=%async_computation.7 | async-start | bytes 1179648 | tf_op jit(solution)/shard_map/all_gather | solution.py:68
  137.9 15.1 %collective-permute-start.1 = (f32[128,1,512]{0,2,1:T(8,128)S(1)}, f32[128,1,512]{0,2,1:T(8,128)S(1)}, u32[]{:S(2)}, u32[]{:S(2)}) collective-permute-start(f32[128,1,512]{0,2,1:T(8,128)S(1)} %slice_add_fusion), channel_id=1, source_target_pairs={{0,16},{8,24},{16,0},{24,8},{1,17},{9,25},{17,1},{25,9},{2,18},{10... | collective-permute-start | bytes 786440 | tf_op jit(solution)/shard_map/ppermute | solution.py:10
  153.7 68.8 %reduce-scatter.7.cloned.1.call-start = ((), (), s32[]{:S(2)}) async-start(), calls=%async_computation.8 | async-start | bytes 2359296 | tf_op jit(solution)/shard_map/reduce_scatter | solution.py:108
  181.1 85.8 %copy-start.2 = (bf16[128,512]{1,0:T(8,128)(2,1)S(1)}, bf16[128,512]{1,0:T(8,128)(2,1)}, u32[]{:S(2)}) copy-start(bf16[128,512]{1,0:T(8,128)(2,1)} %convolution_convert_fusion.3) | copy-start | bytes 393220
  181.1 85.7 %reduce-scatter.9.cloned.1.call-start = ((), (), s32[]{:S(2)}) async-start(), calls=%async_computation.9 | async-start | bytes 2359296 | tf_op jit(solution)/shard_map/reduce_scatter | solution.py:92
  225.3 86.4 %reduce-scatter.11.cloned.1.call-start = ((), (), s32[]{:S(2)}) async-start(), calls=%async_computation.10 | async-start | bytes 2359296 | tf_op jit(solution)/shard_map/reduce_scatter | solution.py:108
  266.8 3.1 copy-start.1
  269.8 72.3 %copy-start.3 = (bf16[8,128,128]{2,1,0:T(8,128)(2,1)S(1)}, bf16[8,128,128]{2,1,0:T(8,128)(2,1)}, u32[]{:S(2)}) copy-start(bf16[8,128,128]{2,1,0:T(8,128)(2,1)} %param.10) | copy-start | bytes 786436
  269.8 72.3 %copy-start.6 = (f32[8,128]{1,0:T(8,128)S(1)}, f32[8,128]{1,0:T(8,128)}, u32[]{:S(2)}) copy-start(f32[8,128]{1,0:T(8,128)} %param.13) | copy-start | bytes 12292
  269.8 72.2 %all-gather.11.cloned.1.call-start = ((), (), s32[]{:S(2)}) async-start(), calls=%async_computation.11 | async-start | bytes 2359296 | tf_op jit(solution)/shard_map/all_gather | solution.py:114
Sparse Core Ops, SparseCore 0:
  16.5 53.9 reduce-scatter.4
  86.4 23.5 all-gather.4
  112.6 23.4 all-gather.6
  153.8 23.5 all-gather.8
  181.2 41.2 reduce-scatter.6
  225.6 41.1 reduce-scatter.8
  270.4 41.2 reduce-scatter.10
  314.2 27.8 all-gather.10
where the time goes:
time: 356 us
  waiting for transfers between devices  303 us (85%)
  matrix products  28.3 us (8%)
  between operations  14.3 us (4%)
  other arithmetic  5.07 us (1%)
  starting transfers between devices  4.28 us (1%)
    reduce_scatter x2, waiting for transfers between devices, body(): lax.psum_scatter(transpose_solve(jnp.int32(0), lax.axis_size('plane') * o...  83.1 us
    reduce_scatter x1, waiting for transfers between devices, body(): lax.psum_scatter(jnp.einsum('bksc,bcr->skr', masked, leaf_y, preferred_el...  54.1 us
    all_gather x2, waiting for transfers between devices, body(): residual_full = lax.all_gather(residual, 'plane', axis=0, tiled=True)  47.3 us
    reduce_scatter x1, waiting for transfers between devices, body(): lax.psum_scatter(couple_back(jnp.int32(0), lax.axis_size('plane') * own_r...  41.5 us
    all_gather x1, waiting for transfers between devices, body(): above = lax.all_gather(jnp.stack(answers), 'plane', axis=1, tiled=True)  28.6 us
    ppermute x2, waiting for transfers between devices, from_partner(): return lax.ppermute(value, axis, pairs)  24.7 us
    all_gather x1, waiting for transfers between devices, body(): solved_full = lax.all_gather(solved, 'plane', axis=0, tiled=True)  23.6 us
  transfers between devices with their start and end apart: 10, of which 10 were waited for; matrix products, arithmetic and copies ran while one was open for 0% of the time, Pallas kernels for 0%

commit v1 on v0

v1 whole, which is shorter than its diff:
```python
import jax
import jax.numpy as jnp
import numpy as np
from jax import lax
from jax.sharding import PartitionSpec as P

F32 = jnp.float32
BF16 = jnp.bfloat16


def bit_orders(planes):
    link_bits = list(range(1, planes.bit_length() - 1))
    turn = len(link_bits) // 2
    return [link_bits, link_bits[turn:] + link_bits[:turn]]


def slot_table(planes):
    orders = bit_orders(planes)
    count = len(orders[0])
    table = np.zeros((planes, planes), np.int32)
    for device in range(planes):
        for slot in range(planes):
            other = slot >> count
            order = orders[(device & 1) ^ other]
            block = device ^ other
            for place, bit in enumerate(order):
                if slot >> (count - 1 - place) & 1:
                    block ^= 1 << bit
            table[device, slot] = block
    return table


def swap_core(value):
    planes = lax.axis_size("plane")
    return lax.ppermute(value, "plane", [(i, i ^ 1) for i in range(planes)])


def swap_link(value, place):
    planes = lax.axis_size("plane")
    orders = bit_orders(planes)
    return lax.ppermute(value, "plane", [(i, i ^ (1 << orders[i & 1][place])) for i in range(planes)])


def swap_layer(value, stride):
    layers = lax.axis_size("layer")
    return lax.ppermute(value, "layer", [(i, i ^ (1 << stride)) for i in range(layers)])


def scatter_sum(value):
    planes = lax.axis_size("plane")
    half = planes // 2
    value = (value[:half].astype(F32) + swap_core(value[half:]).astype(F32)).astype(BF16)
    for place in range(len(bit_orders(planes)[0])):
        half //= 2
        value = (value[:half].astype(F32) + swap_link(value[half:], place).astype(F32)).astype(BF16)
    return value[0]


def gather(value):
    planes = lax.axis_size("plane")
    value = value[None]
    for place in reversed(range(len(bit_orders(planes)[0]))):
        value = jnp.concatenate([value, swap_link(value, place)], axis=0)
    return jnp.concatenate([value, swap_core(value)], axis=0)


def reorder(value, indices, axis):
    pieces = [
        lax.dynamic_index_in_dim(value, indices[i], axis, keepdims=True)
        for i in range(value.shape[axis])
    ]
    return jnp.concatenate(pieces, axis=axis)


def lower_unit(block, first_row):
    row_count = block.shape[-2]
    col_count = block.shape[-1]
    row_ids = first_row + lax.broadcasted_iota(jnp.int32, (row_count, col_count), 0)
    col_ids = lax.broadcasted_iota(jnp.int32, (row_count, col_count), 1)
    below = jnp.where(col_ids < row_ids, block, jnp.zeros_like(block))
    return jnp.where(col_ids == row_ids, jnp.ones_like(block), below)


def body(
    leaf_rhs,
    leaf_inverse,
    leaf_couple,
    couple_mask,
    leaf_diag,
    sep_rhs,
    sep_inverse,
    sep_couple,
    sep_diag,
):
    levels = leaf_couple.shape[1]
    planes = lax.axis_size("plane")
    layers = lax.axis_size("layer")
    own_rows = sep_rhs.shape[1]
    sep_rows = own_rows * planes
    rhs_cols = sep_rhs.shape[2]
    cols = rhs_cols // planes
    layer_id = lax.axis_index("layer")
    me = lax.axis_index("plane")
    first_row = me * own_rows
    table = slot_table(planes)
    inverse_table = np.argsort(table, axis=1).astype(np.int32)
    slot_block = lax.dynamic_index_in_dim(jnp.asarray(table), me, 0, keepdims=False)
    block_slot = lax.dynamic_index_in_dim(jnp.asarray(inverse_table), me, 0, keepdims=False)
    sep_ids = [
        layers - (layers >> level - 1) + jnp.right_shift(layer_id, level)
        for level in range(1, levels + 1)
    ]

    def select_sep(array, level):
        return lax.dynamic_index_in_dim(array, sep_ids[level - 1], 0, keepdims=False)

    mats = []
    for level in range(1, levels + 1):
        mats.append(lower_unit(select_sep(sep_inverse, level), first_row)[None])
        if level < levels:
            mats.append(select_sep(sep_couple, level)[: levels - level])
    sizes = [m.shape[0] for m in mats]
    full = gather(jnp.concatenate(mats, axis=0))
    inverses, couples, at = [], [], 0
    for level in range(1, levels + 1):
        inverses.append(full[:, at])
        at += 1
        if level < levels:
            couples.append(full[:, at : at + levels - level])
            at += levels - level
    diag_full = lax.all_gather(sep_diag, "plane", axis=1, tiled=True)

    leaf_lower = lower_unit(leaf_inverse, 0)
    leaf_y = jnp.einsum("bij,bjr->rbi", leaf_lower, leaf_rhs, preferred_element_type=F32).astype(BF16)
    masked = leaf_couple * couple_mask.astype(BF16)[:, :, None, None]
    partial = jnp.einsum("rbc,bksc->rks", leaf_y, masked, preferred_element_type=F32)
    partial = partial.reshape(planes, cols, levels, planes, own_rows)
    for level in range(1, levels + 1):
        first = (jnp.bitwise_and(layer_id, (1 << level) - 1) == 0).astype(F32)
        term = select_sep(sep_rhs, level).astype(F32).T.reshape(planes, cols, own_rows) * first
        chosen = (jnp.arange(planes) == me).astype(F32)
        partial = partial.at[:, :, level - 1].add(-term[:, :, None, :] * chosen[:, None])
    partial = partial.astype(BF16).reshape(planes, cols, levels, sep_rows)
    partial = reorder(partial, slot_block, 0)
    sums = scatter_sum(partial).astype(F32)
    sums = [sums[:, level] for level in range(levels)]

    def rows_times(matrix, vector):
        out = jnp.einsum("rs,pos->rpo", vector, matrix, preferred_element_type=F32)
        return reorder(out, block_slot, 1).reshape(cols, sep_rows)

    def times_rows(vector, matrix):
        parts = reorder(vector.reshape(cols, planes, own_rows), slot_block, 1)
        return jnp.einsum("rpo,pos->rs", parts, matrix, preferred_element_type=F32)

    sep_z = []
    for level in range(1, levels + 1):
        for upper in range(level - 1, levels):
            theirs = swap_layer(sums[upper].astype(BF16), level - 1).astype(F32)
            sums[upper] = sums[upper] + theirs
        residual = (-sums[level - 1]).astype(BF16)
        solved = rows_times(inverses[level - 1], residual).astype(BF16)
        for slot in range(levels - level):
            sums[level + slot] = sums[level + slot] + rows_times(couples[level - 1][:, slot], solved)
        sep_z.append(solved.astype(F32) / select_sep(diag_full, level)[None])
    answers = [None] * levels
    everywhere = [None] * levels
    for level in range(levels, 0, -1):
        target = sep_z[level - 1]
        for slot in range(levels - level):
            target = target - times_rows(answers[level + slot], couples[level - 1][:, slot])
        answers[level - 1] = times_rows(target.astype(BF16), inverses[level - 1]).astype(BF16)
        everywhere[level - 1] = gather(answers[level - 1])

    above = reorder(jnp.stack(everywhere, axis=2), block_slot, 0).reshape(rhs_cols, levels, sep_rows)
    back = jnp.einsum("rks,bksc->rbc", above, masked, preferred_element_type=F32)
    target = (leaf_y.astype(F32) / leaf_diag[None] - back).astype(BF16)
    leaf_solution = jnp.einsum("bjc,rbj->bcr", leaf_lower, target, preferred_element_type=F32).astype(BF16)
    mine = lax.dynamic_slice_in_dim(above, first_row, own_rows, 2)
    sep_solution = jnp.transpose(mine, (1, 2, 0))[None]
    return (leaf_solution, sep_solution)


def solution(mesh):
    in_specs = (
        P(("layer", "plane"), None, None),
        P(("layer", "plane"), None, None),
        P(("layer", "plane"), None, None, None),
        P(("layer", "plane"), None),
        P(("layer", "plane"), None),
        P(None, "plane", None),
        P(None, "plane", None),
        P(None, None, "plane", None),
        P(None, "plane"),
    )
    out_specs = (P(("layer", "plane"), None, None), P("layer", None, "plane", None))
    return jax.shard_map(body, mesh=mesh, in_specs=in_specs, out_specs=out_specs, check_vma=False)
```

time: 356 us -> 144 us (0.40)
  waiting for transfers between devices: 303 us -> 25.2 us
  other arithmetic: 5.07 us -> 24.6 us
  local copies, waits for them, and re-layouts: 0.69 us -> 18.8 us
  between operations: 14.3 us -> 31.4 us
  starting transfers between devices: 4.28 us -> 16.9 us
  matrix products: 28.3 us -> 16.7 us
  blocking collectives: 0 us -> 9.02 us
    reduce_scatter x4 -> x0, waiting for transfers between devices: 179 us -> none  [the longest x2 83.1 us: body(): lax.psum_scatter(transpose_solve(jnp.int32(0), lax.axis_size('plane') * o...]
    all_gather x4 -> x0, waiting for transfers between devices: 99.5 us -> none  [the longest x2 47.3 us: body(): residual_full = lax.all_gather(residual, 'plane', axis=0, tiled=True)]
    ppermute x2 -> x15, starting transfers between devices: 3.95 us -> 16.9 us  [the longest x8 11.5 us: swap_link(): lax.ppermute(value, 'plane', [(i, i ^ 1 << orders[i & 1][place]) for i in...]
    dot_general x8 -> x9, matrix products: 28.3 us -> 16.7 us  [the longest x1 6.68 us: body(): jnp.einsum('bjc,rbj->bcr', leaf_lower, target, preferred_element_type=F32)]
    all_gather x0 -> x1, blocking collectives: none -> 9.02 us  [body(): diag_full = lax.all_gather(sep_diag, 'plane', axis=1, tiled=True)]
    concatenate x0 -> x9, other arithmetic: none -> 8.38 us  [the longest x6 5 us: gather(): value = jnp.concatenate([value, swap_link(value, place)], axis=0)]
    unnamed x16 -> x83, local copies, waits for them, and re-layouts: 0.57 us -> 8.68 us
    scatter-add x0 -> x2, other arithmetic: none -> 6.54 us  [body(): partial.at[:, :, level - 1].add(-term[:, :, None, :] * chosen[:, None])]
  transfers between devices with their start and end apart: 10 -> 15, of which waited for: 10 -> 7; matrix products, arithmetic and copies ran while one was open for 0% -> 25% of each run, Pallas kernels for 0% -> 0%
where the time goes in v1:
time: 144 us; the launch traced here: 143 us
  between operations  31.4 us (22%)
  waiting for transfers between devices  25.2 us (18%)
  other arithmetic  24.6 us (17%)
  local copies, waits for them, and re-layouts  18.8 us (13%)
  starting transfers between devices  16.9 us (12%)
  matrix products  16.7 us (12%)
  blocking collectives  9.02 us (6%)
    ppermute x8, waiting for transfers between devices, swap_link(): lax.ppermute(value, 'plane', [(i, i ^ 1 << orders[i & 1][place]) for i in...  17 us
    ppermute x8, starting transfers between devices, swap_link(): lax.ppermute(value, 'plane', [(i, i ^ 1 << orders[i & 1][place]) for i in...  11.5 us
    all_gather x1, blocking collectives, body(): diag_full = lax.all_gather(sep_diag, 'plane', axis=1, tiled=True)  9.02 us
    unnamed x83, local copies, waits for them, and re-layouts  8.68 us
    ppermute x4, waiting for transfers between devices, swap_core(): return lax.ppermute(value, 'plane', [(i, i ^ 1) for i in range(planes)])  7.04 us
    dot_general x1, matrix products, body(): jnp.einsum('bjc,rbj->bcr', leaf_lower, target, preferred_element_type=F32)  6.68 us
    scatter-add x2, other arithmetic, body(): partial.at[:, :, level - 1].add(-term[:, :, None, :] * chosen[:, None])  6.54 us
    dot_general x3, matrix products, rows_times(): out = jnp.einsum('rs,pos->rpo', vector, matrix, preferred_element_type=F32)  5.62 us
  transfers between devices with their start and end apart: 15, of which 7 were waited for; matrix products, arithmetic and copies ran while one was open for 25% of the time, Pallas kernels for 0%

profile of v1, /device:TPU:0, one launch (start us, length us, event | category | flops | bytes accessed | tf_op | source)
XLA Modules:
  0.0 142.5 jit_solution(136362168911202297)
XLA Ops:
  3.1 3.0 %collective-permute-start.4 = (bf16[1,3,128,1024]{3,2,0,1:T(8,128)(2,1)S(1)}, bf16[1,3,128,1024]{3,2,0,1:T(8,128)(2,1)S(1)}, u32[]{:S(2)}, u32[]{:S(2)}) collective-permute-start(bf16[1,3,128,1024]{3,2,0,1:T(8,128)(2,1)S(1)} %maximum_bitcast_fusion.2), channel_id=1, source_target_pairs={{0,4},{1,3},{2,6},{3,1},{4,0},{5,7},{6,2},{7,5},{8,12},{9,11},{10,... | collective-permute-start | bytes 2359304 | tf_op jit(solution)/shard_map/ppermute | solution.py:41
  20.5 1.5 %collective-permute-start.5 = (bf16[2,3,128,1024]{3,2,0,1:T(8,128)(2,1)}, bf16[2,3,128,1024]{3,2,0,1:T(8,128)(2,1)}, u32[]{:S(2)}, u32[]{:S(2)}) collective-permute-start(bf16[2,3,128,1024]{3,2,0,1:T(8,128)(2,1)} %pad_maximum_fusion.2), channel_id=1, source_target_pairs={{0,2},{1,5},{2,0},{3,7},{4,6},{5,1},{6,4},{7,3},{8,10},{9,13},{10,... | collective-permute-start | bytes 4718600 | tf_op jit(solution)/shard_map/ppermute | solution.py:41
  22.0 2.5 %fusion.2 = f32[512,2,1024,1]{2,0,1,3:T(8,128)S(1)} fusion(bf16[8,2,1024,128]{3,2,1,0:T(8,128)(2,1)S(1)} %copy-done.14, bf16[8,2]{1,0:T(8,128)(2,1)S(1)} %copy.38, bf16[8,128,512]{2,1,0:T(8,128)(2,1)S(1)} %convolution_convert_fusion.1), kind=kOutput, calls=%fused_computation.19 | convolution fusion | flops 2155872256 | bytes 9437216 | tf_op jit(solution)/shard_map/rbc,bksc->rks/dot_general | solution.py:136
  24.5 3.0 %copy.101 = f32[128,8,8,128]{3,2,1,0:T(8,128)} copy(f32[128,8,8,128]{3,1,2,0:T(8,128)S(1)} %bitcast.202) | data formatting | bytes 8388608
  27.7 3.3 %fusion.5 = f32[8,64,2,8,128]{4,3,1,0,2:T(8,128)} fusion(f32[8,64,2,8,128]{4,3,1,0,2:T(8,128)} %bitcast.201, f32[8]{0:T(128)S(1)} %compare_convert_fusion, f32[8,64,128]{2,1,0:T(8,128)S(1)} %bitcast.210), kind=kLoop, calls=%fused_computation.28 | loop fusion | flops 1048576 | bytes 4456480 | tf_op jit(solution)/shard_map/scatter-add | solution.py:142
  31.0 3.2 %fusion.4 = f32[8,64,2,8,128]{4,3,1,0,2:T(8,128)} fusion(f32[8,64,2,8,128]{4,3,1,0,2:T(8,128)} %fusion.5, f32[8,64,128]{2,1,0:T(8,128)S(1)} %bitcast.211, f32[8]{0:T(128)S(1)} %compare_convert_fusion), kind=kLoop, calls=%fused_computation.26 | loop fusion | flops 1048576 | bytes 4456480 | tf_op jit(solution)/shard_map/scatter-add | solution.py:142
  34.2 3.9 %convert_element_type.145 = bf16[8,64,2,8,128]{4,3,1,0,2:T(8,128)(2,1)} convert(f32[8,64,2,8,128]{4,3,1,0,2:T(8,128)} %fusion.4) | non-fusion elementwise | flops 1048576 | bytes 6291456 | tf_op jit(solution)/shard_map/convert_element_type | solution.py:143
  38.2 4.2 %reshape.264 = bf16[8,64,2,1024]{3,1,0,2:T(8,128)(2,1)} reshape(bf16[8,64,2,8,128]{4,3,1,0,2:T(8,128)(2,1)} %convert_element_type.145) | data formatting | bytes 4194304 | tf_op jit(solution)/shard_map/reshape | solution.py:143
  47.3 3.5 %pad_maximum_fusion.1 = bf16[4,3,128,1024]{3,2,0,1:T(8,128)(2,1)} fusion(bf16[2,3,128,1024]{3,2,0,1:T(8,128)(2,1)} %collective-permute-done.5, bf16[1,3,128,1024]{3,2,0,1:T(8,128)(2,1)S(1)} %collective-permute-done.4, bf16[1,3,128,1024]{3,2,0,1:T(8,128)(2,1)S(1)} %maximum_bitcast_fusion.2), kind=kLoop, calls=%fused_computation.21 | loop fusion | flops 3145728 | bytes 6291456 | tf_op jit(solution)/shard_map/concatenate | solution.py:63
  51.9 6.2 %collective-permute-done = bf16[4,64,2,1024]{3,1,2,0:T(8,128)(2,1)S(1)} collective-permute-done((bf16[4,64,2,1024]{3,1,2,0:T(8,128)(2,1)S(1)}, bf16[4,64,2,1024]{3,1,2,0:T(8,128)(2,1)S(1)}, u32[]{:S(2)}, u32[]{:S(2)}) %collective-permute-start) | collective-permute-done | bytes 1048608 | tf_op jit(solution)/shard_map/ppermute | solution.py:35
  60.0 7.8 %collective-permute-done.1 = bf16[2,64,2,1024]{3,1,2,0:T(8,128)(2,1)S(1)} collective-permute-done((bf16[2,64,2,1024]{3,1,2,0:T(8,128)(2,1)S(1)}, bf16[2,64,2,1024]{3,1,2,0:T(8,128)(2,1)S(1)}, u32[]{:S(2)}, u32[]{:S(2)}) %collective-permute-start.1) | collective-permute-done | bytes 524320 | tf_op jit(solution)/shard_map/ppermute | solution.py:41
  87.0 1.6 %collective-permute-start.3 = (bf16[64,1024]{1,0:T(8,128)(2,1)S(1)}, bf16[64,1024]{1,0:T(8,128)(2,1)S(1)}, u32[]{:S(2)}, u32[]{:S(2)}) collective-permute-start(bf16[64,1024]{1,0:T(8,128)(2,1)S(1)} %get-tuple-element.37), channel_id=1, source_target_pairs={{0,8},{8,0},{16,24},{24,16},{1,9},{9,1},{17,25},{25,17},{2,10},{10... | collective-permute-start | bytes 393224 | tf_op jit(solution)/shard_map/ppermute | solution.py:46
  89.0 3.2 %pad_maximum_fusion = bf16[8,3,128,1024]{3,2,0,1:T(8,128)(2,1)S(1)} fusion(bf16[4,3,128,1024]{3,2,0,1:T(8,128)(2,1)} %collective-permute-done.6, bf16[2,3,128,1024]{3,2,0,1:T(8,128)(2,1)} %collective-permute-done.5, bf16[1,3,128,1024]{3,2,0,1:T(8,128)(2,1)S(1)} %collective-permute-done.4, bf16[1,3,128,1024]{3,2,0,1:T(8,128)(2,1)S(1)} %maximum_bitcast_fusion.2), kind=kLoop, calls=%fused_computation | loop fusion | flops 9437184 | bytes 12582912 | tf_op jit(solution)/shard_map/concatenate | solution.py:64
  93.4 1.5 %copy-done.1 = bf16[8,3,128,1024]{3,2,0,1:T(8,128)(2,1)} copy-done((bf16[8,3,128,1024]{3,2,0,1:T(8,128)(2,1)}, bf16[8,3,128,1024]{3,2,0,1:T(8,128)(2,1)S(1)}, u32[]{:S(2)}) %copy-start.1) | copy-done | bytes 6291480
  96.0 2.5 %fusion.12 = f32[64,8,128]{2,0,1:T(8,128)S(1)} fusion(bf16[64,1024,1]{1,0,2:T(8,128)(2,1)S(1)} %reshape.257, bf16[8,3,128,1024]{3,2,0,1:T(8,128)(2,1)} %copy-done.1), kind=kOutput, calls=%fused_computation.37 | convolution fusion | flops 134217728 | bytes 2490368 | tf_op jit(solution)/shard_map/rs,pos->rpo/dot_general | solution.py:149
  98.7 2.7 %collective-permute-start.8 = (bf16[64,1024]{1,0:T(8,128)(2,1)S(1)}, bf16[64,1024]{1,0:T(8,128)(2,1)S(1)}, u32[]{:S(2)}, u32[]{:S(2)}) collective-permute-start(bf16[64,1024]{1,0:T(8,128)(2,1)S(1)} %fusion.63), channel_id=1, source_target_pairs={{0,16},{8,24},{16,0},{24,8},{1,17},{9,25},{17,1},{25,9},{2,18},{10... | collective-permute-start | bytes 393224 | tf_op jit(solution)/shard_map/ppermute | solution.py:46
  101.4 9.0 %all_gather.3 = f32[3,1024]{1,0:T(4,128)S(1)} all-gather(f32[3,128]{1,0:T(4,128)S(1)} %copy-done.11), channel_id=1, replica_groups=mesh['layer'=4,'plane'=8] {'plane'}, dimensions={1}, use_global_device_ids=true | all-gather | bytes 13824 | tf_op jit(solution)/shard_map/all_gather | solution.py:131
  110.4 2.4 %fusion.14 = bf16[64,8,128]{2,0,1:T(8,128)(2,1)S(1)} fusion(bf16[8,3,128,1024]{3,2,0,1:T(8,128)(2,1)} %copy-done.1, bf16[64,1024]{1,0:T(8,128)(2,1)S(1)} %collective-permute-done.8, bf16[64,1024]{1,0:T(8,128)(2,1)S(1)} %collective-permute-done.7, f32[64,2,1024]{2,0,1:T(8,128)S(1)} %fusion.52, f32[64,8,128]{2,0,1:T(8,128)S(1)} %constant_dynamic-update-slice_fusion.8), kind=kOutput, calls=%fused_computation.39 | convolution fusion | flops 134676480 | bytes 3014656 | tf_op jit(solution)/shard_map/rs,pos->rpo/dot_general | solution.py:149
  115.6 1.4 %collective-permute-start.9 = (bf16[1,64,1024]{2,1,0:T(8,128)(2,1)S(1)}, bf16[1,64,1024]{2,1,0:T(8,128)(2,1)S(1)}, u32[]{:S(2)}, u32[]{:S(2)}) collective-permute-start(bf16[1,64,1024]{2,1,0:T(8,128)(2,1)S(1)} %fusion.27), channel_id=1, source_target_pairs={{0,4},{1,3},{2,6},{3,1},{4,0},{5,7},{6,2},{7,5},{8,12},{9,11},{10,... | collective-permute-start | bytes 393224 | tf_op jit(solution)/shard_map/ppermute | solution.py:41
  117.7 2.9 %collective-permute-done.9 = bf16[1,64,1024]{2,1,0:T(8,128)(2,1)S(1)} collective-permute-done((bf16[1,64,1024]{2,1,0:T(8,128)(2,1)S(1)}, bf16[1,64,1024]{2,1,0:T(8,128)(2,1)S(1)}, u32[]{:S(2)}, u32[]{:S(2)}) %collective-permute-start.9) | collective-permute-done | bytes 131104 | tf_op jit(solution)/shard_map/ppermute | solution.py:41
  120.7 1.4 %collective-permute-start.10 = (bf16[2,64,1024]{2,1,0:T(8,128)(2,1)S(1)}, bf16[2,64,1024]{2,1,0:T(8,128)(2,1)S(1)}, u32[]{:S(2)}, u32[]{:S(2)}) collective-permute-start(bf16[2,64,1024]{2,1,0:T(8,128)(2,1)S(1)} %pad_maximum_fusion.6), channel_id=1, source_target_pairs={{0,2},{1,5},{2,0},{3,7},{4,6},{5,1},{6,4},{7,3},{8,10},{9,13},{10,... | collective-permute-start | bytes 786440 | tf_op jit(solution)/shard_map/ppermute | solution.py:41
  123.5 3.6 %collective-permute-done.10 = bf16[2,64,1024]{2,1,0:T(8,128)(2,1)S(1)} collective-permute-done((bf16[2,64,1024]{2,1,0:T(8,128)(2,1)S(1)}, bf16[2,64,1024]{2,1,0:T(8,128)(2,1)S(1)}, u32[]{:S(2)}, u32[]{:S(2)}) %collective-permute-start.10) | collective-permute-done | bytes 262176 | tf_op jit(solution)/shard_map/ppermute | solution.py:41
  127.2 2.7 %collective-permute-done.13 = bf16[2,64,1024]{2,1,0:T(8,128)(2,1)S(1)} collective-permute-done((bf16[2,64,1024]{2,1,0:T(8,128)(2,1)S(1)}, bf16[2,64,1024]{2,1,0:T(8,128)(2,1)S(1)}, u32[]{:S(2)}, u32[]{:S(2)}) %collective-permute-start.13) | collective-permute-done | bytes 262176 | tf_op jit(solution)/shard_map/ppermute | solution.py:41
  135.8 6.7 %convolution_convert_fusion = bf16[8,128,512]{2,1,0:T(8,128)(2,1)} fusion(bf16[512,2,1024,1]{2,0,1,3:T(8,128)(2,1)} %bitcast.214, bf16[8,2,1024,128]{3,2,1,0:T(8,128)(2,1)} %param.17, bf16[8,2]{1,0:T(8,128)(2,1)S(1)} %copy-done.13, bf16[8,128,512]{2,1,0:T(8,128)(2,1)S(1)} %copy-done.6, f32[8,128]{1,0:T(8,128)S(1)} %copy-done.15, ...), kind=kOutput, calls=%fused_computation.41 | convolution fusion | flops 2292973568 | bytes 8687648 | tf_op jit(solution)/shard_map/bjc,rbj->bcr/dot_general | solution.py:178
  (155 shorter events, 27.3 us)
Async XLA Ops:
  0.6 18.1 %copy-start = (bf16[8,128,512]{2,1,0:T(8,128)(2,1)S(1)}, bf16[8,128,512]{2,1,0:T(8,128)(2,1)}, u32[]{:S(2)}) copy-start(bf16[8,128,512]{2,1,0:T(8,128)(2,1)} %param.15) | copy-start | bytes 3145732
  0.6 17.9 %copy-start.16 = (s32[8,2]{0,1:T(2,128)S(1)}, s32[8,2]{0,1:T(2,128)}, u32[]{:S(2)}) copy-start(s32[8,2]{0,1:T(2,128)} %param.18) | copy-start | bytes 196
  0.7 18.1 %copy-start.7 = (bf16[8,128,128]{2,1,0:T(8,128)(2,1)S(1)}, bf16[8,128,128]{2,1,0:T(8,128)(2,1)}, u32[]{:S(2)}) copy-start(bf16[8,128,128]{2,1,0:T(8,128)(2,1)} %param.16) | copy-start | bytes 786436
  3.1 16.1 %collective-permute-start.4 = (bf16[1,3,128,1024]{3,2,0,1:T(8,128)(2,1)S(1)}, bf16[1,3,128,1024]{3,2,0,1:T(8,128)(2,1)S(1)}, u32[]{:S(2)}, u32[]{:S(2)}) collective-permute-start(bf16[1,3,128,1024]{3,2,0,1:T(8,128)(2,1)S(1)} %maximum_bitcast_fusion.2), channel_id=1, source_target_pairs={{0,4},{1,3},{2,6},{3,1},{4,0},{5,7},{6,2},{7,5},{8,12},{9,11},{10,... | collective-permute-start | bytes 2359304 | tf_op jit(solution)/shard_map/ppermute | solution.py:41
  18.7 3.3 %copy-start.12 = (bf16[8,2]{1,0:T(8,128)(2,1)}, bf16[8,2]{1,0:T(8,128)(2,1)S(1)}, u32[]{:S(2)}) copy-start(bf16[8,2]{1,0:T(8,128)(2,1)S(1)} %copy.38) | copy-start | bytes 100
  18.8 3.2 %copy-start.14 = (bf16[8,2,1024,128]{3,2,1,0:T(8,128)(2,1)S(1)}, bf16[8,2,1024,128]{3,2,1,0:T(8,128)(2,1)}, u32[]{:S(2)}) copy-start(bf16[8,2,1024,128]{3,2,1,0:T(8,128)(2,1)} %param.17) | copy-start | bytes 12582916
  19.2 5.3 %copy-start.5 = (bf16[8,128,512]{2,1,0:T(8,128)(2,1)}, bf16[8,128,512]{2,1,0:T(8,128)(2,1)S(1)}, u32[]{:S(2)}) copy-start(bf16[8,128,512]{2,1,0:T(8,128)(2,1)S(1)} %convolution_convert_fusion.1) | copy-start | bytes 3145732
  20.5 26.8 %collective-permute-start.5 = (bf16[2,3,128,1024]{3,2,0,1:T(8,128)(2,1)}, bf16[2,3,128,1024]{3,2,0,1:T(8,128)(2,1)}, u32[]{:S(2)}, u32[]{:S(2)}) collective-permute-start(bf16[2,3,128,1024]{3,2,0,1:T(8,128)(2,1)} %pad_maximum_fusion.2), channel_id=1, source_target_pairs={{0,2},{1,5},{2,0},{3,7},{4,6},{5,1},{6,4},{7,3},{8,10},{9,13},{10,... | collective-permute-start | bytes 4718600 | tf_op jit(solution)/shard_map/ppermute | solution.py:41
  47.3 3.6 %copy-start.3 = (bf16[8,64,2,1024]{3,1,0,2:T(8,128)(2,1)S(1)}, bf16[8,64,2,1024]{3,1,0,2:T(8,128)(2,1)}, u32[]{:S(2)}) copy-start(bf16[8,64,2,1024]{3,1,0,2:T(8,128)(2,1)} %reshape.264) | copy-start | bytes 6291460
  50.9 38.1 %collective-permute-start.6 = (bf16[4,3,128,1024]{3,2,0,1:T(8,128)(2,1)}, bf16[4,3,128,1024]{3,2,0,1:T(8,128)(2,1)}, u32[]{:S(2)}, u32[]{:S(2)}) collective-permute-start(bf16[4,3,128,1024]{3,2,0,1:T(8,128)(2,1)} %pad_maximum_fusion.1), channel_id=1, source_target_pairs={{0,1},{1,0},{2,3},{3,2},{4,5},{5,4},{6,7},{7,6},{8,9},{9,8},{10,11... | collective-permute-start | bytes 9437192 | tf_op jit(solution)/shard_map/ppermute | solution.py:35
  51.3 6.7 %collective-permute-start = (bf16[4,64,2,1024]{3,1,2,0:T(8,128)(2,1)S(1)}, bf16[4,64,2,1024]{3,1,2,0:T(8,128)(2,1)S(1)}, u32[]{:S(2)}, u32[]{:S(2)}) collective-permute-start(bf16[4,64,2,1024]{3,1,2,0:T(8,128)(2,1)S(1)} %pad_maximum_fusion.3), channel_id=1, source_target_pairs={{0,1},{1,0},{2,3},{3,2},{4,5},{5,4},{6,7},{7,6},{8,9},{9,8},{10,11... | collective-permute-start | bytes 3145736 | tf_op jit(solution)/shard_map/ppermute | solution.py:35
  58.5 9.2 %collective-permute-start.1 = (bf16[2,64,2,1024]{3,1,2,0:T(8,128)(2,1)S(1)}, bf16[2,64,2,1024]{3,1,2,0:T(8,128)(2,1)S(1)}, u32[]{:S(2)}, u32[]{:S(2)}) collective-permute-start(bf16[2,64,2,1024]{3,1,2,0:T(8,128)(2,1)S(1)} %slice.237), channel_id=1, source_target_pairs={{0,2},{1,5},{2,0},{3,7},{4,6},{5,1},{6,4},{7,3},{8,10},{9,13},{10,... | collective-permute-start | bytes 1572872 | tf_op jit(solution)/shard_map/ppermute | solution.py:41
  68.8 16.4 %collective-permute-start.2 = (bf16[1,64,2,1024]{3,1,2,0:T(8,128)(2,1)S(1)}, bf16[1,64,2,1024]{3,1,2,0:T(8,128)(2,1)}, u32[]{:S(2)}, u32[]{:S(2)}) collective-permute-start(bf16[1,64,2,1024]{3,1,2,0:T(8,128)(2,1)S(1)} %slice.239), channel_id=1, source_target_pairs={{0,4},{1,3},{2,6},{3,1},{4,0},{5,7},{6,2},{7,5},{8,12},{9,11},{10,... | collective-permute-start | bytes 786440 | tf_op jit(solution)/shard_map/ppermute | solution.py:41
  87.0 6.4 %collective-permute-start.3 = (bf16[64,1024]{1,0:T(8,128)(2,1)S(1)}, bf16[64,1024]{1,0:T(8,128)(2,1)S(1)}, u32[]{:S(2)}, u32[]{:S(2)}) collective-permute-start(bf16[64,1024]{1,0:T(8,128)(2,1)S(1)} %get-tuple-element.37), channel_id=1, source_target_pairs={{0,8},{8,0},{16,24},{24,16},{1,9},{9,1},{17,25},{25,17},{2,10},{10... | collective-permute-start | bytes 393224 | tf_op jit(solution)/shard_map/ppermute | solution.py:46
  88.6 10.1 %collective-permute-start.7 = (bf16[64,1024]{1,0:T(8,128)(2,1)}, bf16[64,1024]{1,0:T(8,128)(2,1)S(1)}, u32[]{:S(2)}, u32[]{:S(2)}) collective-permute-start(bf16[64,1024]{1,0:T(8,128)(2,1)} %get-tuple-element.36), channel_id=1, source_target_pairs={{0,8},{8,0},{16,24},{24,16},{1,9},{9,1},{17,25},{25,17},{2,10},{10... | collective-permute-start | bytes 393224 | tf_op jit(solution)/shard_map/ppermute | solution.py:46
  95.9 5.5 %copy-start.11 = (f32[3,128]{1,0:T(4,128)S(1)}, f32[3,128]{1,0:T(4,128)}, u32[]{:S(2)}) copy-start(f32[3,128]{1,0:T(4,128)} %param.23) | copy-start | bytes 4612
  96.0 17.1 %copy-start.2 = (bf16[8,3,128,1024]{3,2,0,1:T(8,128)(2,1)S(1)}, bf16[8,3,128,1024]{3,2,0,1:T(8,128)(2,1)}, u32[]{:S(2)}) copy-start(bf16[8,3,128,1024]{3,2,0,1:T(8,128)(2,1)} %copy-done.1) | copy-start | bytes 18874372
  98.7 11.7 %collective-permute-start.8 = (bf16[64,1024]{1,0:T(8,128)(2,1)S(1)}, bf16[64,1024]{1,0:T(8,128)(2,1)S(1)}, u32[]{:S(2)}, u32[]{:S(2)}) collective-permute-start(bf16[64,1024]{1,0:T(8,128)(2,1)S(1)} %fusion.63), channel_id=1, source_target_pairs={{0,16},{8,24},{16,0},{24,8},{1,17},{9,25},{17,1},{25,9},{2,18},{10... | collective-permute-start | bytes 393224 | tf_op jit(solution)/shard_map/ppermute | solution.py:46
  115.6 5.0 %collective-permute-start.9 = (bf16[1,64,1024]{2,1,0:T(8,128)(2,1)S(1)}, bf16[1,64,1024]{2,1,0:T(8,128)(2,1)S(1)}, u32[]{:S(2)}, u32[]{:S(2)}) collective-permute-start(bf16[1,64,1024]{2,1,0:T(8,128)(2,1)S(1)} %fusion.27), channel_id=1, source_target_pairs={{0,4},{1,3},{2,6},{3,1},{4,0},{5,7},{6,2},{7,5},{8,12},{9,11},{10,... | collective-permute-start | bytes 393224 | tf_op jit(solution)/shard_map/ppermute | solution.py:41
  117.0 5.1 %collective-permute-start.12 = (bf16[1,64,1024]{2,1,0:T(8,128)(2,1)S(1)}, bf16[1,64,1024]{2,1,0:T(8,128)(2,1)S(1)}, u32[]{:S(2)}, u32[]{:S(2)}) collective-permute-start(bf16[1,64,1024]{2,1,0:T(8,128)(2,1)S(1)} %bitcast.204), channel_id=1, source_target_pairs={{0,4},{1,3},{2,6},{3,1},{4,0},{5,7},{6,2},{7,5},{8,12},{9,11},{10,... | collective-permute-start | bytes 393224 | tf_op jit(solution)/shard_map/ppermute | solution.py:41
  120.7 6.4 %collective-permute-start.10 = (bf16[2,64,1024]{2,1,0:T(8,128)(2,1)S(1)}, bf16[2,64,1024]{2,1,0:T(8,128)(2,1)S(1)}, u32[]{:S(2)}, u32[]{:S(2)}) collective-permute-start(bf16[2,64,1024]{2,1,0:T(8,128)(2,1)S(1)} %pad_maximum_fusion.6), channel_id=1, source_target_pairs={{0,2},{1,5},{2,0},{3,7},{4,6},{5,1},{6,4},{7,3},{8,10},{9,13},{10,... | collective-permute-start | bytes 786440 | tf_op jit(solution)/shard_map/ppermute | solution.py:41
  122.1 7.8 %collective-permute-start.13 = (bf16[2,64,1024]{2,1,0:T(8,128)(2,1)S(1)}, bf16[2,64,1024]{2,1,0:T(8,128)(2,1)S(1)}, u32[]{:S(2)}, u32[]{:S(2)}) collective-permute-start(bf16[2,64,1024]{2,1,0:T(8,128)(2,1)S(1)} %pad_maximum_fusion.7), channel_id=1, source_target_pairs={{0,2},{1,5},{2,0},{3,7},{4,6},{5,1},{6,4},{7,3},{8,10},{9,13},{10,... | collective-permute-start | bytes 786440 | tf_op jit(solution)/shard_map/ppermute | solution.py:41
  127.2 2.9 %collective-permute-start.11 = (bf16[4,64,1024]{2,1,0:T(8,128)(2,1)S(1)}, bf16[4,64,1024]{2,1,0:T(8,128)(2,1)}, u32[]{:S(2)}, u32[]{:S(2)}) collective-permute-start(bf16[4,64,1024]{2,1,0:T(8,128)(2,1)S(1)} %pad_maximum_fusion.4), channel_id=1, source_target_pairs={{0,1},{1,0},{2,3},{3,2},{4,5},{5,4},{6,7},{7,6},{8,9},{9,8},{10,11... | collective-permute-start | bytes 1572872 | tf_op jit(solution)/shard_map/ppermute | solution.py:35
  130.0 2.1 %collective-permute-start.14 = (bf16[4,64,1024]{2,1,0:T(8,128)(2,1)S(1)}, bf16[4,64,1024]{2,1,0:T(8,128)(2,1)}, u32[]{:S(2)}, u32[]{:S(2)}) collective-permute-start(bf16[4,64,1024]{2,1,0:T(8,128)(2,1)S(1)} %pad_maximum_fusion.5), channel_id=1, source_target_pairs={{0,1},{1,0},{2,3},{3,2},{4,5},{5,4},{6,7},{7,6},{8,9},{9,8},{10,11... | collective-permute-start | bytes 1572872 | tf_op jit(solution)/shard_map/ppermute | solution.py:35
  (8 other events, 16.0 us)

commit v2 on v1

v2 whole, which is shorter than its diff:
```python
import jax
import jax.numpy as jnp
import numpy as np
from jax import lax
from jax.experimental import pallas as pl
from jax.experimental.pallas import tpu as pltpu
from jax.sharding import PartitionSpec as P

F32 = jnp.float32
BF16 = jnp.bfloat16
LANES = 128
TILE = 256
DIAG_ROWS = 16
NT = (((1,), (1,)), ((), ()))
VMEM = pltpu.CompilerParams(vmem_limit_bytes=32 * 1024 * 1024)


def bit_orders(planes):
    link_bits = list(range(1, planes.bit_length() - 1))
    turn = len(link_bits) // 2
    return [link_bits, link_bits[turn:] + link_bits[:turn]]


def slot_table(planes):
    orders = bit_orders(planes)
    count = len(orders[0])
    table = np.zeros((planes, planes), np.int32)
    for device in range(planes):
        for slot in range(planes):
            other = slot >> count
            order = orders[(device & 1) ^ other]
            block = device ^ other
            for place, bit in enumerate(order):
                if slot >> (count - 1 - place) & 1:
                    block ^= 1 << bit
            table[device, slot] = block
    return table


def swap_core(value):
    planes = lax.axis_size("plane")
    return lax.ppermute(value, "plane", [(i, i ^ 1) for i in range(planes)])


def swap_link(value, place):
    planes = lax.axis_size("plane")
    orders = bit_orders(planes)
    return lax.ppermute(value, "plane", [(i, i ^ (1 << orders[i & 1][place])) for i in range(planes)])


def swap_layer(value, stride):
    layers = lax.axis_size("layer")
    return lax.ppermute(value, "layer", [(i, i ^ (1 << stride)) for i in range(layers)])


def added(*terms):
    total = terms[0].astype(F32)
    for term in terms[1:]:
        total = total + term.astype(F32)
    return total.astype(BF16)


def scatter_sum(keep, send):
    places = len(bit_orders(lax.axis_size("plane"))[0])
    terms = [keep, swap_core(send)]
    for place in range(places):
        half = terms[0].shape[0] // 2
        theirs = swap_link(added(*[term[half:] for term in terms]), place)
        terms = [term[:half] for term in terms] + [theirs]
    return added(*[term[0] for term in terms])


def gather(value):
    pieces = [value]
    for place in reversed(range(len(bit_orders(lax.axis_size("plane"))[0]))):
        pieces = pieces + [swap_link(piece, place) for piece in pieces]
    return pieces + [swap_core(piece) for piece in pieces]


def lower_unit(block, first_row):
    row_count = block.shape[-2]
    col_count = block.shape[-1]
    row_ids = first_row + lax.broadcasted_iota(jnp.int32, (row_count, col_count), 0)
    col_ids = lax.broadcasted_iota(jnp.int32, (row_count, col_count), 1)
    below = jnp.where(col_ids < row_ids, block, jnp.zeros_like(block))
    return jnp.where(col_ids == row_ids, jnp.ones_like(block), below)


def nt(left, right):
    return lax.dot_general(left, right, NT, preferred_element_type=F32)


def nn(left, right):
    return jnp.dot(left, right, preferred_element_type=F32)


ME, LAYER, SLOTS = 0, 1, 2


def collect_call(info, sep_inverse, sep_couple, sep_diag, levels, layers):
    own_rows, sep_rows = sep_inverse.shape[1:]

    def sep_id(info, level):
        return layers - (layers >> level - 1) + jnp.right_shift(info[LAYER], level)

    def kernel(info, *refs):
        inverse, couple = refs[:levels], refs[levels : 2 * levels - 1]
        diag = refs[2 * levels - 1]
        outs = refs[2 * levels :]
        for level in range(1, levels + 1):
            out = outs[level - 1]
            out[:own_rows] = lower_unit(inverse[level - 1][0].astype(F32), info[ME] * own_rows).astype(BF16)
            for slot in range(levels - level):
                out[(slot + 1) * own_rows : (slot + 2) * own_rows] = couple[level - 1][0, slot]
        rows = []
        for level in range(1, levels + 1):
            value = diag[pl.ds(sep_id(info, level), 1)]
            high = value.astype(BF16).astype(F32)
            rows += [high, value - high]
        rows.append(jnp.zeros((DIAG_ROWS - len(rows), own_rows), F32))
        last = outs[-1]
        last[own_rows:] = jnp.zeros((DIAG_ROWS, sep_rows), BF16)
        last[own_rows:, :own_rows] = jnp.concatenate(rows, axis=0).astype(BF16)

    specs = [
        pl.BlockSpec((1, own_rows, sep_rows), lambda i, info, level=level: (sep_id(info, level), 0, 0))
        for level in range(1, levels + 1)
    ]
    specs += [
        pl.BlockSpec(
            (1, sep_couple.shape[1], own_rows, sep_rows),
            lambda i, info, level=level: (sep_id(info, level), 0, 0, 0),
        )
        for level in range(1, levels)
    ]
    specs.append(pl.BlockSpec(sep_diag.shape, lambda i, info: (0, 0)))
    shapes = [((1 + levels - level) * own_rows, sep_rows) for level in range(1, levels + 1)]
    shapes[-1] = (own_rows + DIAG_ROWS, sep_rows)
    return pl.pallas_call(
        kernel,
        grid_spec=pltpu.PrefetchScalarGridSpec(
            num_scalar_prefetch=1,
            grid=(1,),
            in_specs=specs,
            out_specs=[pl.BlockSpec(shape, lambda i, info: (0, 0)) for shape in shapes],
        ),
        out_shape=[jax.ShapeDtypeStruct(shape, BF16) for shape in shapes],
        compiler_params=VMEM,
        name="collect",
    )(info, *([sep_inverse] * levels), *([sep_couple] * (levels - 1)), sep_diag)


def leaf_forward_call(info, mask, leaves, couple, sep_rhs, level, layers):
    first = level == 1
    blocks, _, sep_rows, block_rows = couple.shape
    own_rows, rhs_cols = sep_rhs.shape[1:]
    planes = sep_rows // own_rows
    half, cols = planes // 2, rhs_cols // planes
    width = blocks * block_rows
    tile = min(TILE, sep_rows)

    def sep_id(info):
        return layers - (layers >> level - 1) + jnp.right_shift(info[LAYER], level)

    def kernel(info, mask, *refs):
        if first:
            rhs, inverse, couple, own_rhs, y, keep, send, scaled, sums = refs
        else:
            y, couple, own_rhs, keep, send, scaled, sums = refs
        step = pl.program_id(0)

        @pl.when(step == 0)
        def _():
            for b in range(blocks):
                place = slice(b * block_rows, (b + 1) * block_rows)
                if first:
                    lower = lower_unit(inverse[b].astype(F32), 0).astype(BF16)
                    solved = nn(lower, rhs[b]).T.astype(BF16)
                    y[:, place] = solved
                else:
                    solved = y[:, place]
                scaled[:, place] = solved * mask[b, level - 1].astype(F32).astype(BF16)
            alone = (jnp.bitwise_and(info[LAYER], (1 << level) - 1) == 0).astype(F32)
            scaled[:, width:] = (own_rhs[0].astype(F32).T * -alone).astype(BF16)

        weights = jnp.concatenate([couple[b, 0] for b in range(blocks)], axis=1)
        row_ids = step * tile + lax.broadcasted_iota(jnp.int32, (tile, own_rows), 0)
        own_ids = info[ME] * own_rows + lax.broadcasted_iota(jnp.int32, (tile, own_rows), 1)
        chosen = (row_ids == own_ids).astype(F32).astype(BF16)
        total = nt(scaled[:, :width], weights) + nt(scaled[:, width:], chosen)
        sums[...] = total.astype(BF16)
        for slot in range(planes):
            rows = pl.ds(pl.multiple_of(info[SLOTS + slot] * cols, cols), cols)
            if slot < half:
                keep[slot] = sums[rows]
            else:
                send[slot - half] = sums[rows]

    def whole(shape):
        return pl.BlockSpec(shape, lambda t, info, mask: (0,) * len(shape))

    part = pl.BlockSpec((half, cols, tile), lambda t, info, mask: (0, 0, t))
    part_shape = jax.ShapeDtypeStruct((half, cols, sep_rows), BF16)
    y_shape = (rhs_cols, width)
    out = pl.pallas_call(
        kernel,
        grid_spec=pltpu.PrefetchScalarGridSpec(
            num_scalar_prefetch=2,
            grid=(sep_rows // tile,),
            in_specs=[whole(leaf.shape) for leaf in leaves]
            + [
                pl.BlockSpec((blocks, 1, tile, block_rows), lambda t, info, mask: (0, level - 1, t, 0)),
                pl.BlockSpec((1, own_rows, rhs_cols), lambda t, info, mask: (sep_id(info), 0, 0)),
            ],
            out_specs=([whole(y_shape)] if first else []) + [part, part],
            scratch_shapes=[
                pltpu.VMEM((rhs_cols, width + own_rows), BF16),
                pltpu.VMEM((rhs_cols, tile), BF16),
            ],
        ),
        out_shape=([jax.ShapeDtypeStruct(y_shape, BF16)] if first else []) + [part_shape, part_shape],
        compiler_params=VMEM,
        cost_estimate=pl.CostEstimate(
            flops=2 * rhs_cols * width * sep_rows, bytes_accessed=2 * width * sep_rows, transcendentals=0
        ),
        name="leaf_forward",
    )(info, mask, *leaves, couple, sep_rhs)
    return out


def paired(count):
    step = 2 if count % 2 == 0 else 1
    return [range(i, i + step) for i in range(0, count, step)]


def rows_times(pieces, part, vector, out, order):
    for group in paired(len(pieces)):
        rows = jnp.concatenate([pieces[i][part] for i in group], axis=0)
        result = nt(vector, rows)
        for at, i in enumerate(group):
            lanes = pl.ds(pl.multiple_of(order[i] * LANES, LANES), LANES)
            out[:, lanes] = result[:, at * LANES : (at + 1) * LANES].astype(out.dtype)


def times_rows(pieces, part, vector, order):
    total = None
    for group in paired(len(pieces)):
        rows = jnp.concatenate([pieces[i][part] for i in group], axis=0)
        left = jnp.concatenate(
            [vector[:, pl.ds(pl.multiple_of(order[i] * LANES, LANES), LANES)] for i in group], axis=1
        ).astype(BF16)
        term = nn(left, rows)
        total = term if total is None else total + term
    return total


def at_part(index):
    return slice(index * LANES, (index + 1) * LANES)


def vmem_call(kernel, order, arrays, out_shapes, scratch, name, flops):
    vmem = pl.BlockSpec(memory_space=pltpu.VMEM)
    return pl.pallas_call(
        kernel,
        in_specs=[pl.BlockSpec(memory_space=pltpu.SMEM)] + [vmem] * len(arrays),
        out_specs=[vmem] * len(out_shapes),
        out_shape=out_shapes,
        scratch_shapes=scratch,
        compiler_params=VMEM,
        cost_estimate=pl.CostEstimate(
            flops=flops, bytes_accessed=sum(a.size * a.dtype.itemsize for a in arrays), transcendentals=0
        ),
        name=name,
    )(order, *arrays)


def level_forward_call(order, ours, theirs, pieces, couples):
    count = len(pieces)

    def kernel(order, ours, theirs, *refs):
        pieces, outs = refs[:count], refs[count:]
        residual = (-(ours[...].astype(F32) + theirs[...].astype(F32))).astype(BF16)
        y = outs[0]
        rows_times(pieces, at_part(0), residual, y, order)
        for slot in range(couples):
            rows_times(pieces, at_part(slot + 1), y[...], outs[slot + 1], order)

    shapes = [jax.ShapeDtypeStruct(ours.shape, BF16)]
    shapes += [jax.ShapeDtypeStruct(ours.shape, F32)] * couples
    flops = 2 * ours.size * ours.shape[1] * (1 + couples)
    return vmem_call(kernel, order, [ours, theirs, *pieces], shapes, [], "level_forward", flops)


def top_call(order, ours, theirs, pieces, levels):
    count = len(pieces)

    def kernel(order, ours, theirs, *refs):
        pieces, (x, diag, y) = refs[:count], refs[count:]
        for i in range(count):
            lanes = pl.ds(pl.multiple_of(order[i] * LANES, LANES), LANES)
            split = pieces[i][LANES : LANES + DIAG_ROWS, :LANES].astype(F32)
            for level in range(levels):
                diag[level : level + 1, lanes] = split[2 * level : 2 * level + 1] + split[2 * level + 1 : 2 * level + 2]
        residual = (-(ours[...].astype(F32) + theirs[...].astype(F32))).astype(BF16)
        rows_times(pieces, at_part(0), residual, y, order)
        y[...] = y[...].astype(BF16).astype(F32) / diag[levels - 1 : levels]
        target = y[...].astype(BF16)
        y[...] = target.astype(F32)
        x[...] = times_rows(pieces, at_part(0), y, order).astype(BF16)

    shapes = [jax.ShapeDtypeStruct(ours.shape, BF16), jax.ShapeDtypeStruct((levels, ours.shape[1]), F32)]
    scratch = [pltpu.VMEM(ours.shape, F32)]
    flops = 4 * ours.size * ours.shape[1]
    return vmem_call(kernel, order, [ours, theirs, *pieces], shapes, scratch, "top_level", flops)


def level_backward_call(order, y, diag, uppers, pieces, level):
    count, above = len(pieces), len(uppers)

    def kernel(order, y, diag, *refs):
        uppers, pieces, (x, target) = refs[:above], refs[above : above + count], refs[above + count :]
        value = y[...].astype(F32) / diag[level - 1 : level]
        for slot in range(above):
            value = value - times_rows(pieces, at_part(slot + 1), uppers[slot], order)
        target[...] = value.astype(BF16)
        x[...] = times_rows(pieces, at_part(0), target, order).astype(BF16)

    shapes = [jax.ShapeDtypeStruct(y.shape, BF16)]
    scratch = [pltpu.VMEM(y.shape, BF16)]
    flops = 2 * y.size * y.shape[1] * (1 + above)
    return vmem_call(kernel, order, [y, diag, *uppers, *pieces], shapes, scratch, "level_backward", flops)[0]


def leaf_backward_call(info, mask, y, inverse, couple, diag, above, own_rows):
    blocks, levels, sep_rows, block_rows = couple.shape
    rhs_cols = y.shape[0]
    slots = len(above[0])
    cols = rhs_cols // slots
    pair = 2 if blocks % 2 == 0 else 1

    def kernel(info, mask, y, inverse, couple, diag, *refs):
        above = refs[: levels * slots]
        leaf_out, sep_out, whole, sems = refs[levels * slots :]
        step = pl.program_id(0)

        def fetch(level, slot):
            rows = pl.ds(pl.multiple_of(info[SLOTS + slot] * cols, cols), cols)
            return pltpu.make_async_copy(
                above[level * slots + slot], whole.at[level, rows], sems.at[level, slot]
            )

        @pl.when(step == 0)
        def _():
            for level in range(levels):
                for slot in range(slots):
                    fetch(level, slot).start()
            for level in range(levels):
                for slot in range(slots):
                    fetch(level, slot).wait()
            row_ids = info[ME] * own_rows + lax.broadcasted_iota(jnp.int32, (own_rows, sep_rows), 0)
            col_ids = lax.broadcasted_iota(jnp.int32, (own_rows, sep_rows), 1)
            chosen = (row_ids == col_ids).astype(F32).astype(BF16)
            for level in range(levels):
                sep_out[0, level] = nt(chosen, whole[level]).astype(BF16)

        terms = None
        for level in range(levels):
            weights = jnp.concatenate(
                [
                    couple[b, level] * mask[step * pair + b, level].astype(F32).astype(BF16)
                    for b in range(pair)
                ],
                axis=1,
            )
            term = nn(whole[level], weights)
            terms = term if terms is None else terms + term
        for b in range(pair):
            place = slice(b * block_rows, (b + 1) * block_rows)
            scale = 1.0 / diag[pl.ds(step * pair + b, 1)]
            target = (y[:, place].astype(F32) * scale - terms[:, place]).astype(BF16)
            lower = lower_unit(inverse[b].astype(F32), 0).T.astype(BF16)
            leaf_out[b] = nt(lower, target).astype(BF16)

    anywhere = pl.BlockSpec(memory_space=pl.ANY)
    return pl.pallas_call(
        kernel,
        grid_spec=pltpu.PrefetchScalarGridSpec(
            num_scalar_prefetch=2,
            grid=(blocks // pair,),
            in_specs=[
                pl.BlockSpec((rhs_cols, pair * block_rows), lambda t, info, mask: (0, t)),
                pl.BlockSpec((pair, block_rows, block_rows), lambda t, info, mask: (t, 0, 0)),
                pl.BlockSpec((pair, levels, sep_rows, block_rows), lambda t, info, mask: (t, 0, 0, 0)),
                pl.BlockSpec(diag.shape, lambda t, info, mask: (0, 0)),
            ]
            + [anywhere] * (levels * slots),
            out_specs=[
                pl.BlockSpec((pair, block_rows, rhs_cols), lambda t, info, mask: (t, 0, 0)),
                pl.BlockSpec((1, levels, own_rows, rhs_cols), lambda t, info, mask: (0, 0, 0, 0)),
            ],
            scratch_shapes=[
                pltpu.VMEM((levels, rhs_cols, sep_rows), BF16),
                pltpu.SemaphoreType.DMA((levels, slots)),
            ],
        ),
        out_shape=[
            jax.ShapeDtypeStruct((blocks, block_rows, rhs_cols), BF16),
            jax.ShapeDtypeStruct((1, levels, own_rows, rhs_cols), BF16),
        ],
        compiler_params=VMEM,
        cost_estimate=pl.CostEstimate(
            flops=2 * rhs_cols * blocks * block_rows * levels * sep_rows,
            bytes_accessed=2 * blocks * block_rows * levels * sep_rows,
            transcendentals=0,
        ),
        name="leaf_backward",
    )(info, mask, y, inverse, couple, diag, *[piece for level in above for piece in level])


def repacked(pieces, block_slot, parts, own_rows):
    planes, sep_rows = len(pieces), pieces[0].shape[-1]
    whole = jnp.concatenate(
        [lax.dynamic_index_in_dim(jnp.stack(pieces), block_slot[i], 0) for i in range(planes)], axis=0
    )
    count = planes * own_rows // LANES
    mats = whole[:, : parts * own_rows].reshape(count, planes // count, parts, own_rows, sep_rows)
    mats = jnp.transpose(mats, (0, 2, 1, 3, 4)).reshape(count, parts * LANES, sep_rows)
    rest = whole[:, parts * own_rows :, :own_rows]
    rest = rest.reshape(count, planes // count, rest.shape[1], own_rows)
    rest = jnp.transpose(rest, (0, 2, 1, 3)).reshape(count, rest.shape[2], LANES)
    rest = jnp.pad(rest, ((0, 0), (0, 0), (0, sep_rows - LANES)))
    mats = jnp.concatenate([mats, rest], axis=1)
    return [mats[i] for i in range(count)]


def body(
    leaf_rhs,
    leaf_inverse,
    leaf_couple,
    couple_mask,
    leaf_diag,
    sep_rhs,
    sep_inverse,
    sep_couple,
    sep_diag,
):
    levels = leaf_couple.shape[1]
    planes = lax.axis_size("plane")
    layers = lax.axis_size("layer")
    own_rows = sep_rhs.shape[1]
    layer_id = lax.axis_index("layer").astype(jnp.int32)
    me = lax.axis_index("plane").astype(jnp.int32)
    table = slot_table(planes)
    slot_block = lax.dynamic_index_in_dim(jnp.asarray(table), me, 0, keepdims=False)
    info = jnp.concatenate([jnp.stack([me, layer_id]), slot_block])

    groups = [
        gather(own) for own in collect_call(info, sep_inverse, sep_couple, sep_diag, levels, layers)
    ]
    order = slot_block
    if own_rows != LANES:
        inverse_table = np.argsort(table, axis=1).astype(np.int32)
        block_slot = lax.dynamic_index_in_dim(jnp.asarray(inverse_table), me, 0, keepdims=False)
        groups = [
            repacked(group, block_slot, 1 + levels - level, own_rows)
            for level, group in enumerate(groups, 1)
        ]
        order = jnp.arange(len(groups[0]), dtype=jnp.int32)

    sums = []
    leaf_y = None
    for level in range(1, levels + 1):
        leaves = [leaf_rhs, leaf_inverse] if level == 1 else [leaf_y]
        out = leaf_forward_call(info, couple_mask, leaves, leaf_couple, sep_rhs, level, layers)
        if level == 1:
            leaf_y = out[0]
        sums.append(scatter_sum(*out[-2:]))

    solved = []
    for level in range(1, levels + 1):
        theirs = [swap_layer(sums[upper], level - 1) for upper in range(level - 1, levels)]
        if level < levels:
            out = level_forward_call(order, sums[level - 1], theirs[0], groups[level - 1], levels - level)
            solved.append(out[0])
            for slot in range(levels - level):
                upper = level + slot
                sums[upper] = added(sums[upper], theirs[1 + slot], out[1 + slot])
    answers = [None] * levels
    answers[-1], diag = top_call(order, sums[-1], theirs[0], groups[-1], levels)
    for level in range(levels - 1, 0, -1):
        answers[level - 1] = level_backward_call(
            order, solved[level - 1], diag, answers[level:], groups[level - 1], level
        )
    above = [None] * levels
    for level in range(levels, 0, -1):
        above[level - 1] = gather(answers[level - 1])
    return tuple(
        leaf_backward_call(info, couple_mask, leaf_y, leaf_inverse, leaf_couple, leaf_diag, above, own_rows)
    )


def solution(mesh):
    in_specs = (
        P(("layer", "plane"), None, None),
        P(("layer", "plane"), None, None),
        P(("layer", "plane"), None, None, None),
        P(("layer", "plane"), None),
        P(("layer", "plane"), None),
        P(None, "plane", None),
        P(None, "plane", None),
        P(None, None, "plane", None),
        P(None, "plane"),
    )
    out_specs = (P(("layer", "plane"), None, None), P("layer", None, "plane", None))
    return jax.shard_map(body, mesh=mesh, in_specs=in_specs, out_specs=out_specs, check_vma=False)
```

time: 144 us -> 102 us (0.71)
  between operations: 31.4 us -> 0.82 us
  other arithmetic: 24.6 us -> 0.51 us
  Pallas kernels: 0 us -> 22.7 us
  matrix products: 16.7 us -> 0 us
  waiting for transfers between devices: 25.2 us -> 40 us
  starting transfers between devices: 16.9 us -> 29.5 us
  local copies, waits for them, and re-layouts: 18.8 us -> 7.97 us
  blocking collectives: 9.02 us -> 0 us
    pallas_call x0 -> x7, Pallas kernels: none -> 22.7 us  [the longest x1 9.62 us: leaf_backward_call(): pl.pallas_call(kernel, grid_spec=pltpu.PrefetchScalarGridSpec(num_scalar_...]
    dot_general x9 -> x0, matrix products: 16.7 us -> none  [the longest x1 6.68 us: body(): jnp.einsum('bjc,rbj->bcr', leaf_lower, target, preferred_element_type=F32)]
    ppermute x8 -> x16, waiting for transfers between devices: 17 us -> 28 us  [swap_link(): lax.ppermute(value, 'plane', [(i, i ^ 1 << orders[i & 1][place]) for i in...]
    ppermute x8 -> x16, starting transfers between devices: 11.5 us -> 21.1 us  [swap_link(): lax.ppermute(value, 'plane', [(i, i ^ 1 << orders[i & 1][place]) for i in...]
    ppermute x3, waiting for transfers between devices: 1.12 us -> 10.7 us  [swap_layer(): lax.ppermute(value, 'layer', [(i, i ^ 1 << stride) for i in range(layers)])]
    all_gather x1 -> x0, blocking collectives: 9.02 us -> none  [body(): diag_full = lax.all_gather(sep_diag, 'plane', axis=1, tiled=True)]
    concatenate x9 -> x1, other arithmetic: 8.38 us -> 0.08 us  [body(): info = jnp.concatenate([jnp.stack([me, layer_id]), slot_block])]
    scatter-add x2 -> x0, other arithmetic: 6.54 us -> none  [body(): partial.at[:, :, level - 1].add(-term[:, :, None, :] * chosen[:, None])]
  transfers between devices with their start and end apart: 15 -> 37, of which waited for: 7 -> 14; matrix products, arithmetic and copies ran while one was open for 25% -> 0% of each run, Pallas kernels for 0% -> 6%
where the time goes in v2:
time: 102 us
  waiting for transfers between devices  40 us (39%)
  starting transfers between devices  29.5 us (29%)
  Pallas kernels  22.7 us (22%)
  local copies, waits for them, and re-layouts  7.97 us (8%)
    ppermute x16, waiting for transfers between devices, swap_link(): lax.ppermute(value, 'plane', [(i, i ^ 1 << orders[i & 1][place]) for i in...  28 us
    ppermute x16, starting transfers between devices, swap_link(): lax.ppermute(value, 'plane', [(i, i ^ 1 << orders[i & 1][place]) for i in...  21.1 us
    ppermute x3, waiting for transfers between devices, swap_layer(): lax.ppermute(value, 'layer', [(i, i ^ 1 << stride) for i in range(layers)])  10.7 us
    pallas_call x1, Pallas kernels, leaf_backward_call(): pl.pallas_call(kernel, grid_spec=pltpu.PrefetchScalarGridSpec(num_scalar_...  9.62 us
    unnamed x23, local copies, waits for them, and re-layouts  7.27 us
    pallas_call x2, Pallas kernels, leaf_forward_call(): pl.pallas_call(kernel, grid_spec=pltpu.PrefetchScalarGridSpec(num_scalar_...  7.07 us
    pallas_call x3, Pallas kernels, vmem_call(): pl.pallas_call(kernel, in_specs=[pl.BlockSpec(memory_space=pltpu.SMEM)] +...  5.3 us
    ppermute x3, starting transfers between devices, swap_layer(): lax.ppermute(value, 'layer', [(i, i ^ 1 << stride) for i in range(layers)])  4.99 us
  transfers between devices with their start and end apart: 37, of which 14 were waited for; matrix products, arithmetic and copies ran while one was open for 0% of the time, Pallas kernels for 6%

profile of v2, /device:TPU:0, one launch (start us, length us, event | category | flops | bytes accessed | tf_op | source)
XLA Modules:
  0.0 101.5 jit_solution(11126440205520980067)
XLA Ops:
  2.2 2.2 %copy-done = bf16[8,2,1024,128]{3,2,1,0:T(8,128)(2,1)S(1)} copy-done((bf16[8,2,1024,128]{3,2,1,0:T(8,128)(2,1)S(1)}, bf16[8,2,1024,128]{3,2,1,0:T(8,128)(2,1)}, u32[]{:S(2)}) %copy-start) | copy-done | bytes 4194328
  7.5 3.7 %leaf_forward.2 = (bf16[512,1024]{1,0:T(8,128)(2,1)S(1)}, bf16[4,64,1024]{2,1,0:T(8,128)(2,1)S(1)}, bf16[4,64,1024]{2,1,0:T(8,128)(2,1)S(1)}) custom-call(s32[10]{0:T(128)S(1)} %pad_add_fusion.info, s32[8,2]{1,0:T(8,128)S(1)} %copy.14.mask, bf16[8,128,512]{2,1,0:T(8,128)(2,1)S(1)} %copy-done.5, bf16[8,128,128]{2,1,0:T(8,128)(2,1)S(1)} %copy-done.7, ...), custom_call_target="tpu_custom_call" | custom-call | flops 1073741824 | bytes 2097152 | tf_op jit(solution)/shard_map/leaf_forward/pallas_call | solution.py:205
  13.7 2.6 %collective-permute-start.4 = (bf16[256,1024]{1,0:T(8,128)(2,1)S(1)}, bf16[256,1024]{1,0:T(8,128)(2,1)S(1)}, u32[]{:S(2)}, u32[]{:S(2)}) collective-permute-start(bf16[256,1024]{1,0:T(8,128)(2,1)S(1)} %get-tuple-element.16.refs_0_.refs_1_), channel_id=1, source_target_pairs={{0,4},{1,3},{2,6},{3,1},{4,0},{5,7},{6,2},{7,5},{8,12},{9,11},{10,... | collective-permute-start | bytes 1572872 | tf_op jit(solution)/shard_map/ppermute | solution.py:48
  16.3 3.3 %leaf_forward.3 = (bf16[4,64,1024]{2,1,0:T(8,128)(2,1)S(1)}, bf16[4,64,1024]{2,1,0:T(8,128)(2,1)S(1)}) custom-call(s32[10]{0:T(128)S(1)} %pad_add_fusion.info, s32[8,2]{1,0:T(8,128)S(1)} %copy.14.mask, bf16[512,1024]{1,0:T(8,128)(2,1)S(1)} %get-tuple-element.13.refs_0_.y, bf16[8,2,1024,128]{3,2,1,0:T(8,128)(2,1)S(1)} %copy-done.1, ...), custom_call_target="tpu_custom_call" | custom-call | flops 1073741824 | bytes 2097152 | tf_op jit(solution)/shard_map/leaf_forward/pallas_call | solution.py:205
  22.0 2.3 %collective-permute-done.4.refs_1_.refs_2_ = bf16[256,1024]{1,0:T(8,128)(2,1)S(1)} collective-permute-done((bf16[256,1024]{1,0:T(8,128)(2,1)S(1)}, bf16[256,1024]{1,0:T(8,128)(2,1)S(1)}, u32[]{:S(2)}, u32[]{:S(2)}) %collective-permute-start.4) | collective-permute-done | bytes 524320 | tf_op jit(solution)/shard_map/ppermute | solution.py:48
  24.4 2.2 %collective-permute-start.1 = (bf16[2,64,1024]{2,1,0:T(8,128)(2,1)S(1)}, bf16[2,64,1024]{2,1,0:T(8,128)(2,1)S(1)}, u32[]{:S(2)}, u32[]{:S(2)}) collective-permute-start(bf16[2,64,1024]{2,1,0:T(8,128)(2,1)S(1)} %add_convert_fusion.1), channel_id=1, source_target_pairs={{0,2},{1,5},{2,0},{3,7},{4,6},{5,1},{6,4},{7,3},{8,10},{9,13},{10,... | collective-permute-start | bytes 786440 | tf_op jit(solution)/shard_map/ppermute | solution.py:48
  26.7 4.5 %collective-permute-done.16.refs_1_ = bf16[144,1024]{1,0:T(8,128)(2,1)S(1)} collective-permute-done((bf16[144,1024]{1,0:T(8,128)(2,1)S(1)}, bf16[144,1024]{1,0:T(8,128)(2,1)S(1)}, u32[]{:S(2)}, u32[]{:S(2)}) %collective-permute-start.16) | collective-permute-done | bytes 294944 | tf_op jit(solution)/shard_map/ppermute | solution.py:48
  31.2 1.7 %collective-permute-start.12 = (bf16[2,64,1024]{2,1,0:T(8,128)(2,1)S(1)}, bf16[2,64,1024]{2,1,0:T(8,128)(2,1)S(1)}, u32[]{:S(2)}, u32[]{:S(2)}) collective-permute-start(bf16[2,64,1024]{2,1,0:T(8,128)(2,1)S(1)} %add_convert_fusion), channel_id=1, source_target_pairs={{0,2},{1,5},{2,0},{3,7},{4,6},{5,1},{6,4},{7,3},{8,10},{9,13},{10,... | collective-permute-start | bytes 786440 | tf_op jit(solution)/shard_map/ppermute | solution.py:48
  32.9 2.1 %collective-permute-done.1 = bf16[2,64,1024]{2,1,0:T(8,128)(2,1)S(1)} collective-permute-done((bf16[2,64,1024]{2,1,0:T(8,128)(2,1)S(1)}, bf16[2,64,1024]{2,1,0:T(8,128)(2,1)S(1)}, u32[]{:S(2)}, u32[]{:S(2)}) %collective-permute-start.1) | collective-permute-done | bytes 262176 | tf_op jit(solution)/shard_map/ppermute | solution.py:48
  36.6 6.8 %collective-permute-done.12 = bf16[2,64,1024]{2,1,0:T(8,128)(2,1)S(1)} collective-permute-done((bf16[2,64,1024]{2,1,0:T(8,128)(2,1)S(1)}, bf16[2,64,1024]{2,1,0:T(8,128)(2,1)S(1)}, u32[]{:S(2)}, u32[]{:S(2)}) %collective-permute-start.12) | collective-permute-done | bytes 262176 | tf_op jit(solution)/shard_map/ppermute | solution.py:48
  43.4 1.6 %collective-permute-start.2 = (bf16[1,64,1024]{2,1,0:T(8,128)(2,1)S(1)}, bf16[1,64,1024]{2,1,0:T(8,128)(2,1)S(1)}, u32[]{:S(2)}, u32[]{:S(2)}) collective-permute-start(bf16[1,64,1024]{2,1,0:T(8,128)(2,1)S(1)} %add_convert_fusion.6), channel_id=1, source_target_pairs={{0,4},{1,3},{2,6},{3,1},{4,0},{5,7},{6,2},{7,5},{8,12},{9,11},{10,... | collective-permute-start | bytes 393224 | tf_op jit(solution)/shard_map/ppermute | solution.py:48
  45.1 1.6 %collective-permute-done.17.refs_2_ = bf16[144,1024]{1,0:T(8,128)(2,1)S(1)} collective-permute-done((bf16[144,1024]{1,0:T(8,128)(2,1)S(1)}, bf16[144,1024]{1,0:T(8,128)(2,1)S(1)}, u32[]{:S(2)}, u32[]{:S(2)}) %collective-permute-start.17) | collective-permute-done | bytes 294944 | tf_op jit(solution)/shard_map/ppermute | solution.py:48
  50.3 3.9 %collective-permute-done.13 = bf16[1,64,1024]{2,1,0:T(8,128)(2,1)S(1)} collective-permute-done((bf16[1,64,1024]{2,1,0:T(8,128)(2,1)S(1)}, bf16[1,64,1024]{2,1,0:T(8,128)(2,1)S(1)}, u32[]{:S(2)}, u32[]{:S(2)}) %collective-permute-start.13) | collective-permute-done | bytes 131104 | tf_op jit(solution)/shard_map/ppermute | solution.py:48
  54.2 1.8 %collective-permute-start.3 = (bf16[64,1024]{1,0:T(8,128)(2,1)S(1)}, bf16[64,1024]{1,0:T(8,128)(2,1)S(1)}, u32[]{:S(2)}, u32[]{:S(2)}) collective-permute-start(bf16[64,1024]{1,0:T(8,128)(2,1)S(1)} %fusion.ours), channel_id=1, source_target_pairs={{0,8},{8,0},{16,24},{24,16},{1,9},{9,1},{17,25},{25,17},{2,10},{10... | collective-permute-start | bytes 393224 | tf_op jit(solution)/shard_map/ppermute | solution.py:53
  56.4 4.1 %collective-permute-done.3.theirs = bf16[64,1024]{1,0:T(8,128)(2,1)S(1)} collective-permute-done((bf16[64,1024]{1,0:T(8,128)(2,1)S(1)}, bf16[64,1024]{1,0:T(8,128)(2,1)S(1)}, u32[]{:S(2)}, u32[]{:S(2)}) %collective-permute-start.3) | collective-permute-done | bytes 131104 | tf_op jit(solution)/shard_map/ppermute | solution.py:53
  61.6 2.0 %level_forward.1 = (bf16[64,1024]{1,0:T(8,128)(2,1)S(1)}, f32[64,1024]{1,0:T(8,128)S(1)}) custom-call(s32[8]{0:T(128)S(1)} %dynamic-slice_bitcast_fusion.order, bf16[64,1024]{1,0:T(8,128)(2,1)S(1)} %fusion.ours, bf16[64,1024]{1,0:T(8,128)(2,1)S(1)} %collective-permute-done.3.theirs, bf16[256,1024]{1,0:T(8,128)(2,1)S(1)} %get-tuple-element.16.refs_0_.refs_1_, ...), custom_call_target="tpu_custom_call" | custom-call | flops 268435456 | bytes 4456448 | tf_op jit(solution)/shard_map/level_forward/pallas_call | solution.py:263
  63.7 2.9 %collective-permute-start.15 = (bf16[64,1024]{1,0:T(8,128)(2,1)S(1)}, bf16[64,1024]{1,0:T(8,128)(2,1)S(1)}, u32[]{:S(2)}, u32[]{:S(2)}) collective-permute-start(bf16[64,1024]{1,0:T(8,128)(2,1)S(1)} %add_convert_fusion.2.ours), channel_id=1, source_target_pairs={{0,16},{8,24},{16,0},{24,8},{1,17},{9,25},{17,1},{25,9},{2,18},{10... | collective-permute-start | bytes 393224 | tf_op jit(solution)/shard_map/ppermute | solution.py:53
  66.6 6.5 %collective-permute-done.15.theirs = bf16[64,1024]{1,0:T(8,128)(2,1)S(1)} collective-permute-done((bf16[64,1024]{1,0:T(8,128)(2,1)S(1)}, bf16[64,1024]{1,0:T(8,128)(2,1)S(1)}, u32[]{:S(2)}, u32[]{:S(2)}) %collective-permute-start.15) | collective-permute-done | bytes 131104 | tf_op jit(solution)/shard_map/ppermute | solution.py:53
  73.1 1.8 %top_level.1 = (bf16[64,1024]{1,0:T(8,128)(2,1)S(1)}, f32[2,1024]{1,0:T(2,128)S(1)}) custom-call(s32[8]{0:T(128)S(1)} %dynamic-slice_bitcast_fusion.order, bf16[64,1024]{1,0:T(8,128)(2,1)S(1)} %add_convert_fusion.2.ours, bf16[64,1024]{1,0:T(8,128)(2,1)S(1)} %collective-permute-done.15.theirs, bf16[144,1024]{1,0:T(8,128)(2,1)S(1)} %get-tuple-element.21.refs_0_, ...), custom_call_target="tpu_custom_call" | custom-call | flops 268435456 | bytes 2621440 | tf_op jit(solution)/shard_map/top_level/pallas_call | solution.py:263
  76.4 1.7 %collective-permute-start.23 = (bf16[64,1024]{1,0:T(8,128)(2,1)S(1)}, bf16[64,1024]{1,0:T(8,128)(2,1)S(1)}, u32[]{:S(2)}, u32[]{:S(2)}) collective-permute-start(bf16[64,1024]{1,0:T(8,128)(2,1)S(1)} %level_backward.1.refs_0_), channel_id=1, source_target_pairs={{0,4},{1,3},{2,6},{3,1},{4,0},{5,7},{6,2},{7,5},{8,12},{9,11},{10,... | collective-permute-start | bytes 393224 | tf_op jit(solution)/shard_map/ppermute | solution.py:48
  80.5 1.8 %collective-permute-done.23.refs_1_ = bf16[64,1024]{1,0:T(8,128)(2,1)S(1)} collective-permute-done((bf16[64,1024]{1,0:T(8,128)(2,1)S(1)}, bf16[64,1024]{1,0:T(8,128)(2,1)S(1)}, u32[]{:S(2)}, u32[]{:S(2)}) %collective-permute-start.23) | collective-permute-done | bytes 131104 | tf_op jit(solution)/shard_map/ppermute | solution.py:48
  83.8 1.6 %collective-permute-start.25 = (bf16[64,1024]{1,0:T(8,128)(2,1)S(1)}, bf16[64,1024]{1,0:T(8,128)(2,1)S(1)}, u32[]{:S(2)}, u32[]{:S(2)}) collective-permute-start(bf16[64,1024]{1,0:T(8,128)(2,1)S(1)} %collective-permute-done.23.refs_1_), channel_id=1, source_target_pairs={{0,2},{1,5},{2,0},{3,7},{4,6},{5,1},{6,4},{7,3},{8,10},{9,13},{10,... | collective-permute-start | bytes 393224 | tf_op jit(solution)/shard_map/ppermute | solution.py:48
  86.7 2.0 %collective-permute-done.25.refs_3_ = bf16[64,1024]{1,0:T(8,128)(2,1)S(1)} collective-permute-done((bf16[64,1024]{1,0:T(8,128)(2,1)S(1)}, bf16[64,1024]{1,0:T(8,128)(2,1)S(1)}, u32[]{:S(2)}, u32[]{:S(2)}) %collective-permute-start.25) | collective-permute-done | bytes 131104 | tf_op jit(solution)/shard_map/ppermute | solution.py:48
  91.9 9.6 %leaf_backward.1 = (bf16[8,128,512]{2,1,0:T(8,128)(2,1)}, bf16[1,2,128,512]{3,2,1,0:T(8,128)(2,1)}) custom-call(s32[10]{0:T(128)S(1)} %pad_add_fusion.info, s32[8,2]{1,0:T(8,128)S(1)} %copy.14.mask, bf16[512,1024]{1,0:T(8,128)(2,1)S(1)} %get-tuple-element.13.refs_0_.y, bf16[8,128,128]{2,1,0:T(8,128)(2,1)S(1)} %copy-done.8, ...), custom_call_target="tpu_custom_call" | custom-call | flops 2147483648 | bytes 4194304 | tf_op jit(solution)/shard_map/leaf_backward/pallas_call | solution.py:385
  (89 shorter events, 26.2 us)
Async XLA Ops:
  11.3 10.0 %collective-permute-start = (bf16[4,64,1024]{2,1,0:T(8,128)(2,1)S(1)}, bf16[4,64,1024]{2,1,0:T(8,128)(2,1)S(1)}, u32[]{:S(2)}, u32[]{:S(2)}) collective-permute-start(bf16[4,64,1024]{2,1,0:T(8,128)(2,1)S(1)} %get-tuple-element.15), channel_id=1, source_target_pairs={{0,1},{1,0},{2,3},{3,2},{4,5},{5,4},{6,7},{7,6},{8,9},{9,8},{10,11... | collective-permute-start | bytes 1572872 | tf_op jit(solution)/shard_map/ppermute | solution.py:42
  13.7 10.7 %collective-permute-start.4 = (bf16[256,1024]{1,0:T(8,128)(2,1)S(1)}, bf16[256,1024]{1,0:T(8,128)(2,1)S(1)}, u32[]{:S(2)}, u32[]{:S(2)}) collective-permute-start(bf16[256,1024]{1,0:T(8,128)(2,1)S(1)} %get-tuple-element.16.refs_0_.refs_1_), channel_id=1, source_target_pairs={{0,4},{1,3},{2,6},{3,1},{4,0},{5,7},{6,2},{7,5},{8,12},{9,11},{10,... | collective-permute-start | bytes 1572872 | tf_op jit(solution)/shard_map/ppermute | solution.py:48
  19.6 7.0 %collective-permute-start.11 = (bf16[4,64,1024]{2,1,0:T(8,128)(2,1)S(1)}, bf16[4,64,1024]{2,1,0:T(8,128)(2,1)S(1)}, u32[]{:S(2)}, u32[]{:S(2)}) collective-permute-start(bf16[4,64,1024]{2,1,0:T(8,128)(2,1)S(1)} %get-tuple-element.19), channel_id=1, source_target_pairs={{0,1},{1,0},{2,3},{3,2},{4,5},{5,4},{6,7},{7,6},{8,9},{9,8},{10,11... | collective-permute-start | bytes 1572872 | tf_op jit(solution)/shard_map/ppermute | solution.py:42
  19.9 28.3 %collective-permute-start.5 = (bf16[256,1024]{1,0:T(8,128)(2,1)S(1)}, bf16[256,1024]{1,0:T(8,128)(2,1)S(1)}, u32[]{:S(2)}, u32[]{:S(2)}) collective-permute-start(bf16[256,1024]{1,0:T(8,128)(2,1)S(1)} %get-tuple-element.16.refs_0_.refs_1_), channel_id=1, source_target_pairs={{0,2},{1,5},{2,0},{3,7},{4,6},{5,1},{6,4},{7,3},{8,10},{9,13},{10,... | collective-permute-start | bytes 1572872 | tf_op jit(solution)/shard_map/ppermute | solution.py:48
  21.3 27.2 %collective-permute-start.7 = (bf16[256,1024]{1,0:T(8,128)(2,1)S(1)}, bf16[256,1024]{1,0:T(8,128)(2,1)S(1)}, u32[]{:S(2)}, u32[]{:S(2)}) collective-permute-start(bf16[256,1024]{1,0:T(8,128)(2,1)S(1)} %get-tuple-element.16.refs_0_.refs_1_), channel_id=1, source_target_pairs={{0,1},{1,0},{2,3},{3,2},{4,5},{5,4},{6,7},{7,6},{8,9},{9,8},{10,11... | collective-permute-start | bytes 1572872 | tf_op jit(solution)/shard_map/ppermute | solution.py:42
  21.3 9.9 %collective-permute-start.16 = (bf16[144,1024]{1,0:T(8,128)(2,1)S(1)}, bf16[144,1024]{1,0:T(8,128)(2,1)S(1)}, u32[]{:S(2)}, u32[]{:S(2)}) collective-permute-start(bf16[144,1024]{1,0:T(8,128)(2,1)S(1)} %get-tuple-element.21.refs_0_), channel_id=1, source_target_pairs={{0,4},{1,3},{2,6},{3,1},{4,0},{5,7},{6,2},{7,5},{8,12},{9,11},{10,... | collective-permute-start | bytes 884744 | tf_op jit(solution)/shard_map/ppermute | solution.py:48
  24.4 10.6 %collective-permute-start.1 = (bf16[2,64,1024]{2,1,0:T(8,128)(2,1)S(1)}, bf16[2,64,1024]{2,1,0:T(8,128)(2,1)S(1)}, u32[]{:S(2)}, u32[]{:S(2)}) collective-permute-start(bf16[2,64,1024]{2,1,0:T(8,128)(2,1)S(1)} %add_convert_fusion.1), channel_id=1, source_target_pairs={{0,2},{1,5},{2,0},{3,7},{4,6},{5,1},{6,4},{7,3},{8,10},{9,13},{10,... | collective-permute-start | bytes 786440 | tf_op jit(solution)/shard_map/ppermute | solution.py:48
  26.6 23.6 %collective-permute-start.6 = (bf16[256,1024]{1,0:T(8,128)(2,1)S(1)}, bf16[256,1024]{1,0:T(8,128)(2,1)S(1)}, u32[]{:S(2)}, u32[]{:S(2)}) collective-permute-start(bf16[256,1024]{1,0:T(8,128)(2,1)S(1)} %collective-permute-done.4.refs_1_.refs_2_), channel_id=1, source_target_pairs={{0,2},{1,5},{2,0},{3,7},{4,6},{5,1},{6,4},{7,3},{8,10},{9,13},{10,... | collective-permute-start | bytes 1572872 | tf_op jit(solution)/shard_map/ppermute | solution.py:48
  31.2 12.2 %collective-permute-start.12 = (bf16[2,64,1024]{2,1,0:T(8,128)(2,1)S(1)}, bf16[2,64,1024]{2,1,0:T(8,128)(2,1)S(1)}, u32[]{:S(2)}, u32[]{:S(2)}) collective-permute-start(bf16[2,64,1024]{2,1,0:T(8,128)(2,1)S(1)} %add_convert_fusion), channel_id=1, source_target_pairs={{0,2},{1,5},{2,0},{3,7},{4,6},{5,1},{6,4},{7,3},{8,10},{9,13},{10,... | collective-permute-start | bytes 786440 | tf_op jit(solution)/shard_map/ppermute | solution.py:48
  35.0 11.7 %collective-permute-start.17 = (bf16[144,1024]{1,0:T(8,128)(2,1)S(1)}, bf16[144,1024]{1,0:T(8,128)(2,1)S(1)}, u32[]{:S(2)}, u32[]{:S(2)}) collective-permute-start(bf16[144,1024]{1,0:T(8,128)(2,1)S(1)} %get-tuple-element.21.refs_0_), channel_id=1, source_target_pairs={{0,2},{1,5},{2,0},{3,7},{4,6},{5,1},{6,4},{7,3},{8,10},{9,13},{10,... | collective-permute-start | bytes 884744 | tf_op jit(solution)/shard_map/ppermute | solution.py:48
  46.7 9.4 %collective-permute-start.18 = (bf16[144,1024]{1,0:T(8,128)(2,1)S(1)}, bf16[144,1024]{1,0:T(8,128)(2,1)S(1)}, u32[]{:S(2)}, u32[]{:S(2)}) collective-permute-start(bf16[144,1024]{1,0:T(8,128)(2,1)S(1)} %collective-permute-done.16.refs_1_), channel_id=1, source_target_pairs={{0,2},{1,5},{2,0},{3,7},{4,6},{5,1},{6,4},{7,3},{8,10},{9,13},{10,... | collective-permute-start | bytes 884744 | tf_op jit(solution)/shard_map/ppermute | solution.py:48
  48.1 12.4 %collective-permute-start.8 = (bf16[256,1024]{1,0:T(8,128)(2,1)S(1)}, bf16[256,1024]{1,0:T(8,128)(2,1)S(1)}, u32[]{:S(2)}, u32[]{:S(2)}) collective-permute-start(bf16[256,1024]{1,0:T(8,128)(2,1)S(1)} %collective-permute-done.4.refs_1_.refs_2_), channel_id=1, source_target_pairs={{0,1},{1,0},{2,3},{3,2},{4,5},{5,4},{6,7},{7,6},{8,9},{9,8},{10,11... | collective-permute-start | bytes 1572872 | tf_op jit(solution)/shard_map/ppermute | solution.py:42
  48.5 12.5 %collective-permute-start.9 = (bf16[256,1024]{1,0:T(8,128)(2,1)S(1)}, bf16[256,1024]{1,0:T(8,128)(2,1)S(1)}, u32[]{:S(2)}, u32[]{:S(2)}) collective-permute-start(bf16[256,1024]{1,0:T(8,128)(2,1)S(1)} %collective-permute-done.5.refs_2_.refs_3_), channel_id=1, source_target_pairs={{0,1},{1,0},{2,3},{3,2},{4,5},{5,4},{6,7},{7,6},{8,9},{9,8},{10,11... | collective-permute-start | bytes 1572872 | tf_op jit(solution)/shard_map/ppermute | solution.py:42
  50.2 11.0 %collective-permute-start.10 = (bf16[256,1024]{1,0:T(8,128)(2,1)S(1)}, bf16[256,1024]{1,0:T(8,128)(2,1)S(1)}, u32[]{:S(2)}, u32[]{:S(2)}) collective-permute-start(bf16[256,1024]{1,0:T(8,128)(2,1)S(1)} %collective-permute-done.6.refs_3_.refs_4_), channel_id=1, source_target_pairs={{0,1},{1,0},{2,3},{3,2},{4,5},{5,4},{6,7},{7,6},{8,9},{9,8},{10,11... | collective-permute-start | bytes 1572872 | tf_op jit(solution)/shard_map/ppermute | solution.py:42
  54.2 6.3 %collective-permute-start.3 = (bf16[64,1024]{1,0:T(8,128)(2,1)S(1)}, bf16[64,1024]{1,0:T(8,128)(2,1)S(1)}, u32[]{:S(2)}, u32[]{:S(2)}) collective-permute-start(bf16[64,1024]{1,0:T(8,128)(2,1)S(1)} %fusion.ours), channel_id=1, source_target_pairs={{0,8},{8,0},{16,24},{24,16},{1,9},{9,1},{17,25},{25,17},{2,10},{10... | collective-permute-start | bytes 393224 | tf_op jit(solution)/shard_map/ppermute | solution.py:53
  56.1 7.5 %collective-permute-start.14 = (bf16[64,1024]{1,0:T(8,128)(2,1)S(1)}, bf16[64,1024]{1,0:T(8,128)(2,1)S(1)}, u32[]{:S(2)}, u32[]{:S(2)}) collective-permute-start(bf16[64,1024]{1,0:T(8,128)(2,1)S(1)} %fusion.1), channel_id=1, source_target_pairs={{0,8},{8,0},{16,24},{24,16},{1,9},{9,1},{17,25},{25,17},{2,10},{10... | collective-permute-start | bytes 393224 | tf_op jit(solution)/shard_map/ppermute | solution.py:53
  60.6 6.0 %collective-permute-start.19 = (bf16[144,1024]{1,0:T(8,128)(2,1)S(1)}, bf16[144,1024]{1,0:T(8,128)(2,1)S(1)}, u32[]{:S(2)}, u32[]{:S(2)}) collective-permute-start(bf16[144,1024]{1,0:T(8,128)(2,1)S(1)} %get-tuple-element.21.refs_0_), channel_id=1, source_target_pairs={{0,1},{1,0},{2,3},{3,2},{4,5},{5,4},{6,7},{7,6},{8,9},{9,8},{10,11... | collective-permute-start | bytes 884744 | tf_op jit(solution)/shard_map/ppermute | solution.py:42
  60.6 6.0 %collective-permute-start.20 = (bf16[144,1024]{1,0:T(8,128)(2,1)S(1)}, bf16[144,1024]{1,0:T(8,128)(2,1)S(1)}, u32[]{:S(2)}, u32[]{:S(2)}) collective-permute-start(bf16[144,1024]{1,0:T(8,128)(2,1)S(1)} %collective-permute-done.16.refs_1_), channel_id=1, source_target_pairs={{0,1},{1,0},{2,3},{3,2},{4,5},{5,4},{6,7},{7,6},{8,9},{9,8},{10,11... | collective-permute-start | bytes 884744 | tf_op jit(solution)/shard_map/ppermute | solution.py:42
  63.7 9.4 %collective-permute-start.15 = (bf16[64,1024]{1,0:T(8,128)(2,1)S(1)}, bf16[64,1024]{1,0:T(8,128)(2,1)S(1)}, u32[]{:S(2)}, u32[]{:S(2)}) collective-permute-start(bf16[64,1024]{1,0:T(8,128)(2,1)S(1)} %add_convert_fusion.2.ours), channel_id=1, source_target_pairs={{0,16},{8,24},{16,0},{24,8},{1,17},{9,25},{17,1},{25,9},{2,18},{10... | collective-permute-start | bytes 393224 | tf_op jit(solution)/shard_map/ppermute | solution.py:53
  76.4 6.0 %collective-permute-start.23 = (bf16[64,1024]{1,0:T(8,128)(2,1)S(1)}, bf16[64,1024]{1,0:T(8,128)(2,1)S(1)}, u32[]{:S(2)}, u32[]{:S(2)}) collective-permute-start(bf16[64,1024]{1,0:T(8,128)(2,1)S(1)} %level_backward.1.refs_0_), channel_id=1, source_target_pairs={{0,4},{1,3},{2,6},{3,1},{4,0},{5,7},{6,2},{7,5},{8,12},{9,11},{10,... | collective-permute-start | bytes 393224 | tf_op jit(solution)/shard_map/ppermute | solution.py:48
  78.1 5.7 %collective-permute-start.24 = (bf16[64,1024]{1,0:T(8,128)(2,1)S(1)}, bf16[64,1024]{1,0:T(8,128)(2,1)S(1)}, u32[]{:S(2)}, u32[]{:S(2)}) collective-permute-start(bf16[64,1024]{1,0:T(8,128)(2,1)S(1)} %level_backward.1.refs_0_), channel_id=1, source_target_pairs={{0,2},{1,5},{2,0},{3,7},{4,6},{5,1},{6,4},{7,3},{8,10},{9,13},{10,... | collective-permute-start | bytes 393224 | tf_op jit(solution)/shard_map/ppermute | solution.py:48
  79.3 6.1 %collective-permute-start.26 = (bf16[64,1024]{1,0:T(8,128)(2,1)S(1)}, bf16[64,1024]{1,0:T(8,128)(2,1)S(1)}, u32[]{:S(2)}, u32[]{:S(2)}) collective-permute-start(bf16[64,1024]{1,0:T(8,128)(2,1)S(1)} %level_backward.1.refs_0_), channel_id=1, source_target_pairs={{0,1},{1,0},{2,3},{3,2},{4,5},{5,4},{6,7},{7,6},{8,9},{9,8},{10,11... | collective-permute-start | bytes 393224 | tf_op jit(solution)/shard_map/ppermute | solution.py:42
  79.3 6.3 %collective-permute-start.30 = (bf16[64,1024]{1,0:T(8,128)(2,1)S(1)}, bf16[64,1024]{1,0:T(8,128)(2,1)S(1)}, u32[]{:S(2)}, u32[]{:S(2)}) collective-permute-start(bf16[64,1024]{1,0:T(8,128)(2,1)S(1)} %get-tuple-element.23.refs_0_.refs_8_), channel_id=1, source_target_pairs={{0,4},{1,3},{2,6},{3,1},{4,0},{5,7},{6,2},{7,5},{8,12},{9,11},{10,... | collective-permute-start | bytes 393224 | tf_op jit(solution)/shard_map/ppermute | solution.py:48
  80.1 6.1 %collective-permute-start.31 = (bf16[64,1024]{1,0:T(8,128)(2,1)S(1)}, bf16[64,1024]{1,0:T(8,128)(2,1)S(1)}, u32[]{:S(2)}, u32[]{:S(2)}) collective-permute-start(bf16[64,1024]{1,0:T(8,128)(2,1)S(1)} %get-tuple-element.23.refs_0_.refs_8_), channel_id=1, source_target_pairs={{0,2},{1,5},{2,0},{3,7},{4,6},{5,1},{6,4},{7,3},{8,10},{9,13},{10,... | collective-permute-start | bytes 393224 | tf_op jit(solution)/shard_map/ppermute | solution.py:48
  (24 other events, 148.6 us)

commit v3 on v0

v3 whole, which is shorter than its diff:
```python
import jax
import jax.numpy as jnp
from jax import lax
from jax.experimental import pallas as pl
from jax.experimental.pallas import tpu as pltpu
from jax.sharding import PartitionSpec as P

F32 = jnp.float32
BF16 = jnp.bfloat16
LANES = 128
TILE = 256
DIAG_ROWS = 16
NT = (((1,), (1,)), ((), ()))
VMEM = pltpu.CompilerParams(vmem_limit_bytes=32 * 1024 * 1024)


def bit_orders(planes):
    link_bits = list(range(1, planes.bit_length() - 1))
    turn = len(link_bits) // 2
    return [link_bits, link_bits[turn:] + link_bits[:turn]]


def slot_table(planes, parity):
    orders = bit_orders(planes)
    count = len(orders[0])
    table = []
    for slot in range(planes):
        other = slot >> count
        block = other
        for place, bit in enumerate(orders[parity ^ other]):
            if slot >> (count - 1 - place) & 1:
                block ^= 1 << bit
        table.append(block)
    return table


def swap_core(value):
    planes = lax.axis_size("plane")
    return lax.ppermute(value, "plane", [(i, i ^ 1) for i in range(planes)])


def swap_link(value, place):
    planes, layers = lax.axis_size("plane"), lax.axis_size("layer")
    orders = bit_orders(planes)
    pairs = []
    for layer in range(layers):
        for i in range(planes):
            bit = orders[(i ^ layer) & 1][place]
            pairs.append((layer * planes + i, layer * planes + (i ^ (1 << bit))))
    return lax.ppermute(value, ("layer", "plane"), pairs)


def swap_layer(value, stride):
    layers = lax.axis_size("layer")
    return lax.ppermute(value, "layer", [(i, i ^ (1 << stride)) for i in range(layers)])


def after(value, *others):
    return lax.optimization_barrier((value, *others))[0]


def after_all(values, *others):
    return lax.optimization_barrier((*values, *others))[: len(values)]


def added(*terms):
    total = terms[0].astype(F32)
    for term in terms[1:]:
        total = total + term.astype(F32)
    return total.astype(BF16)


def scatter_sum(low, high, first_after):
    arrived = []
    for place in range(len(bit_orders(lax.axis_size("plane"))[0])):
        send = added(*high)
        if place == 0:
            send = after(send, *first_after)
        arrived.append(swap_link(send, place))
        terms = [*low, arrived[-1]]
        half = terms[0].shape[0] // 2
        low, high = [term[:half] for term in terms], [term[half:] for term in terms]
    return added(*[term[0] for term in terms]), arrived


def gather(value, cross=True):
    pieces = [value]
    for place in reversed(range(len(bit_orders(lax.axis_size("plane"))[0]))):
        pieces = pieces + [swap_link(piece, place) for piece in pieces]
    return pieces + [swap_core(piece) for piece in pieces] if cross else pieces


def lower_unit(block, first_row):
    row_count = block.shape[-2]
    col_count = block.shape[-1]
    row_ids = first_row + lax.broadcasted_iota(jnp.int32, (row_count, col_count), 0)
    col_ids = lax.broadcasted_iota(jnp.int32, (row_count, col_count), 1)
    below = jnp.where(col_ids < row_ids, block, jnp.zeros_like(block))
    return jnp.where(col_ids == row_ids, jnp.ones_like(block), below)


def nt(left, right):
    return lax.dot_general(left, right, NT, preferred_element_type=F32)


def nn(left, right):
    return jnp.dot(left, right, preferred_element_type=F32)


def places():
    return lax.axis_index("plane").astype(jnp.int32), lax.axis_index("layer").astype(jnp.int32)


def slot_blocks(planes):
    me, layer_id = places()
    parity = jnp.bitwise_and(jnp.bitwise_xor(me, layer_id), 1)
    even, odd = slot_table(planes, 0), slot_table(planes, 1)
    return [jnp.bitwise_xor(me, even[i] + parity * (odd[i] - even[i])) for i in range(planes)]


def at_multiple(index, size):
    return pl.ds(pl.multiple_of(index * size, size), size)


def sep_index(layer_id, level, layers):
    return layers - (layers >> level - 1) + jnp.right_shift(layer_id, level)


def kernel_call(kernel, arrays, spaces, out_shapes, scratch, name, flops=1, out_space=pltpu.VMEM, aliases={}):
    arrays = [
        pltpu.with_memory_space_constraint(array, space) if space == pltpu.HBM else array
        for array, space in zip(arrays, spaces)
    ]
    return pl.pallas_call(
        kernel,
        in_specs=[pl.BlockSpec(memory_space=space) for space in spaces],
        out_specs=[pl.BlockSpec(memory_space=out_space)] * len(out_shapes),
        out_shape=out_shapes,
        scratch_shapes=scratch,
        input_output_aliases=aliases,
        compiler_params=VMEM,
        cost_estimate=pl.CostEstimate(flops=flops, bytes_accessed=1, transcendentals=0),
        name=name,
    )(*arrays)


def collect_call(sep_inverse, sep_couple, sep_diag, levels, layers):
    own_rows, sep_rows = sep_inverse.shape[1:]

    def kernel(inverse, couple, diag_in, *refs):
        outs, (held, diag, sems, couple_sems) = refs[:levels], refs[levels:]
        me, layer_id = places()
        diag_load = pltpu.make_async_copy(diag_in, diag, sems.at[levels])
        diag_load.start()
        loads, moves = [], []
        for level in range(1, levels + 1):
            sep = sep_index(layer_id, level, layers)
            loads.append(pltpu.make_async_copy(inverse.at[sep], held.at[level - 1], sems.at[level - 1]))
            loads[-1].start()
            for slot in range(levels - level):
                rows = slice((slot + 1) * own_rows, (slot + 2) * own_rows)
                moves.append(
                    pltpu.make_async_copy(
                        couple.at[sep, slot], outs[level - 1].at[rows], couple_sems.at[level - 1, slot]
                    )
                )
                moves[-1].start()
        diag_load.wait()
        rows = []
        for level in range(1, levels + 1):
            value = diag[pl.ds(sep_index(layer_id, level, layers), 1)]
            high = value.astype(BF16).astype(F32)
            rows += [high, value - high]
        rows.append(jnp.zeros((DIAG_ROWS - len(rows), own_rows), F32))
        below = levels * own_rows
        outs[0][below:] = jnp.zeros((DIAG_ROWS, sep_rows), BF16)
        outs[0][below:, :own_rows] = jnp.concatenate(rows, axis=0).astype(BF16)
        for level in range(1, levels + 1):
            loads[level - 1].wait()
            lower = lower_unit(held[level - 1].astype(F32), me * own_rows)
            outs[level - 1][:own_rows] = lower.astype(BF16)
        for move in moves:
            move.wait()

    shapes = [((1 + levels - level) * own_rows, sep_rows) for level in range(1, levels + 1)]
    shapes[0] = (levels * own_rows + DIAG_ROWS, sep_rows)
    return kernel_call(
        kernel,
        [sep_inverse, sep_couple, sep_diag],
        [pltpu.HBM] * 3,
        [jax.ShapeDtypeStruct(shape, BF16) for shape in shapes],
        [
            pltpu.VMEM((levels, own_rows, sep_rows), BF16),
            pltpu.VMEM(sep_diag.shape, F32),
            pltpu.SemaphoreType.DMA((levels + 1,)),
            pltpu.SemaphoreType.DMA((levels, levels)),
        ],
        "collect",
        flops=20_000_000_000,
    )


def leaf_forward_call(mask, leaves, couple, sep_rhs, slots, layers):
    first = len(leaves) == 2
    blocks, levels, sep_rows, block_rows = couple.shape
    own_rows, rhs_cols = sep_rhs.shape[1:]
    planes = sep_rows // own_rows
    cols = rhs_cols // planes
    here = len(slots) * cols
    width = blocks * block_rows
    tile = min(TILE, sep_rows)
    tiles = sep_rows // tile

    def kernel(mask, *refs):
        if first:
            rhs, inverse, couple, own_rhs, y, *parts, scaled, turned = refs
        else:
            y, couple, own_rhs, *parts, scaled, turned = refs
        me, layer_id = places()
        order = slot_blocks(planes)
        if first:
            for b in range(blocks):
                lower = lower_unit(inverse[b].astype(F32), 0).astype(BF16)
                y[:, b * block_rows : (b + 1) * block_rows] = nn(lower, rhs[b]).T.astype(BF16)
        for level in range(levels):
            alone = (jnp.bitwise_and(layer_id, (2 << level) - 1) == 0).astype(F32)
            own = own_rhs[sep_index(layer_id, level + 1, layers)].astype(F32)
            turned[...] = (own.T * -alone).astype(BF16)
            for at, slot in enumerate(slots):
                rows = slice(at * cols, (at + 1) * cols)
                scaled[level, rows, width:] = turned[at_multiple(order[slot], cols)]
                for b in range(blocks):
                    place = slice(b * block_rows, (b + 1) * block_rows)
                    used = mask[level : level + 1, b : b + 1].astype(F32).astype(BF16)
                    scaled[level, rows, place] = y[at_multiple(order[slot], cols), place] * used
        for level in range(levels):
            for t in range(tiles):
                lanes = slice(t * tile, (t + 1) * tile)
                row_ids = t * tile + lax.broadcasted_iota(jnp.int32, (tile, own_rows), 0)
                own_ids = me * own_rows + lax.broadcasted_iota(jnp.int32, (tile, own_rows), 1)
                chosen = (row_ids == own_ids).astype(F32).astype(BF16)
                weights = jnp.concatenate([couple[b, level, lanes] for b in range(blocks)] + [chosen], axis=1)
                total = nt(scaled[level], weights).astype(BF16)
                half = len(slots) // 2
                for at in range(len(slots)):
                    parts[at // half][at % half, level, :, lanes] = total[at * cols : (at + 1) * cols]

    part = jax.ShapeDtypeStruct((len(slots) // 2, levels, cols, sep_rows), BF16)
    y_shape = [jax.ShapeDtypeStruct((rhs_cols, width), BF16)] if first else []
    scratch = [pltpu.VMEM((levels, here, width + own_rows), BF16), pltpu.VMEM((rhs_cols, own_rows), BF16)]
    arrays = [mask, *leaves, couple, sep_rhs]
    return vmem_call(kernel, arrays, y_shape + [part] * 2, scratch, "leaf_forward")


def paired(count):
    step = 2 if count % 2 == 0 else 1
    return [range(i, i + step) for i in range(0, count, step)]


def rows_times(pieces, part, vector, out, order):
    for group in paired(len(pieces)):
        rows = jnp.concatenate([pieces[i][part] for i in group], axis=0)
        result = nt(vector, rows)
        for at, i in enumerate(group):
            lanes = pl.ds(pl.multiple_of(order[i] * LANES, LANES), LANES)
            out[:, lanes] = result[:, at * LANES : (at + 1) * LANES].astype(out.dtype)


def times_rows(pieces, part, vector, order):
    total = None
    for group in paired(len(pieces)):
        rows = jnp.concatenate([pieces[i][part] for i in group], axis=0)
        left = jnp.concatenate(
            [vector[:, pl.ds(pl.multiple_of(order[i] * LANES, LANES), LANES)] for i in group], axis=1
        ).astype(BF16)
        term = nn(left, rows)
        total = term if total is None else total + term
    return total


def at_part(index):
    return slice(index * LANES, (index + 1) * LANES)


def vmem_call(kernel, arrays, out_shapes, scratch, name):
    return kernel_call(kernel, arrays, [pltpu.VMEM] * len(arrays), out_shapes, scratch, name)


def piece_order(count, planes):
    return slot_blocks(planes) if count == planes else list(range(count))


def level_forward_call(planes, sums, pieces):
    count = len(pieces)
    levels = sums.shape[0]

    def kernel(sums, *refs):
        order = piece_order(count, planes)
        pieces, (y, outs, work) = refs[:count], refs[count:]
        rows_times(pieces, at_part(0), -sums[0], y, order)
        for level in range(1, levels):
            rows_times(pieces, at_part(level), y[...], work, order)
            outs[level - 1] = (sums[level].astype(F32) + work[...]).astype(BF16)

    shape = sums.shape[1:]
    shapes = [jax.ShapeDtypeStruct(shape, BF16), jax.ShapeDtypeStruct((levels - 1, *shape), BF16)]
    return vmem_call(kernel, [sums, *pieces], shapes, [pltpu.VMEM(shape, F32)], "level_forward")


def backward_call(planes, sums, solved, groups):
    levels = len(groups)
    count = len(groups[0])
    lower = levels - 1

    def kernel(sums, *refs):
        order = piece_order(count, planes)
        solved, refs = refs[:lower], refs[lower:]
        pieces, (out, diag, work) = [refs[i * count : (i + 1) * count] for i in range(levels)], refs[-3:]
        for i in range(count):
            split = pieces[0][i][levels * LANES : levels * LANES + DIAG_ROWS, :LANES].astype(F32)
            for level in range(levels):
                value = split[2 * level : 2 * level + 1] + split[2 * level + 1 : 2 * level + 2]
                diag[level : level + 1, at_multiple(order[i], LANES)] = value
        rows_times(pieces[-1], at_part(0), -sums[0], work, order)
        for level in range(levels, 0, -1):
            y = work if level == levels else solved[level - 1]
            value = y[...].astype(F32) / diag[level - 1 : level]
            for slot in range(levels - level):
                upper = out.at[level + slot]
                value = value - times_rows(pieces[level - 1], at_part(slot + 1), upper, order)
            work[...] = value.astype(BF16)
            out[level - 1] = times_rows(pieces[level - 1], at_part(0), work, order).astype(BF16)

    arrays = [sums, *solved, *[piece for group in groups for piece in group]]
    shape = sums.shape[1:]
    shapes = [jax.ShapeDtypeStruct((levels, *shape), BF16)]
    scratch = [pltpu.VMEM((levels, shape[1]), F32), pltpu.VMEM(shape, BF16)]
    return vmem_call(kernel, arrays, shapes, scratch, "backward")[0]


def leaf_backward_call(mask, y, inverse, couple, diag, above, groups, before, own_rows):
    blocks, levels, sep_rows, block_rows = couple.shape
    rhs_cols, width = y.shape
    planes = sep_rows // own_rows
    cols = rhs_cols // planes
    slots = [slot for group in groups for slot in group]
    size = len(groups[0]) * cols
    here = len(slots) * cols
    pair = 2 if blocks % 2 == 0 else 1
    steps = blocks // pair
    kept = len(before)

    def kernel(mask, y, inverse, couple, diag, *refs):
        pieces, refs = dict(zip(slots, refs)), refs[len(slots) + kept :]
        leaf_to, sep_to, whole, ys, leaf_out, sep_out, sems = refs
        me = places()[0]
        order = slot_blocks(planes)
        stores = []

        def store(source, target):
            stores.append(pltpu.make_async_copy(source, target, sems.at[len(stores)]))
            stores[-1].start()

        lanes = []
        for j, group in enumerate(groups):
            lanes.append(at_multiple(order[group[0]] // len(group), size))
            rows = slice(j * size, (j + 1) * size)
            ys[rows] = y[lanes[j]]
            for slot in group:
                row = j * size + lax.rem(order[slot], len(group)) * cols
                for level in range(levels):
                    whole[level, pl.ds(pl.multiple_of(row, cols), cols)] = pieces[slot][level]
        row_ids = me * own_rows + lax.broadcasted_iota(jnp.int32, (own_rows, sep_rows), 0)
        col_ids = lax.broadcasted_iota(jnp.int32, (own_rows, sep_rows), 1)
        chosen = (row_ids == col_ids).astype(F32).astype(BF16)
        for level in range(levels):
            sep_out[level] = nt(chosen, whole[level]).astype(BF16)
            for j in range(len(groups)):
                store(sep_out.at[level, :, j * size : (j + 1) * size], sep_to.at[0, level, :, lanes[j]])
        for step in range(steps):
            terms = [None] * pair
            for level in range(levels):
                weights = jnp.concatenate([couple[step * pair + b, level] for b in range(pair)], axis=1)
                value = nn(whole[level], weights)
                for b in range(pair):
                    place = slice(b * block_rows, (b + 1) * block_rows)
                    at = step * pair + b
                    term = value[:, place] * mask[level : level + 1, at : at + 1].astype(F32)
                    terms[b] = term if terms[b] is None else terms[b] + term
            for b in range(pair):
                at = step * pair + b
                place = slice(at * block_rows, (at + 1) * block_rows)
                scale = 1.0 / diag[at : at + 1]
                target = (ys[:, place].astype(F32) * scale - terms[b]).astype(BF16)
                lower = lower_unit(inverse[at].astype(F32), 0).T.astype(BF16)
                leaf_out[at] = nt(lower, target).astype(BF16)
            at = slice(step * pair, (step + 1) * pair)
            for j in range(len(groups)):
                store(leaf_out.at[at, :, j * size : (j + 1) * size], leaf_to.at[at, :, lanes[j]])
        for copy in stores:
            copy.wait()

    arrays = [mask, y, inverse, couple, diag, *[above[slot] for slot in slots], *before]
    shapes = [
        jax.ShapeDtypeStruct((blocks, block_rows, rhs_cols), BF16),
        jax.ShapeDtypeStruct((1, levels, own_rows, rhs_cols), BF16),
    ]
    scratch = [
        pltpu.VMEM((levels, here, sep_rows), BF16),
        pltpu.VMEM((here, width), BF16),
        pltpu.VMEM((blocks, block_rows, here), BF16),
        pltpu.VMEM((levels, own_rows, here), BF16),
        pltpu.SemaphoreType.DMA(((levels + steps) * len(groups),)),
    ]
    spaces = [pltpu.VMEM] * (len(arrays) - kept) + [pl.ANY] * kept
    aliases = {len(arrays) - kept + i: i for i in range(kept)}
    return kernel_call(
        kernel, arrays, spaces, shapes, scratch, "leaf_backward", out_space=pl.ANY, aliases=aliases
    )


def repacked(pieces, block_slot, parts, own_rows):
    planes, sep_rows = len(pieces), pieces[0].shape[-1]
    whole = jnp.concatenate(
        [lax.dynamic_index_in_dim(jnp.stack(pieces), block_slot[i], 0) for i in range(planes)], axis=0
    )
    count = planes * own_rows // LANES
    mats = whole[:, : parts * own_rows].reshape(count, planes // count, parts, own_rows, sep_rows)
    mats = jnp.transpose(mats, (0, 2, 1, 3, 4)).reshape(count, parts * LANES, sep_rows)
    rest = whole[:, parts * own_rows :, :own_rows]
    rest = rest.reshape(count, planes // count, rest.shape[1], own_rows)
    rest = jnp.transpose(rest, (0, 2, 1, 3)).reshape(count, rest.shape[2], LANES)
    rest = jnp.pad(rest, ((0, 0), (0, 0), (0, sep_rows - LANES)))
    mats = jnp.concatenate([mats, rest], axis=1)
    return [mats[i] for i in range(count)]


def body(
    leaf_rhs,
    leaf_inverse,
    leaf_couple,
    couple_mask,
    leaf_diag,
    sep_rhs,
    sep_inverse,
    sep_couple,
    sep_diag,
):
    levels = leaf_couple.shape[1]
    planes = lax.axis_size("plane")
    layers = lax.axis_size("layer")
    own_rows = sep_rhs.shape[1]

    own = collect_call(sep_inverse, sep_couple, sep_diag, levels, layers)
    mask = after(couple_mask.T, own[0])

    links = len(bit_orders(planes)[0])
    four = links == 2
    near = swap_link(own[0], links - 1) if four else own[0]
    quarter = planes // 4
    highs = [slot for slot in range(planes) if slot // quarter % 2 == 1]
    lows = [slot for slot in range(planes) if slot // quarter % 2 == 0]
    leaf_y, keep, send = leaf_forward_call(
        mask, [leaf_rhs, leaf_inverse], leaf_couple, sep_rhs, highs, layers
    )
    high = [after(keep, near), swap_core(send)]
    keep, send = leaf_forward_call(mask, [leaf_y], leaf_couple, sep_rhs, lows, layers)
    own_crossed = [swap_core(own[0]), swap_core(own[-1])] if four else []
    low = [after(keep, *own_crossed), swap_core(send)]
    sums, arrived = scatter_sum(low, high, [])

    def fitted(pieces, level):
        if own_rows == LANES:
            return pieces
        me = lax.axis_index("plane")
        parity = jnp.bitwise_and(jnp.bitwise_xor(me, lax.axis_index("layer")), 1)
        slots = jnp.bitwise_xor(me, jnp.asarray([slot_table(planes, 0), slot_table(planes, 1)])[parity])
        return repacked(pieces, jnp.argsort(slots).astype(jnp.int32), 1 + levels - level, own_rows)

    if four:
        near_crossed = swap_core(after(near, keep))
        side = swap_layer(near, 0)
        far = swap_link(after(near, arrived[0]), 0)
        last_own = after(own[-1], arrived[0])
        last_near = swap_link(last_own, 1)
        sums = after(sums, near_crossed, side)
        last = [own[-1], last_near, swap_link(after(last_own, arrived[1]), 0)]
    else:
        first = gather(own[0])
    groups, solved = [], []
    for level in range(1, levels + 1):
        sums = added(sums, swap_layer(sums, level - 1))
        if level == 1:
            if four:
                side, far = after_all([side, far], sums, last_near)
                first = [own[0], near, side, far, own_crossed[0], near_crossed, swap_core(side), swap_core(far)]
            groups.append(fitted(first, 1))
        elif four and level == levels:
            groups.append(fitted(last + [swap_core(piece) for piece in last[2:4]], level))
        else:
            groups.append(fitted(gather(own[level - 1]), level))
        if level < levels:
            y, sums = level_forward_call(planes, sums, groups[level - 1])
            solved.append(y)
        if level == 1 and four:
            last = last + [swap_link(last_near, 0), own_crossed[1], swap_core(after(last_near, y))]
    answers = backward_call(planes, sums, solved, groups)
    leaves = [mask, leaf_y, leaf_inverse, leaf_couple, leaf_diag]
    if not four or 2 * answers.shape[1] != LANES:
        above = dict(enumerate(gather(answers)))
        return tuple(leaf_backward_call(*leaves, above, [list(range(planes))], [], own_rows))
    above = dict(enumerate(gather(answers, cross=False)))
    for slot in range(3):
        above[4 + slot] = swap_core(above[slot])
    early = leaf_backward_call(*leaves, above, [[0, 4], [1, 6], [2, 5]], [], own_rows)
    above[7] = swap_core(after(above[3], early[0]))
    return tuple(leaf_backward_call(*leaves, above, [[3, 7]], early, own_rows))


def solution(mesh):
    in_specs = (
        P(("layer", "plane"), None, None),
        P(("layer", "plane"), None, None),
        P(("layer", "plane"), None, None, None),
        P(("layer", "plane"), None),
        P(("layer", "plane"), None),
        P(None, "plane", None),
        P(None, "plane", None),
        P(None, None, "plane", None),
        P(None, "plane"),
    )
    out_specs = (P(("layer", "plane"), None, None), P("layer", None, "plane", None))
    return jax.shard_map(body, mesh=mesh, in_specs=in_specs, out_specs=out_specs, check_vma=False)
```

time: 356 us -> 76.2 us (0.21)
  waiting for transfers between devices: 303 us -> 33.3 us
  matrix products: 28.3 us -> 0 us
  starting transfers between devices: 4.28 us -> 25.5 us
  Pallas kernels: 0 us -> 15.7 us
  between operations: 14.3 us -> 0.85 us
  other arithmetic: 5.07 us -> 0.58 us
    reduce_scatter x4 -> x0, waiting for transfers between devices: 179 us -> none  [the longest x2 83.1 us: body(): lax.psum_scatter(transpose_solve(jnp.int32(0), lax.axis_size('plane') * o...]
    all_gather x4 -> x0, waiting for transfers between devices: 99.5 us -> none  [the longest x2 47.3 us: body(): residual_full = lax.all_gather(residual, 'plane', axis=0, tiled=True)]
    dot_general x8 -> x0, matrix products: 28.3 us -> none  [the longest x1 6.69 us: body(): jnp.einsum('bjc,bjr->bcr', leaf_lower, leaf_target, preferred_element_typ...]
    ppermute x2 -> x27, starting transfers between devices: 3.95 us -> 25.5 us  [the longest x10 16.7 us: swap_link(): return lax.ppermute(value, ('layer', 'plane'), pairs)]
    pallas_call x0 -> x7, Pallas kernels: none -> 15.7 us  [kernel_call(): pl.pallas_call(kernel, in_specs=[pl.BlockSpec(memory_space=space) for spa...]
    ppermute x2 -> x27, waiting for transfers between devices: 24.7 us -> 33.3 us  [the longest x10 22.8 us: swap_link(): return lax.ppermute(value, ('layer', 'plane'), pairs)]
  transfers between devices with their start and end apart: 10 -> 27, of which waited for: 10 -> 12; matrix products, arithmetic and copies ran while one was open for 0% -> 1% of each run, Pallas kernels for 0% -> 13%
where the time goes in v3:
time: 76.2 us; the launch traced here: 76 us
  waiting for transfers between devices  33.3 us (44%)
  starting transfers between devices  25.5 us (33%)
  Pallas kernels  15.7 us (21%)
  between operations  0.85 us (1%)
    ppermute x10, waiting for transfers between devices, swap_link(): return lax.ppermute(value, ('layer', 'plane'), pairs)  22.8 us
    ppermute x10, starting transfers between devices, swap_link(): return lax.ppermute(value, ('layer', 'plane'), pairs)  16.7 us
    pallas_call x7, Pallas kernels, kernel_call(): pl.pallas_call(kernel, in_specs=[pl.BlockSpec(memory_space=space) for spa...  15.7 us
    ppermute x3, waiting for transfers between devices, swap_layer(): lax.ppermute(value, 'layer', [(i, i ^ 1 << stride) for i in range(layers)])  7.25 us
    ppermute x3, starting transfers between devices, swap_layer(): lax.ppermute(value, 'layer', [(i, i ^ 1 << stride) for i in range(layers)])  6.46 us
    ppermute x14, waiting for transfers between devices, swap_core(): return lax.ppermute(value, 'plane', [(i, i ^ 1) for i in range(planes)])  3.31 us
    ppermute x14, starting transfers between devices, swap_core(): return lax.ppermute(value, 'plane', [(i, i ^ 1) for i in range(planes)])  2.39 us
  transfers between devices with their start and end apart: 27, of which 12 were waited for; matrix products, arithmetic and copies ran while one was open for 1% of the time, Pallas kernels for 13%

profile of v3, /device:TPU:0, one launch (start us, length us, event | category | flops | bytes accessed | tf_op | source)
XLA Modules:
  0.0 76.0 jit_solution(12912085608202824273)
XLA Ops:
  2.1 3.0 %collective-permute-start.3 = (bf16[272,1024]{1,0:T(8,128)(2,1)S(1)}, bf16[272,1024]{1,0:T(8,128)(2,1)S(1)}, u32[]{:S(2)}, u32[]{:S(2)}) collective-permute-start(bf16[272,1024]{1,0:T(8,128)(2,1)S(1)} %get-tuple-element.25.refs_0_.refs_1_), channel_id=1, source_target_pairs={{0,4},{1,3},{2,6},{3,1},{4,0},{5,7},{6,2},{7,5},{8,10},{9,13},{10,... | collective-permute-start | bytes 1671176 | tf_op jit(solution)/shard_map/ppermute | solution.py:50
  5.2 2.2 %leaf_forward.2 = (bf16[512,1024]{1,0:T(8,128)(2,1)S(1)}, bf16[2,2,64,1024]{3,2,1,0:T(8,128)(2,1)S(1)}, bf16[2,2,64,1024]{3,2,1,0:T(8,128)(2,1)S(1)}) custom-call(s32[2,8]{1,0:T(2,128)S(1)} %bitcast.3, bf16[8,128,512]{2,1,0:T(8,128)(2,1)S(1)} %copy-done.3, bf16[8,128,128]{2,1,0:T(8,128)(2,1)S(1)} %copy-done.1, bf16[8,2,1024,128]{3,2,1,0:T(8,128)(2,1)S(1)} %copy-done, ...), custom_call_target="tpu_custom_call" | custom-call | flops 1 | bytes 1 | tf_op jit(solution)/shard_map/leaf_forward/pallas_call | solution.py:134
  8.0 1.8 %leaf_forward.3 = (bf16[2,2,64,1024]{3,2,1,0:T(8,128)(2,1)S(1)}, bf16[2,2,64,1024]{3,2,1,0:T(8,128)(2,1)S(1)}) custom-call(s32[2,8]{1,0:T(2,128)S(1)} %bitcast.4, bf16[512,1024]{1,0:T(8,128)(2,1)S(1)} %get-tuple-element.27.refs_0_.y, bf16[8,2,1024,128]{3,2,1,0:T(8,128)(2,1)S(1)} %copy-done, bf16[3,128,512]{2,1,0:T(8,128)(2,1)S(1)} %copy-done.2), custom_call_target="tpu_custom_call" | custom-call | flops 1 | bytes 1 | tf_op jit(solution)/shard_map/leaf_forward/pallas_call | solution.py:134
  9.9 2.8 %collective-permute-done.3.refs_1_.refs_2_ = bf16[272,1024]{1,0:T(8,128)(2,1)S(1)} collective-permute-done((bf16[272,1024]{1,0:T(8,128)(2,1)S(1)}, bf16[272,1024]{1,0:T(8,128)(2,1)S(1)}, u32[]{:S(2)}, u32[]{:S(2)}) %collective-permute-start.3) | collective-permute-done | bytes 557088 | tf_op jit(solution)/shard_map/ppermute | solution.py:50
  12.9 2.1 %collective-permute-start.5 = (bf16[2,2,64,1024]{3,2,1,0:T(8,128)(2,1)S(1)}, bf16[2,2,64,1024]{3,2,1,0:T(8,128)(2,1)S(1)}, u32[]{:S(2)}, u32[]{:S(2)}) collective-permute-start(bf16[2,2,64,1024]{3,2,1,0:T(8,128)(2,1)S(1)} %add_convert_fusion), channel_id=1, source_target_pairs={{0,2},{1,5},{2,0},{3,7},{4,6},{5,1},{6,4},{7,3},{8,12},{9,11},{10,... | collective-permute-start | bytes 1572872 | tf_op jit(solution)/shard_map/ppermute | solution.py:50
  14.9 1.5 %collective-permute-done.1.refs_13_ = bf16[128,1024]{1,0:T(8,128)(2,1)S(1)} collective-permute-done((bf16[128,1024]{1,0:T(8,128)(2,1)S(1)}, bf16[128,1024]{1,0:T(8,128)(2,1)S(1)}, u32[]{:S(2)}, u32[]{:S(2)}) %collective-permute-start.1) | collective-permute-done | bytes 262176 | tf_op jit(solution)/shard_map/ppermute | solution.py:39
  16.6 1.6 %collective-permute-start.8 = (bf16[272,1024]{1,0:T(8,128)(2,1)S(1)}, bf16[272,1024]{1,0:T(8,128)(2,1)S(1)}, u32[]{:S(2)}, u32[]{:S(2)}) collective-permute-start(bf16[272,1024]{1,0:T(8,128)(2,1)S(1)} %collective-permute-done.3.refs_1_.refs_2_), channel_id=1, source_target_pairs={{0,8},{8,0},{16,24},{24,16},{1,9},{9,1},{17,25},{25,17},{2,10},{10... | collective-permute-start | bytes 1671176 | tf_op jit(solution)/shard_map/ppermute | solution.py:55
  18.2 3.9 %collective-permute-done.5 = bf16[2,2,64,1024]{3,2,1,0:T(8,128)(2,1)S(1)} collective-permute-done((bf16[2,2,64,1024]{3,2,1,0:T(8,128)(2,1)S(1)}, bf16[2,2,64,1024]{3,2,1,0:T(8,128)(2,1)S(1)}, u32[]{:S(2)}, u32[]{:S(2)}) %collective-permute-start.5) | collective-permute-done | bytes 524320 | tf_op jit(solution)/shard_map/ppermute | solution.py:50
  22.3 2.1 %collective-permute-start.6 = (bf16[1,2,64,1024]{3,2,1,0:T(8,128)(2,1)S(1)}, bf16[1,2,64,1024]{3,2,1,0:T(8,128)(2,1)S(1)}, u32[]{:S(2)}, u32[]{:S(2)}) collective-permute-start(bf16[1,2,64,1024]{3,2,1,0:T(8,128)(2,1)S(1)} %add_convert_fusion.3), channel_id=1, source_target_pairs={{0,4},{1,3},{2,6},{3,1},{4,0},{5,7},{6,2},{7,5},{8,10},{9,13},{10,... | collective-permute-start | bytes 786440 | tf_op jit(solution)/shard_map/ppermute | solution.py:50
  25.8 5.7 %collective-permute-done.6 = bf16[1,2,64,1024]{3,2,1,0:T(8,128)(2,1)S(1)} collective-permute-done((bf16[1,2,64,1024]{3,2,1,0:T(8,128)(2,1)S(1)}, bf16[1,2,64,1024]{3,2,1,0:T(8,128)(2,1)S(1)}, u32[]{:S(2)}, u32[]{:S(2)}) %collective-permute-start.6) | collective-permute-done | bytes 262176 | tf_op jit(solution)/shard_map/ppermute | solution.py:50
  31.7 2.2 %collective-permute-start.9 = (bf16[2,64,1024]{2,1,0:T(8,128)(2,1)S(1)}, bf16[2,64,1024]{2,1,0:T(8,128)(2,1)S(1)}, u32[]{:S(2)}, u32[]{:S(2)}) collective-permute-start(bf16[2,64,1024]{2,1,0:T(8,128)(2,1)S(1)} %fusion), channel_id=1, source_target_pairs={{0,8},{8,0},{16,24},{24,16},{1,9},{9,1},{17,25},{25,17},{2,10},{10... | collective-permute-start | bytes 786440 | tf_op jit(solution)/shard_map/ppermute | solution.py:55
  33.9 1.5 %collective-permute-start.11 = (bf16[128,1024]{1,0:T(8,128)(2,1)S(1)}, bf16[128,1024]{1,0:T(8,128)(2,1)S(1)}, u32[]{:S(2)}, u32[]{:S(2)}) collective-permute-start(bf16[128,1024]{1,0:T(8,128)(2,1)S(1)} %get-tuple-element.43.refs_9_), channel_id=1, source_target_pairs={{0,4},{1,3},{2,6},{3,1},{4,0},{5,7},{6,2},{7,5},{8,10},{9,13},{10,... | collective-permute-start | bytes 786440 | tf_op jit(solution)/shard_map/ppermute | solution.py:50
  35.4 3.9 %collective-permute-done.9 = bf16[2,64,1024]{2,1,0:T(8,128)(2,1)S(1)} collective-permute-done((bf16[2,64,1024]{2,1,0:T(8,128)(2,1)S(1)}, bf16[2,64,1024]{2,1,0:T(8,128)(2,1)S(1)}, u32[]{:S(2)}, u32[]{:S(2)}) %collective-permute-start.9) | collective-permute-done | bytes 262176 | tf_op jit(solution)/shard_map/ppermute | solution.py:55
  43.0 1.5 %level_forward.1 = (bf16[64,1024]{1,0:T(8,128)(2,1)S(1)}, bf16[1,64,1024]{2,1,0:T(8,128)(2,1)S(1)}) custom-call(bf16[2,64,1024]{2,1,0:T(8,128)(2,1)S(1)} %add_convert_fusion.1.sums, bf16[272,1024]{1,0:T(8,128)(2,1)S(1)} %get-tuple-element.25.refs_0_.refs_1_, bf16[272,1024]{1,0:T(8,128)(2,1)S(1)} %collective-permute-done.3.refs_1_.refs_2_, ...), custom_call_target="tpu_custom_call" | custom-call | flops 1 | bytes 1 | tf_op jit(solution)/shard_map/level_forward/pallas_call | solution.py:134
  44.6 2.7 %collective-permute-start.14 = (bf16[1,64,1024]{2,1,0:T(8,128)(2,1)S(1)}, bf16[1,64,1024]{2,1,0:T(8,128)(2,1)S(1)}, u32[]{:S(2)}, u32[]{:S(2)}) collective-permute-start(bf16[1,64,1024]{2,1,0:T(8,128)(2,1)S(1)} %get-tuple-element.41), channel_id=1, source_target_pairs={{0,16},{8,24},{16,0},{24,8},{1,17},{9,25},{17,1},{25,9},{2,18},{10... | collective-permute-start | bytes 393224 | tf_op jit(solution)/shard_map/ppermute | solution.py:55
  47.2 2.8 %collective-permute-done.15.refs_11_ = bf16[128,1024]{1,0:T(8,128)(2,1)S(1)} collective-permute-done((bf16[128,1024]{1,0:T(8,128)(2,1)S(1)}, bf16[128,1024]{1,0:T(8,128)(2,1)S(1)}, u32[]{:S(2)}, u32[]{:S(2)}) %collective-permute-start.15) | collective-permute-done | bytes 262176 | tf_op jit(solution)/shard_map/ppermute | solution.py:50
  50.5 3.4 %collective-permute-done.14 = bf16[1,64,1024]{2,1,0:T(8,128)(2,1)S(1)} collective-permute-done((bf16[1,64,1024]{2,1,0:T(8,128)(2,1)S(1)}, bf16[1,64,1024]{2,1,0:T(8,128)(2,1)S(1)}, u32[]{:S(2)}, u32[]{:S(2)}) %collective-permute-start.14) | collective-permute-done | bytes 131104 | tf_op jit(solution)/shard_map/ppermute | solution.py:55
  53.9 2.2 %backward.1.refs_0_ = bf16[2,64,1024]{2,1,0:T(8,128)(2,1)S(1)} custom-call(bf16[1,64,1024]{2,1,0:T(8,128)(2,1)S(1)} %add_convert_fusion.4.sums, bf16[64,1024]{1,0:T(8,128)(2,1)S(1)} %get-tuple-element.42.refs_0_, bf16[272,1024]{1,0:T(8,128)(2,1)S(1)} %get-tuple-element.25.refs_0_.refs_1_, bf16[272,1024]{1,0:T(8,128)(2,1)S(1)} %collective-permute-done.3.refs_1_.refs_2_, ...), custom_call_target="tpu_custom_call" | custom-call | flops 1 | bytes 1 | tf_op jit(solution)/shard_map/backward/pallas_call | solution.py:134
  56.1 1.6 %collective-permute-start.23 = (bf16[2,64,1024]{2,1,0:T(8,128)(2,1)S(1)}, bf16[2,64,1024]{2,1,0:T(8,128)(2,1)S(1)}, u32[]{:S(2)}, u32[]{:S(2)}) collective-permute-start(bf16[2,64,1024]{2,1,0:T(8,128)(2,1)S(1)} %backward.1.refs_0_), channel_id=1, source_target_pairs={{0,2},{1,5},{2,0},{3,7},{4,6},{5,1},{6,4},{7,3},{8,12},{9,11},{10,... | collective-permute-start | bytes 786440 | tf_op jit(solution)/shard_map/ppermute | solution.py:50
  59.1 6.1 %collective-permute-done.23.refs_4_ = bf16[2,64,1024]{2,1,0:T(8,128)(2,1)S(1)} collective-permute-done((bf16[2,64,1024]{2,1,0:T(8,128)(2,1)S(1)}, bf16[2,64,1024]{2,1,0:T(8,128)(2,1)S(1)}, u32[]{:S(2)}, u32[]{:S(2)}) %collective-permute-start.23) | collective-permute-done | bytes 262176 | tf_op jit(solution)/shard_map/ppermute | solution.py:50
  65.7 1.5 %collective-permute-start.21 = (bf16[2,64,1024]{2,1,0:T(8,128)(2,1)S(1)}, bf16[2,64,1024]{2,1,0:T(8,128)(2,1)S(1)}, u32[]{:S(2)}, u32[]{:S(2)}) collective-permute-start(bf16[2,64,1024]{2,1,0:T(8,128)(2,1)S(1)} %collective-permute-done.20.refs_2_), channel_id=1, source_target_pairs={{0,2},{1,5},{2,0},{3,7},{4,6},{5,1},{6,4},{7,3},{8,12},{9,11},{10,... | collective-permute-start | bytes 786440 | tf_op jit(solution)/shard_map/ppermute | solution.py:50
  67.2 4.2 %leaf_backward.2 = (bf16[8,128,512]{2,1,0:T(8,128)(2,1)}, bf16[1,2,128,512]{3,2,1,0:T(8,128)(2,1)}) custom-call(s32[2,8]{1,0:T(2,128)S(1)} %bitcast.5, bf16[512,1024]{1,0:T(8,128)(2,1)S(1)} %get-tuple-element.27.refs_0_.y, bf16[8,128,128]{2,1,0:T(8,128)(2,1)S(1)} %copy-done.1, bf16[8,2,1024,128]{3,2,1,0:T(8,128)(2,1)S(1)} %copy-done, ...), custom_call_target="tpu_custom_call" | custom-call | flops 1 | bytes 1 | tf_op jit(solution)/shard_map/leaf_backward/pallas_call | solution.py:134
  72.1 1.5 %collective-permute-done.26.refs_1_ = bf16[2,64,1024]{2,1,0:T(8,128)(2,1)S(1)} collective-permute-done((bf16[2,64,1024]{2,1,0:T(8,128)(2,1)S(1)}, bf16[2,64,1024]{2,1,0:T(8,128)(2,1)S(1)}, u32[]{:S(2)}, u32[]{:S(2)}) %collective-permute-start.26) | collective-permute-done | bytes 262176 | tf_op jit(solution)/shard_map/ppermute | solution.py:39
  73.6 2.4 %leaf_backward.3 = (bf16[8,128,512]{2,1,0:T(8,128)(2,1)}, bf16[1,2,128,512]{3,2,1,0:T(8,128)(2,1)}) custom-call(s32[2,8]{1,0:T(2,128)S(1)} %bitcast.6, bf16[512,1024]{1,0:T(8,128)(2,1)S(1)} %get-tuple-element.27.refs_0_.y, bf16[8,128,128]{2,1,0:T(8,128)(2,1)S(1)} %copy-done.1, ...), custom_call_target="tpu_custom_call", output_to_operand_aliasing={{0}: (7, {}), {1}: (8, {})} | custom-call | flops 1 | bytes 1 | tf_op jit(solution)/shard_map/leaf_backward/pallas_call | solution.py:134
  (54 shorter events, 11.2 us)
Async XLA Ops:
  2.1 10.5 %collective-permute-start.3 = (bf16[272,1024]{1,0:T(8,128)(2,1)S(1)}, bf16[272,1024]{1,0:T(8,128)(2,1)S(1)}, u32[]{:S(2)}, u32[]{:S(2)}) collective-permute-start(bf16[272,1024]{1,0:T(8,128)(2,1)S(1)} %get-tuple-element.25.refs_0_.refs_1_), channel_id=1, source_target_pairs={{0,4},{1,3},{2,6},{3,1},{4,0},{5,7},{6,2},{7,5},{8,10},{9,13},{10,... | collective-permute-start | bytes 1671176 | tf_op jit(solution)/shard_map/ppermute | solution.py:50
  7.4 5.3 %collective-permute-start.4 = (bf16[2,2,64,1024]{3,2,1,0:T(8,128)(2,1)S(1)}, bf16[2,2,64,1024]{3,2,1,0:T(8,128)(2,1)S(1)}, u32[]{:S(2)}, u32[]{:S(2)}) collective-permute-start(bf16[2,2,64,1024]{3,2,1,0:T(8,128)(2,1)S(1)} %get-tuple-element.34), channel_id=1, source_target_pairs={{0,1},{1,0},{2,3},{3,2},{4,5},{5,4},{6,7},{7,6},{8,9},{9,8},{10,11... | collective-permute-start | bytes 1572872 | tf_op jit(solution)/shard_map/ppermute | solution.py:39
  7.5 9.0 %collective-permute-start = (bf16[272,1024]{1,0:T(8,128)(2,1)S(1)}, bf16[272,1024]{1,0:T(8,128)(2,1)S(1)}, u32[]{:S(2)}, u32[]{:S(2)}) collective-permute-start(bf16[272,1024]{1,0:T(8,128)(2,1)S(1)} %get-tuple-element.25.refs_0_.refs_1_), channel_id=1, source_target_pairs={{0,1},{1,0},{2,3},{3,2},{4,5},{5,4},{6,7},{7,6},{8,9},{9,8},{10,11... | collective-permute-start | bytes 1671176 | tf_op jit(solution)/shard_map/ppermute | solution.py:39
  9.8 8.5 %collective-permute-start.2 = (bf16[2,2,64,1024]{3,2,1,0:T(8,128)(2,1)S(1)}, bf16[2,2,64,1024]{3,2,1,0:T(8,128)(2,1)S(1)}, u32[]{:S(2)}, u32[]{:S(2)}) collective-permute-start(bf16[2,2,64,1024]{3,2,1,0:T(8,128)(2,1)S(1)} %get-tuple-element.31), channel_id=1, source_target_pairs={{0,1},{1,0},{2,3},{3,2},{4,5},{5,4},{6,7},{7,6},{8,9},{9,8},{10,11... | collective-permute-start | bytes 1572872 | tf_op jit(solution)/shard_map/ppermute | solution.py:39
  12.9 9.2 %collective-permute-start.5 = (bf16[2,2,64,1024]{3,2,1,0:T(8,128)(2,1)S(1)}, bf16[2,2,64,1024]{3,2,1,0:T(8,128)(2,1)S(1)}, u32[]{:S(2)}, u32[]{:S(2)}) collective-permute-start(bf16[2,2,64,1024]{3,2,1,0:T(8,128)(2,1)S(1)} %add_convert_fusion), channel_id=1, source_target_pairs={{0,2},{1,5},{2,0},{3,7},{4,6},{5,1},{6,4},{7,3},{8,12},{9,11},{10,... | collective-permute-start | bytes 1572872 | tf_op jit(solution)/shard_map/ppermute | solution.py:50
  16.5 15.2 %collective-permute-start.7 = (bf16[272,1024]{1,0:T(8,128)(2,1)S(1)}, bf16[272,1024]{1,0:T(8,128)(2,1)S(1)}, u32[]{:S(2)}, u32[]{:S(2)}) collective-permute-start(bf16[272,1024]{1,0:T(8,128)(2,1)S(1)} %collective-permute-done.3.refs_1_.refs_2_), channel_id=1, source_target_pairs={{0,1},{1,0},{2,3},{3,2},{4,5},{5,4},{6,7},{7,6},{8,9},{9,8},{10,11... | collective-permute-start | bytes 1671176 | tf_op jit(solution)/shard_map/ppermute | solution.py:39
  16.6 15.1 %collective-permute-start.8 = (bf16[272,1024]{1,0:T(8,128)(2,1)S(1)}, bf16[272,1024]{1,0:T(8,128)(2,1)S(1)}, u32[]{:S(2)}, u32[]{:S(2)}) collective-permute-start(bf16[272,1024]{1,0:T(8,128)(2,1)S(1)} %collective-permute-done.3.refs_1_.refs_2_), channel_id=1, source_target_pairs={{0,8},{8,0},{16,24},{24,16},{1,9},{9,1},{17,25},{25,17},{2,10},{10... | collective-permute-start | bytes 1671176 | tf_op jit(solution)/shard_map/ppermute | solution.py:55
  22.3 9.3 %collective-permute-start.6 = (bf16[1,2,64,1024]{3,2,1,0:T(8,128)(2,1)S(1)}, bf16[1,2,64,1024]{3,2,1,0:T(8,128)(2,1)S(1)}, u32[]{:S(2)}, u32[]{:S(2)}) collective-permute-start(bf16[1,2,64,1024]{3,2,1,0:T(8,128)(2,1)S(1)} %add_convert_fusion.3), channel_id=1, source_target_pairs={{0,4},{1,3},{2,6},{3,1},{4,0},{5,7},{6,2},{7,5},{8,10},{9,13},{10,... | collective-permute-start | bytes 786440 | tf_op jit(solution)/shard_map/ppermute | solution.py:50
  24.4 15.9 %collective-permute-start.10 = (bf16[272,1024]{1,0:T(8,128)(2,1)S(1)}, bf16[272,1024]{1,0:T(8,128)(2,1)S(1)}, u32[]{:S(2)}, u32[]{:S(2)}) collective-permute-start(bf16[272,1024]{1,0:T(8,128)(2,1)S(1)} %collective-permute-done.3.refs_1_.refs_2_), channel_id=1, source_target_pairs={{0,2},{1,5},{2,0},{3,7},{4,6},{5,1},{6,4},{7,3},{8,12},{9,11},{10,... | collective-permute-start | bytes 1671176 | tf_op jit(solution)/shard_map/ppermute | solution.py:50
  31.7 7.6 %collective-permute-start.9 = (bf16[2,64,1024]{2,1,0:T(8,128)(2,1)S(1)}, bf16[2,64,1024]{2,1,0:T(8,128)(2,1)S(1)}, u32[]{:S(2)}, u32[]{:S(2)}) collective-permute-start(bf16[2,64,1024]{2,1,0:T(8,128)(2,1)S(1)} %fusion), channel_id=1, source_target_pairs={{0,8},{8,0},{16,24},{24,16},{1,9},{9,1},{17,25},{25,17},{2,10},{10... | collective-permute-start | bytes 786440 | tf_op jit(solution)/shard_map/ppermute | solution.py:55
  33.9 6.4 %collective-permute-start.11 = (bf16[128,1024]{1,0:T(8,128)(2,1)S(1)}, bf16[128,1024]{1,0:T(8,128)(2,1)S(1)}, u32[]{:S(2)}, u32[]{:S(2)}) collective-permute-start(bf16[128,1024]{1,0:T(8,128)(2,1)S(1)} %get-tuple-element.43.refs_9_), channel_id=1, source_target_pairs={{0,4},{1,3},{2,6},{3,1},{4,0},{5,7},{6,2},{7,5},{8,10},{9,13},{10,... | collective-permute-start | bytes 786440 | tf_op jit(solution)/shard_map/ppermute | solution.py:50
  40.3 2.5 %collective-permute-start.12 = (bf16[272,1024]{1,0:T(8,128)(2,1)S(1)}, bf16[272,1024]{1,0:T(8,128)(2,1)S(1)}, u32[]{:S(2)}, u32[]{:S(2)}) collective-permute-start(bf16[272,1024]{1,0:T(8,128)(2,1)S(1)} %collective-permute-done.8.refs_2_.refs_3_), channel_id=1, source_target_pairs={{0,1},{1,0},{2,3},{3,2},{4,5},{5,4},{6,7},{7,6},{8,9},{9,8},{10,11... | collective-permute-start | bytes 1671176 | tf_op jit(solution)/shard_map/ppermute | solution.py:39
  40.3 2.8 %collective-permute-start.13 = (bf16[272,1024]{1,0:T(8,128)(2,1)S(1)}, bf16[272,1024]{1,0:T(8,128)(2,1)S(1)}, u32[]{:S(2)}, u32[]{:S(2)}) collective-permute-start(bf16[272,1024]{1,0:T(8,128)(2,1)S(1)} %collective-permute-done.10.refs_3_.refs_4_), channel_id=1, source_target_pairs={{0,1},{1,0},{2,3},{3,2},{4,5},{5,4},{6,7},{7,6},{8,9},{9,8},{10,11... | collective-permute-start | bytes 1671176 | tf_op jit(solution)/shard_map/ppermute | solution.py:39
  40.8 6.4 %collective-permute-start.16 = (bf16[128,1024]{1,0:T(8,128)(2,1)S(1)}, bf16[128,1024]{1,0:T(8,128)(2,1)S(1)}, u32[]{:S(2)}, u32[]{:S(2)}) collective-permute-start(bf16[128,1024]{1,0:T(8,128)(2,1)S(1)} %collective-permute-done.11.refs_10_), channel_id=1, source_target_pairs={{0,2},{1,5},{2,0},{3,7},{4,6},{5,1},{6,4},{7,3},{8,12},{9,11},{10,... | collective-permute-start | bytes 786440 | tf_op jit(solution)/shard_map/ppermute | solution.py:50
  42.3 7.7 %collective-permute-start.15 = (bf16[128,1024]{1,0:T(8,128)(2,1)S(1)}, bf16[128,1024]{1,0:T(8,128)(2,1)S(1)}, u32[]{:S(2)}, u32[]{:S(2)}) collective-permute-start(bf16[128,1024]{1,0:T(8,128)(2,1)S(1)} %get-tuple-element.43.refs_9_), channel_id=1, source_target_pairs={{0,2},{1,5},{2,0},{3,7},{4,6},{5,1},{6,4},{7,3},{8,12},{9,11},{10,... | collective-permute-start | bytes 786440 | tf_op jit(solution)/shard_map/ppermute | solution.py:50
  44.6 9.3 %collective-permute-start.14 = (bf16[1,64,1024]{2,1,0:T(8,128)(2,1)S(1)}, bf16[1,64,1024]{2,1,0:T(8,128)(2,1)S(1)}, u32[]{:S(2)}, u32[]{:S(2)}) collective-permute-start(bf16[1,64,1024]{2,1,0:T(8,128)(2,1)S(1)} %get-tuple-element.41), channel_id=1, source_target_pairs={{0,16},{8,24},{16,0},{24,8},{1,17},{9,25},{17,1},{25,9},{2,18},{10... | collective-permute-start | bytes 393224 | tf_op jit(solution)/shard_map/ppermute | solution.py:55
  47.2 6.7 %collective-permute-start.19 = (bf16[128,1024]{1,0:T(8,128)(2,1)S(1)}, bf16[128,1024]{1,0:T(8,128)(2,1)S(1)}, u32[]{:S(2)}, u32[]{:S(2)}) collective-permute-start(bf16[128,1024]{1,0:T(8,128)(2,1)S(1)} %collective-permute-done.16.refs_12_), channel_id=1, source_target_pairs={{0,1},{1,0},{2,3},{3,2},{4,5},{5,4},{6,7},{7,6},{8,9},{9,8},{10,11... | collective-permute-start | bytes 786440 | tf_op jit(solution)/shard_map/ppermute | solution.py:39
  50.0 3.9 %collective-permute-start.18 = (bf16[128,1024]{1,0:T(8,128)(2,1)S(1)}, bf16[128,1024]{1,0:T(8,128)(2,1)S(1)}, u32[]{:S(2)}, u32[]{:S(2)}) collective-permute-start(bf16[128,1024]{1,0:T(8,128)(2,1)S(1)} %collective-permute-done.15.refs_11_), channel_id=1, source_target_pairs={{0,1},{1,0},{2,3},{3,2},{4,5},{5,4},{6,7},{7,6},{8,9},{9,8},{10,11... | collective-permute-start | bytes 786440 | tf_op jit(solution)/shard_map/ppermute | solution.py:39
  50.0 4.0 %collective-permute-start.17 = (bf16[128,1024]{1,0:T(8,128)(2,1)S(1)}, bf16[128,1024]{1,0:T(8,128)(2,1)S(1)}, u32[]{:S(2)}, u32[]{:S(2)}) collective-permute-start(bf16[128,1024]{1,0:T(8,128)(2,1)S(1)} %collective-permute-done.11.refs_10_), channel_id=1, source_target_pairs={{0,1},{1,0},{2,3},{3,2},{4,5},{5,4},{6,7},{7,6},{8,9},{9,8},{10,11... | collective-permute-start | bytes 786440 | tf_op jit(solution)/shard_map/ppermute | solution.py:39
  56.1 9.1 %collective-permute-start.23 = (bf16[2,64,1024]{2,1,0:T(8,128)(2,1)S(1)}, bf16[2,64,1024]{2,1,0:T(8,128)(2,1)S(1)}, u32[]{:S(2)}, u32[]{:S(2)}) collective-permute-start(bf16[2,64,1024]{2,1,0:T(8,128)(2,1)S(1)} %backward.1.refs_0_), channel_id=1, source_target_pairs={{0,2},{1,5},{2,0},{3,7},{4,6},{5,1},{6,4},{7,3},{8,12},{9,11},{10,... | collective-permute-start | bytes 786440 | tf_op jit(solution)/shard_map/ppermute | solution.py:50
  57.7 7.5 %collective-permute-start.20 = (bf16[2,64,1024]{2,1,0:T(8,128)(2,1)S(1)}, bf16[2,64,1024]{2,1,0:T(8,128)(2,1)S(1)}, u32[]{:S(2)}, u32[]{:S(2)}) collective-permute-start(bf16[2,64,1024]{2,1,0:T(8,128)(2,1)S(1)} %backward.1.refs_0_), channel_id=1, source_target_pairs={{0,4},{1,3},{2,6},{3,1},{4,0},{5,7},{6,2},{7,5},{8,10},{9,13},{10,... | collective-permute-start | bytes 786440 | tf_op jit(solution)/shard_map/ppermute | solution.py:50
  59.1 8.1 %collective-permute-start.22 = (bf16[2,64,1024]{2,1,0:T(8,128)(2,1)S(1)}, bf16[2,64,1024]{2,1,0:T(8,128)(2,1)S(1)}, u32[]{:S(2)}, u32[]{:S(2)}) collective-permute-start(bf16[2,64,1024]{2,1,0:T(8,128)(2,1)S(1)} %backward.1.refs_0_), channel_id=1, source_target_pairs={{0,1},{1,0},{2,3},{3,2},{4,5},{5,4},{6,7},{7,6},{8,9},{9,8},{10,11... | collective-permute-start | bytes 786440 | tf_op jit(solution)/shard_map/ppermute | solution.py:39
  65.2 2.0 %collective-permute-start.24 = (bf16[2,64,1024]{2,1,0:T(8,128)(2,1)S(1)}, bf16[2,64,1024]{2,1,0:T(8,128)(2,1)S(1)}, u32[]{:S(2)}, u32[]{:S(2)}) collective-permute-start(bf16[2,64,1024]{2,1,0:T(8,128)(2,1)S(1)} %collective-permute-done.23.refs_4_), channel_id=1, source_target_pairs={{0,1},{1,0},{2,3},{3,2},{4,5},{5,4},{6,7},{7,6},{8,9},{9,8},{10,11... | collective-permute-start | bytes 786440 | tf_op jit(solution)/shard_map/ppermute | solution.py:39
  65.7 6.4 %collective-permute-start.21 = (bf16[2,64,1024]{2,1,0:T(8,128)(2,1)S(1)}, bf16[2,64,1024]{2,1,0:T(8,128)(2,1)S(1)}, u32[]{:S(2)}, u32[]{:S(2)}) collective-permute-start(bf16[2,64,1024]{2,1,0:T(8,128)(2,1)S(1)} %collective-permute-done.20.refs_2_), channel_id=1, source_target_pairs={{0,2},{1,5},{2,0},{3,7},{4,6},{5,1},{6,4},{7,3},{8,12},{9,11},{10,... | collective-permute-start | bytes 786440 | tf_op jit(solution)/shard_map/ppermute | solution.py:50
  (9 other events, 50.4 us)

commit v4 on v3

--- a/solution.py
+++ b/solution.py
@@ -250,6 +250,15 @@
     scratch = [pltpu.VMEM((levels, here, width + own_rows), BF16), pltpu.VMEM((rhs_cols, own_rows), BF16)]
     arrays = [mask, *leaves, couple, sep_rhs]
     return vmem_call(kernel, arrays, y_shape + [part] * 2, scratch, "leaf_forward")
+
+
+def added_call(ours, theirs, flops):
+    def kernel(ours, theirs, out):
+        out[...] = (ours[...].astype(F32) + theirs[...].astype(F32)).astype(BF16)
+
+    spaces = [pltpu.VMEM] * 2
+    shapes = [jax.ShapeDtypeStruct(ours.shape, BF16)]
+    return kernel_call(kernel, [ours, theirs], spaces, shapes, [], "added", flops)[0]
 
 
 def paired(count):
@@ -489,10 +498,12 @@
         first = gather(own[0])
     groups, solved = [], []
     for level in range(1, levels + 1):
-        sums = added(sums, swap_layer(sums, level - 1))
+        theirs = swap_layer(sums, level - 1)
+        if four and level == 1:
+            theirs = after(theirs, last_near)
+        sums = added_call(sums, theirs, 4_000_000_000) if level == 1 else added(sums, theirs)
         if level == 1:
             if four:
-                side, far = after_all([side, far], sums, last_near)
                 first = [own[0], near, side, far, own_crossed[0], near_crossed, swap_core(side), swap_core(far)]
             groups.append(fitted(first, 1))
         elif four and level == levels:
@@ -503,7 +514,9 @@
             y, sums = level_forward_call(planes, sums, groups[level - 1])
             solved.append(y)
         if level == 1 and four:
-            last = last + [swap_link(last_near, 0), own_crossed[1], swap_core(after(last_near, y))]
+            last_near = after(last_near, y)
+            last = last + [swap_link(last_near, 0), own_crossed[1], swap_core(last_near)]
+            sums = after(sums, last[2])
     answers = backward_call(planes, sums, solved, groups)
     leaves = [mask, leaf_y, leaf_inverse, leaf_couple, leaf_diag]
     if not four or 2 * answers.shape[1] != LANES:

time: 76.2 us -> 72 us (0.945)
  waiting for transfers between devices: 33.3 us -> 29.2 us
    ppermute x10, waiting for transfers between devices: 22.8 us -> 20.5 us  [swap_link(): return lax.ppermute(value, ('layer', 'plane'), pairs)]
    ppermute x3, waiting for transfers between devices: 7.25 us -> 5.61 us  [swap_layer(): lax.ppermute(value, 'layer', [(i, i ^ 1 << stride) for i in range(layers)])]
    pallas_call x7 -> x8, Pallas kernels: 15.7 us -> 15.8 us  [kernel_call(): pl.pallas_call(kernel, in_specs=[pl.BlockSpec(memory_space=space) for spa...]
  transfers between devices with their start and end apart: 27 -> 27, of which waited for: 12 -> 11; matrix products, arithmetic and copies ran while one was open for 1% -> 1% of each run, Pallas kernels for 13% -> 14%
where the time goes in v4:
time: 72 us; the launch traced here: 71.8 us
  waiting for transfers between devices  29.2 us (41%)
  starting transfers between devices  25.4 us (35%)
  Pallas kernels  15.8 us (22%)
  between operations  0.87 us (1%)
    ppermute x10, waiting for transfers between devices, swap_link(): return lax.ppermute(value, ('layer', 'plane'), pairs)  20.5 us
    ppermute x10, starting transfers between devices, swap_link(): return lax.ppermute(value, ('layer', 'plane'), pairs)  16.4 us
    pallas_call x8, Pallas kernels, kernel_call(): pl.pallas_call(kernel, in_specs=[pl.BlockSpec(memory_space=space) for spa...  15.8 us
    ppermute x3, starting transfers between devices, swap_layer(): lax.ppermute(value, 'layer', [(i, i ^ 1 << stride) for i in range(layers)])  6.4 us
    ppermute x3, waiting for transfers between devices, swap_layer(): lax.ppermute(value, 'layer', [(i, i ^ 1 << stride) for i in range(layers)])  5.61 us
    ppermute x14, waiting for transfers between devices, swap_core(): return lax.ppermute(value, 'plane', [(i, i ^ 1) for i in range(planes)])  3.1 us
    ppermute x14, starting transfers between devices, swap_core(): return lax.ppermute(value, 'plane', [(i, i ^ 1) for i in range(planes)])  2.63 us
  transfers between devices with their start and end apart: 27, of which 11 were waited for; matrix products, arithmetic and copies ran while one was open for 1% of the time, Pallas kernels for 14%

profile of v4, /device:TPU:0, one launch (start us, length us, event | category | flops | bytes accessed | tf_op | source)
XLA Modules:
  0.0 71.8 jit_solution(6517463959824110089)
XLA Ops:
  2.1 3.0 %collective-permute-start.3 = (bf16[272,1024]{1,0:T(8,128)(2,1)S(1)}, bf16[272,1024]{1,0:T(8,128)(2,1)S(1)}, u32[]{:S(2)}, u32[]{:S(2)}) collective-permute-start(bf16[272,1024]{1,0:T(8,128)(2,1)S(1)} %get-tuple-element.25.refs_0_.refs_1_), channel_id=1, source_target_pairs={{0,4},{1,3},{2,6},{3,1},{4,0},{5,7},{6,2},{7,5},{8,10},{9,13},{10,... | collective-permute-start | bytes 1671176 | tf_op jit(solution)/shard_map/ppermute | solution.py:50
  5.2 2.2 %leaf_forward.2 = (bf16[512,1024]{1,0:T(8,128)(2,1)S(1)}, bf16[2,2,64,1024]{3,2,1,0:T(8,128)(2,1)S(1)}, bf16[2,2,64,1024]{3,2,1,0:T(8,128)(2,1)S(1)}) custom-call(s32[2,8]{1,0:T(2,128)S(1)} %bitcast.3, bf16[8,128,512]{2,1,0:T(8,128)(2,1)S(1)} %copy-done.3, bf16[8,128,128]{2,1,0:T(8,128)(2,1)S(1)} %copy-done.1, bf16[8,2,1024,128]{3,2,1,0:T(8,128)(2,1)S(1)} %copy-done, ...), custom_call_target="tpu_custom_call" | custom-call | flops 1 | bytes 1 | tf_op jit(solution)/shard_map/leaf_forward/pallas_call | solution.py:134
  8.0 1.8 %leaf_forward.3 = (bf16[2,2,64,1024]{3,2,1,0:T(8,128)(2,1)S(1)}, bf16[2,2,64,1024]{3,2,1,0:T(8,128)(2,1)S(1)}) custom-call(s32[2,8]{1,0:T(2,128)S(1)} %bitcast.4, bf16[512,1024]{1,0:T(8,128)(2,1)S(1)} %get-tuple-element.27.refs_0_.y, bf16[8,2,1024,128]{3,2,1,0:T(8,128)(2,1)S(1)} %copy-done, bf16[3,128,512]{2,1,0:T(8,128)(2,1)S(1)} %copy-done.2), custom_call_target="tpu_custom_call" | custom-call | flops 1 | bytes 1 | tf_op jit(solution)/shard_map/leaf_forward/pallas_call | solution.py:134
  9.9 2.8 %collective-permute-done.3.refs_1_.refs_2_ = bf16[272,1024]{1,0:T(8,128)(2,1)S(1)} collective-permute-done((bf16[272,1024]{1,0:T(8,128)(2,1)S(1)}, bf16[272,1024]{1,0:T(8,128)(2,1)S(1)}, u32[]{:S(2)}, u32[]{:S(2)}) %collective-permute-start.3) | collective-permute-done | bytes 557088 | tf_op jit(solution)/shard_map/ppermute | solution.py:50
  12.9 2.1 %collective-permute-start.5 = (bf16[2,2,64,1024]{3,2,1,0:T(8,128)(2,1)S(1)}, bf16[2,2,64,1024]{3,2,1,0:T(8,128)(2,1)S(1)}, u32[]{:S(2)}, u32[]{:S(2)}) collective-permute-start(bf16[2,2,64,1024]{3,2,1,0:T(8,128)(2,1)S(1)} %add_convert_fusion), channel_id=1, source_target_pairs={{0,2},{1,5},{2,0},{3,7},{4,6},{5,1},{6,4},{7,3},{8,12},{9,11},{10,... | collective-permute-start | bytes 1572872 | tf_op jit(solution)/shard_map/ppermute | solution.py:50
  15.0 1.5 %collective-permute-done.1.refs_13_ = bf16[128,1024]{1,0:T(8,128)(2,1)S(1)} collective-permute-done((bf16[128,1024]{1,0:T(8,128)(2,1)S(1)}, bf16[128,1024]{1,0:T(8,128)(2,1)S(1)}, u32[]{:S(2)}, u32[]{:S(2)}) %collective-permute-start.1) | collective-permute-done | bytes 262176 | tf_op jit(solution)/shard_map/ppermute | solution.py:39
  16.6 1.6 %collective-permute-start.8 = (bf16[272,1024]{1,0:T(8,128)(2,1)S(1)}, bf16[272,1024]{1,0:T(8,128)(2,1)S(1)}, u32[]{:S(2)}, u32[]{:S(2)}) collective-permute-start(bf16[272,1024]{1,0:T(8,128)(2,1)S(1)} %collective-permute-done.3.refs_1_.refs_2_), channel_id=1, source_target_pairs={{0,8},{8,0},{16,24},{24,16},{1,9},{9,1},{17,25},{25,17},{2,10},{10... | collective-permute-start | bytes 1671176 | tf_op jit(solution)/shard_map/ppermute | solution.py:55
  18.3 3.9 %collective-permute-done.5 = bf16[2,2,64,1024]{3,2,1,0:T(8,128)(2,1)S(1)} collective-permute-done((bf16[2,2,64,1024]{3,2,1,0:T(8,128)(2,1)S(1)}, bf16[2,2,64,1024]{3,2,1,0:T(8,128)(2,1)S(1)}, u32[]{:S(2)}, u32[]{:S(2)}) %collective-permute-start.5) | collective-permute-done | bytes 524320 | tf_op jit(solution)/shard_map/ppermute | solution.py:50
  22.3 2.1 %collective-permute-start.6 = (bf16[1,2,64,1024]{3,2,1,0:T(8,128)(2,1)S(1)}, bf16[1,2,64,1024]{3,2,1,0:T(8,128)(2,1)S(1)}, u32[]{:S(2)}, u32[]{:S(2)}) collective-permute-start(bf16[1,2,64,1024]{3,2,1,0:T(8,128)(2,1)S(1)} %add_convert_fusion.2), channel_id=1, source_target_pairs={{0,4},{1,3},{2,6},{3,1},{4,0},{5,7},{6,2},{7,5},{8,10},{9,13},{10,... | collective-permute-start | bytes 786440 | tf_op jit(solution)/shard_map/ppermute | solution.py:50
  26.4 5.2 %collective-permute-done.6 = bf16[1,2,64,1024]{3,2,1,0:T(8,128)(2,1)S(1)} collective-permute-done((bf16[1,2,64,1024]{3,2,1,0:T(8,128)(2,1)S(1)}, bf16[1,2,64,1024]{3,2,1,0:T(8,128)(2,1)S(1)}, u32[]{:S(2)}, u32[]{:S(2)}) %collective-permute-start.6) | collective-permute-done | bytes 262176 | tf_op jit(solution)/shard_map/ppermute | solution.py:50
  31.7 2.2 %collective-permute-start.9 = (bf16[2,64,1024]{2,1,0:T(8,128)(2,1)S(1)}, bf16[2,64,1024]{2,1,0:T(8,128)(2,1)S(1)}, u32[]{:S(2)}, u32[]{:S(2)}) collective-permute-start(bf16[2,64,1024]{2,1,0:T(8,128)(2,1)S(1)} %fusion.ours), channel_id=1, source_target_pairs={{0,8},{8,0},{16,24},{24,16},{1,9},{9,1},{17,25},{25,17},{2,10},{10... | collective-permute-start | bytes 786440 | tf_op jit(solution)/shard_map/ppermute | solution.py:55
  36.6 2.7 %collective-permute-done.9.theirs = bf16[2,64,1024]{2,1,0:T(8,128)(2,1)S(1)} collective-permute-done((bf16[2,64,1024]{2,1,0:T(8,128)(2,1)S(1)}, bf16[2,64,1024]{2,1,0:T(8,128)(2,1)S(1)}, u32[]{:S(2)}, u32[]{:S(2)}) %collective-permute-start.9) | collective-permute-done | bytes 262176 | tf_op jit(solution)/shard_map/ppermute | solution.py:55
  40.9 1.7 %collective-permute-start.16 = (bf16[128,1024]{1,0:T(8,128)(2,1)S(1)}, bf16[128,1024]{1,0:T(8,128)(2,1)S(1)}, u32[]{:S(2)}, u32[]{:S(2)}) collective-permute-start(bf16[128,1024]{1,0:T(8,128)(2,1)S(1)} %collective-permute-done.10.refs_10_), channel_id=1, source_target_pairs={{0,2},{1,5},{2,0},{3,7},{4,6},{5,1},{6,4},{7,3},{8,12},{9,11},{10,... | collective-permute-start | bytes 786440 | tf_op jit(solution)/shard_map/ppermute | solution.py:50
  42.6 2.6 %collective-permute-start.15 = (bf16[1,64,1024]{2,1,0:T(8,128)(2,1)S(1)}, bf16[1,64,1024]{2,1,0:T(8,128)(2,1)S(1)}, u32[]{:S(2)}, u32[]{:S(2)}) collective-permute-start(bf16[1,64,1024]{2,1,0:T(8,128)(2,1)S(1)} %get-tuple-element.42), channel_id=1, source_target_pairs={{0,16},{8,24},{16,0},{24,8},{1,17},{9,25},{17,1},{25,9},{2,18},{10... | collective-permute-start | bytes 393224 | tf_op jit(solution)/shard_map/ppermute | solution.py:55
  45.7 1.7 %collective-permute-done.16.refs_12_ = bf16[128,1024]{1,0:T(8,128)(2,1)S(1)} collective-permute-done((bf16[128,1024]{1,0:T(8,128)(2,1)S(1)}, bf16[128,1024]{1,0:T(8,128)(2,1)S(1)}, u32[]{:S(2)}, u32[]{:S(2)}) %collective-permute-start.16) | collective-permute-done | bytes 262176 | tf_op jit(solution)/shard_map/ppermute | solution.py:50
  47.4 2.9 %collective-permute-done.15 = bf16[1,64,1024]{2,1,0:T(8,128)(2,1)S(1)} collective-permute-done((bf16[1,64,1024]{2,1,0:T(8,128)(2,1)S(1)}, bf16[1,64,1024]{2,1,0:T(8,128)(2,1)S(1)}, u32[]{:S(2)}, u32[]{:S(2)}) %collective-permute-start.15) | collective-permute-done | bytes 131104 | tf_op jit(solution)/shard_map/ppermute | solution.py:55
  50.4 2.2 %backward.1.refs_0_ = bf16[2,64,1024]{2,1,0:T(8,128)(2,1)S(1)} custom-call(bf16[1,64,1024]{2,1,0:T(8,128)(2,1)S(1)} %add_convert_fusion.3.sums, bf16[64,1024]{1,0:T(8,128)(2,1)S(1)} %get-tuple-element.43.refs_0_, bf16[272,1024]{1,0:T(8,128)(2,1)S(1)} %get-tuple-element.25.refs_0_.refs_1_, bf16[272,1024]{1,0:T(8,128)(2,1)S(1)} %collective-permute-done.3.refs_1_.refs_2_, ...), custom_call_target="tpu_custom_call" | custom-call | flops 1 | bytes 1 | tf_op jit(solution)/shard_map/backward/pallas_call | solution.py:134
  52.6 1.5 %collective-permute-start.23 = (bf16[2,64,1024]{2,1,0:T(8,128)(2,1)S(1)}, bf16[2,64,1024]{2,1,0:T(8,128)(2,1)S(1)}, u32[]{:S(2)}, u32[]{:S(2)}) collective-permute-start(bf16[2,64,1024]{2,1,0:T(8,128)(2,1)S(1)} %backward.1.refs_0_), channel_id=1, source_target_pairs={{0,2},{1,5},{2,0},{3,7},{4,6},{5,1},{6,4},{7,3},{8,12},{9,11},{10,... | collective-permute-start | bytes 786440 | tf_op jit(solution)/shard_map/ppermute | solution.py:50
  54.1 1.5 %collective-permute-start.20 = (bf16[2,64,1024]{2,1,0:T(8,128)(2,1)S(1)}, bf16[2,64,1024]{2,1,0:T(8,128)(2,1)S(1)}, u32[]{:S(2)}, u32[]{:S(2)}) collective-permute-start(bf16[2,64,1024]{2,1,0:T(8,128)(2,1)S(1)} %backward.1.refs_0_), channel_id=1, source_target_pairs={{0,4},{1,3},{2,6},{3,1},{4,0},{5,7},{6,2},{7,5},{8,10},{9,13},{10,... | collective-permute-start | bytes 786440 | tf_op jit(solution)/shard_map/ppermute | solution.py:50
  55.6 5.4 %collective-permute-done.23.refs_4_ = bf16[2,64,1024]{2,1,0:T(8,128)(2,1)S(1)} collective-permute-done((bf16[2,64,1024]{2,1,0:T(8,128)(2,1)S(1)}, bf16[2,64,1024]{2,1,0:T(8,128)(2,1)S(1)}, u32[]{:S(2)}, u32[]{:S(2)}) %collective-permute-start.23) | collective-permute-done | bytes 262176 | tf_op jit(solution)/shard_map/ppermute | solution.py:50
  61.5 1.5 %collective-permute-start.21 = (bf16[2,64,1024]{2,1,0:T(8,128)(2,1)S(1)}, bf16[2,64,1024]{2,1,0:T(8,128)(2,1)S(1)}, u32[]{:S(2)}, u32[]{:S(2)}) collective-permute-start(bf16[2,64,1024]{2,1,0:T(8,128)(2,1)S(1)} %collective-permute-done.20.refs_2_), channel_id=1, source_target_pairs={{0,2},{1,5},{2,0},{3,7},{4,6},{5,1},{6,4},{7,3},{8,12},{9,11},{10,... | collective-permute-start | bytes 786440 | tf_op jit(solution)/shard_map/ppermute | solution.py:50
  63.0 4.2 %leaf_backward.2 = (bf16[8,128,512]{2,1,0:T(8,128)(2,1)}, bf16[1,2,128,512]{3,2,1,0:T(8,128)(2,1)}) custom-call(s32[2,8]{1,0:T(2,128)S(1)} %bitcast.5, bf16[512,1024]{1,0:T(8,128)(2,1)S(1)} %get-tuple-element.27.refs_0_.y, bf16[8,128,128]{2,1,0:T(8,128)(2,1)S(1)} %copy-done.1, bf16[8,2,1024,128]{3,2,1,0:T(8,128)(2,1)S(1)} %copy-done, ...), custom_call_target="tpu_custom_call" | custom-call | flops 1 | bytes 1 | tf_op jit(solution)/shard_map/leaf_backward/pallas_call | solution.py:134
  67.9 1.5 %collective-permute-done.26.refs_1_ = bf16[2,64,1024]{2,1,0:T(8,128)(2,1)S(1)} collective-permute-done((bf16[2,64,1024]{2,1,0:T(8,128)(2,1)S(1)}, bf16[2,64,1024]{2,1,0:T(8,128)(2,1)S(1)}, u32[]{:S(2)}, u32[]{:S(2)}) %collective-permute-start.26) | collective-permute-done | bytes 262176 | tf_op jit(solution)/shard_map/ppermute | solution.py:39
  69.4 2.4 %leaf_backward.3 = (bf16[8,128,512]{2,1,0:T(8,128)(2,1)}, bf16[1,2,128,512]{3,2,1,0:T(8,128)(2,1)}) custom-call(s32[2,8]{1,0:T(2,128)S(1)} %bitcast.6, bf16[512,1024]{1,0:T(8,128)(2,1)S(1)} %get-tuple-element.27.refs_0_.y, bf16[8,128,128]{2,1,0:T(8,128)(2,1)S(1)} %copy-done.1, ...), custom_call_target="tpu_custom_call", output_to_operand_aliasing={{0}: (7, {}), {1}: (8, {})} | custom-call | flops 1 | bytes 1 | tf_op jit(solution)/shard_map/leaf_backward/pallas_call | solution.py:134
  (54 shorter events, 10.8 us)
Async XLA Ops:
  2.1 10.5 %collective-permute-start.3 = (bf16[272,1024]{1,0:T(8,128)(2,1)S(1)}, bf16[272,1024]{1,0:T(8,128)(2,1)S(1)}, u32[]{:S(2)}, u32[]{:S(2)}) collective-permute-start(bf16[272,1024]{1,0:T(8,128)(2,1)S(1)} %get-tuple-element.25.refs_0_.refs_1_), channel_id=1, source_target_pairs={{0,4},{1,3},{2,6},{3,1},{4,0},{5,7},{6,2},{7,5},{8,10},{9,13},{10,... | collective-permute-start | bytes 1671176 | tf_op jit(solution)/shard_map/ppermute | solution.py:50
  7.4 5.3 %collective-permute-start.4 = (bf16[2,2,64,1024]{3,2,1,0:T(8,128)(2,1)S(1)}, bf16[2,2,64,1024]{3,2,1,0:T(8,128)(2,1)S(1)}, u32[]{:S(2)}, u32[]{:S(2)}) collective-permute-start(bf16[2,2,64,1024]{3,2,1,0:T(8,128)(2,1)S(1)} %get-tuple-element.34), channel_id=1, source_target_pairs={{0,1},{1,0},{2,3},{3,2},{4,5},{5,4},{6,7},{7,6},{8,9},{9,8},{10,11... | collective-permute-start | bytes 1572872 | tf_op jit(solution)/shard_map/ppermute | solution.py:39
  7.5 9.0 %collective-permute-start = (bf16[272,1024]{1,0:T(8,128)(2,1)S(1)}, bf16[272,1024]{1,0:T(8,128)(2,1)S(1)}, u32[]{:S(2)}, u32[]{:S(2)}) collective-permute-start(bf16[272,1024]{1,0:T(8,128)(2,1)S(1)} %get-tuple-element.25.refs_0_.refs_1_), channel_id=1, source_target_pairs={{0,1},{1,0},{2,3},{3,2},{4,5},{5,4},{6,7},{7,6},{8,9},{9,8},{10,11... | collective-permute-start | bytes 1671176 | tf_op jit(solution)/shard_map/ppermute | solution.py:39
  9.8 8.5 %collective-permute-start.2 = (bf16[2,2,64,1024]{3,2,1,0:T(8,128)(2,1)S(1)}, bf16[2,2,64,1024]{3,2,1,0:T(8,128)(2,1)S(1)}, u32[]{:S(2)}, u32[]{:S(2)}) collective-permute-start(bf16[2,2,64,1024]{3,2,1,0:T(8,128)(2,1)S(1)} %get-tuple-element.31), channel_id=1, source_target_pairs={{0,1},{1,0},{2,3},{3,2},{4,5},{5,4},{6,7},{7,6},{8,9},{9,8},{10,11... | collective-permute-start | bytes 1572872 | tf_op jit(solution)/shard_map/ppermute | solution.py:39
  12.9 9.2 %collective-permute-start.5 = (bf16[2,2,64,1024]{3,2,1,0:T(8,128)(2,1)S(1)}, bf16[2,2,64,1024]{3,2,1,0:T(8,128)(2,1)S(1)}, u32[]{:S(2)}, u32[]{:S(2)}) collective-permute-start(bf16[2,2,64,1024]{3,2,1,0:T(8,128)(2,1)S(1)} %add_convert_fusion), channel_id=1, source_target_pairs={{0,2},{1,5},{2,0},{3,7},{4,6},{5,1},{6,4},{7,3},{8,12},{9,11},{10,... | collective-permute-start | bytes 1572872 | tf_op jit(solution)/shard_map/ppermute | solution.py:50
  16.5 15.2 %collective-permute-start.7 = (bf16[272,1024]{1,0:T(8,128)(2,1)S(1)}, bf16[272,1024]{1,0:T(8,128)(2,1)S(1)}, u32[]{:S(2)}, u32[]{:S(2)}) collective-permute-start(bf16[272,1024]{1,0:T(8,128)(2,1)S(1)} %collective-permute-done.3.refs_1_.refs_2_), channel_id=1, source_target_pairs={{0,1},{1,0},{2,3},{3,2},{4,5},{5,4},{6,7},{7,6},{8,9},{9,8},{10,11... | collective-permute-start | bytes 1671176 | tf_op jit(solution)/shard_map/ppermute | solution.py:39
  16.6 15.1 %collective-permute-start.8 = (bf16[272,1024]{1,0:T(8,128)(2,1)S(1)}, bf16[272,1024]{1,0:T(8,128)(2,1)S(1)}, u32[]{:S(2)}, u32[]{:S(2)}) collective-permute-start(bf16[272,1024]{1,0:T(8,128)(2,1)S(1)} %collective-permute-done.3.refs_1_.refs_2_), channel_id=1, source_target_pairs={{0,8},{8,0},{16,24},{24,16},{1,9},{9,1},{17,25},{25,17},{2,10},{10... | collective-permute-start | bytes 1671176 | tf_op jit(solution)/shard_map/ppermute | solution.py:55
  22.3 9.3 %collective-permute-start.6 = (bf16[1,2,64,1024]{3,2,1,0:T(8,128)(2,1)S(1)}, bf16[1,2,64,1024]{3,2,1,0:T(8,128)(2,1)S(1)}, u32[]{:S(2)}, u32[]{:S(2)}) collective-permute-start(bf16[1,2,64,1024]{3,2,1,0:T(8,128)(2,1)S(1)} %add_convert_fusion.2), channel_id=1, source_target_pairs={{0,4},{1,3},{2,6},{3,1},{4,0},{5,7},{6,2},{7,5},{8,10},{9,13},{10,... | collective-permute-start | bytes 786440 | tf_op jit(solution)/shard_map/ppermute | solution.py:50
  24.4 10.6 %collective-permute-start.11 = (bf16[272,1024]{1,0:T(8,128)(2,1)S(1)}, bf16[272,1024]{1,0:T(8,128)(2,1)S(1)}, u32[]{:S(2)}, u32[]{:S(2)}) collective-permute-start(bf16[272,1024]{1,0:T(8,128)(2,1)S(1)} %collective-permute-done.3.refs_1_.refs_2_), channel_id=1, source_target_pairs={{0,2},{1,5},{2,0},{3,7},{4,6},{5,1},{6,4},{7,3},{8,12},{9,11},{10,... | collective-permute-start | bytes 1671176 | tf_op jit(solution)/shard_map/ppermute | solution.py:50
  25.8 10.8 %collective-permute-start.10 = (bf16[128,1024]{1,0:T(8,128)(2,1)S(1)}, bf16[128,1024]{1,0:T(8,128)(2,1)S(1)}, u32[]{:S(2)}, u32[]{:S(2)}) collective-permute-start(bf16[128,1024]{1,0:T(8,128)(2,1)S(1)} %get-tuple-element.41.refs_9_), channel_id=1, source_target_pairs={{0,4},{1,3},{2,6},{3,1},{4,0},{5,7},{6,2},{7,5},{8,10},{9,13},{10,... | collective-permute-start | bytes 786440 | tf_op jit(solution)/shard_map/ppermute | solution.py:50
  31.7 7.6 %collective-permute-start.9 = (bf16[2,64,1024]{2,1,0:T(8,128)(2,1)S(1)}, bf16[2,64,1024]{2,1,0:T(8,128)(2,1)S(1)}, u32[]{:S(2)}, u32[]{:S(2)}) collective-permute-start(bf16[2,64,1024]{2,1,0:T(8,128)(2,1)S(1)} %fusion.ours), channel_id=1, source_target_pairs={{0,8},{8,0},{16,24},{24,16},{1,9},{9,1},{17,25},{25,17},{2,10},{10... | collective-permute-start | bytes 786440 | tf_op jit(solution)/shard_map/ppermute | solution.py:55
  33.9 5.5 %collective-permute-start.12 = (bf16[272,1024]{1,0:T(8,128)(2,1)S(1)}, bf16[272,1024]{1,0:T(8,128)(2,1)S(1)}, u32[]{:S(2)}, u32[]{:S(2)}) collective-permute-start(bf16[272,1024]{1,0:T(8,128)(2,1)S(1)} %collective-permute-done.8.refs_2_.refs_3_), channel_id=1, source_target_pairs={{0,1},{1,0},{2,3},{3,2},{4,5},{5,4},{6,7},{7,6},{8,9},{9,8},{10,11... | collective-permute-start | bytes 1671176 | tf_op jit(solution)/shard_map/ppermute | solution.py:39
  34.9 4.5 %collective-permute-start.13 = (bf16[272,1024]{1,0:T(8,128)(2,1)S(1)}, bf16[272,1024]{1,0:T(8,128)(2,1)S(1)}, u32[]{:S(2)}, u32[]{:S(2)}) collective-permute-start(bf16[272,1024]{1,0:T(8,128)(2,1)S(1)} %collective-permute-done.11.refs_3_.refs_4_), channel_id=1, source_target_pairs={{0,1},{1,0},{2,3},{3,2},{4,5},{5,4},{6,7},{7,6},{8,9},{9,8},{10,11... | collective-permute-start | bytes 1671176 | tf_op jit(solution)/shard_map/ppermute | solution.py:39
  35.7 6.9 %collective-permute-start.14 = (bf16[128,1024]{1,0:T(8,128)(2,1)S(1)}, bf16[128,1024]{1,0:T(8,128)(2,1)S(1)}, u32[]{:S(2)}, u32[]{:S(2)}) collective-permute-start(bf16[128,1024]{1,0:T(8,128)(2,1)S(1)} %get-tuple-element.41.refs_9_), channel_id=1, source_target_pairs={{0,2},{1,5},{2,0},{3,7},{4,6},{5,1},{6,4},{7,3},{8,12},{9,11},{10,... | collective-permute-start | bytes 786440 | tf_op jit(solution)/shard_map/ppermute | solution.py:50
  40.9 6.4 %collective-permute-start.16 = (bf16[128,1024]{1,0:T(8,128)(2,1)S(1)}, bf16[128,1024]{1,0:T(8,128)(2,1)S(1)}, u32[]{:S(2)}, u32[]{:S(2)}) collective-permute-start(bf16[128,1024]{1,0:T(8,128)(2,1)S(1)} %collective-permute-done.10.refs_10_), channel_id=1, source_target_pairs={{0,2},{1,5},{2,0},{3,7},{4,6},{5,1},{6,4},{7,3},{8,12},{9,11},{10,... | collective-permute-start | bytes 786440 | tf_op jit(solution)/shard_map/ppermute | solution.py:50
  42.6 7.7 %collective-permute-start.15 = (bf16[1,64,1024]{2,1,0:T(8,128)(2,1)S(1)}, bf16[1,64,1024]{2,1,0:T(8,128)(2,1)S(1)}, u32[]{:S(2)}, u32[]{:S(2)}) collective-permute-start(bf16[1,64,1024]{2,1,0:T(8,128)(2,1)S(1)} %get-tuple-element.42), channel_id=1, source_target_pairs={{0,16},{8,24},{16,0},{24,8},{1,17},{9,25},{17,1},{25,9},{2,18},{10... | collective-permute-start | bytes 393224 | tf_op jit(solution)/shard_map/ppermute | solution.py:55
  45.2 5.2 %collective-permute-start.18 = (bf16[128,1024]{1,0:T(8,128)(2,1)S(1)}, bf16[128,1024]{1,0:T(8,128)(2,1)S(1)}, u32[]{:S(2)}, u32[]{:S(2)}) collective-permute-start(bf16[128,1024]{1,0:T(8,128)(2,1)S(1)} %collective-permute-done.14.refs_11_), channel_id=1, source_target_pairs={{0,1},{1,0},{2,3},{3,2},{4,5},{5,4},{6,7},{7,6},{8,9},{9,8},{10,11... | collective-permute-start | bytes 786440 | tf_op jit(solution)/shard_map/ppermute | solution.py:39
  45.2 5.2 %collective-permute-start.17 = (bf16[128,1024]{1,0:T(8,128)(2,1)S(1)}, bf16[128,1024]{1,0:T(8,128)(2,1)S(1)}, u32[]{:S(2)}, u32[]{:S(2)}) collective-permute-start(bf16[128,1024]{1,0:T(8,128)(2,1)S(1)} %collective-permute-done.10.refs_10_), channel_id=1, source_target_pairs={{0,1},{1,0},{2,3},{3,2},{4,5},{5,4},{6,7},{7,6},{8,9},{9,8},{10,11... | collective-permute-start | bytes 786440 | tf_op jit(solution)/shard_map/ppermute | solution.py:39
  47.4 3.0 %collective-permute-start.19 = (bf16[128,1024]{1,0:T(8,128)(2,1)S(1)}, bf16[128,1024]{1,0:T(8,128)(2,1)S(1)}, u32[]{:S(2)}, u32[]{:S(2)}) collective-permute-start(bf16[128,1024]{1,0:T(8,128)(2,1)S(1)} %collective-permute-done.16.refs_12_), channel_id=1, source_target_pairs={{0,1},{1,0},{2,3},{3,2},{4,5},{5,4},{6,7},{7,6},{8,9},{9,8},{10,11... | collective-permute-start | bytes 786440 | tf_op jit(solution)/shard_map/ppermute | solution.py:39
  52.6 8.4 %collective-permute-start.23 = (bf16[2,64,1024]{2,1,0:T(8,128)(2,1)S(1)}, bf16[2,64,1024]{2,1,0:T(8,128)(2,1)S(1)}, u32[]{:S(2)}, u32[]{:S(2)}) collective-permute-start(bf16[2,64,1024]{2,1,0:T(8,128)(2,1)S(1)} %backward.1.refs_0_), channel_id=1, source_target_pairs={{0,2},{1,5},{2,0},{3,7},{4,6},{5,1},{6,4},{7,3},{8,12},{9,11},{10,... | collective-permute-start | bytes 786440 | tf_op jit(solution)/shard_map/ppermute | solution.py:50
  54.1 6.9 %collective-permute-start.20 = (bf16[2,64,1024]{2,1,0:T(8,128)(2,1)S(1)}, bf16[2,64,1024]{2,1,0:T(8,128)(2,1)S(1)}, u32[]{:S(2)}, u32[]{:S(2)}) collective-permute-start(bf16[2,64,1024]{2,1,0:T(8,128)(2,1)S(1)} %backward.1.refs_0_), channel_id=1, source_target_pairs={{0,4},{1,3},{2,6},{3,1},{4,0},{5,7},{6,2},{7,5},{8,10},{9,13},{10,... | collective-permute-start | bytes 786440 | tf_op jit(solution)/shard_map/ppermute | solution.py:50
  55.6 7.4 %collective-permute-start.22 = (bf16[2,64,1024]{2,1,0:T(8,128)(2,1)S(1)}, bf16[2,64,1024]{2,1,0:T(8,128)(2,1)S(1)}, u32[]{:S(2)}, u32[]{:S(2)}) collective-permute-start(bf16[2,64,1024]{2,1,0:T(8,128)(2,1)S(1)} %backward.1.refs_0_), channel_id=1, source_target_pairs={{0,1},{1,0},{2,3},{3,2},{4,5},{5,4},{6,7},{7,6},{8,9},{9,8},{10,11... | collective-permute-start | bytes 786440 | tf_op jit(solution)/shard_map/ppermute | solution.py:39
  61.0 2.0 %collective-permute-start.24 = (bf16[2,64,1024]{2,1,0:T(8,128)(2,1)S(1)}, bf16[2,64,1024]{2,1,0:T(8,128)(2,1)S(1)}, u32[]{:S(2)}, u32[]{:S(2)}) collective-permute-start(bf16[2,64,1024]{2,1,0:T(8,128)(2,1)S(1)} %collective-permute-done.23.refs_4_), channel_id=1, source_target_pairs={{0,1},{1,0},{2,3},{3,2},{4,5},{5,4},{6,7},{7,6},{8,9},{9,8},{10,11... | collective-permute-start | bytes 786440 | tf_op jit(solution)/shard_map/ppermute | solution.py:39
  61.5 6.4 %collective-permute-start.21 = (bf16[2,64,1024]{2,1,0:T(8,128)(2,1)S(1)}, bf16[2,64,1024]{2,1,0:T(8,128)(2,1)S(1)}, u32[]{:S(2)}, u32[]{:S(2)}) collective-permute-start(bf16[2,64,1024]{2,1,0:T(8,128)(2,1)S(1)} %collective-permute-done.20.refs_2_), channel_id=1, source_target_pairs={{0,2},{1,5},{2,0},{3,7},{4,6},{5,1},{6,4},{7,3},{8,12},{9,11},{10,... | collective-permute-start | bytes 786440 | tf_op jit(solution)/shard_map/ppermute | solution.py:50
  (9 other events, 49.9 us)

commit v5 on v4

--- a/solution.py
+++ b/solution.py
@@ -70,17 +70,14 @@
     return total.astype(BF16)
 
 
-def scatter_sum(low, high, first_after):
-    arrived = []
+def scatter_sum(low, high):
+    parts = list(low)
     for place in range(len(bit_orders(lax.axis_size("plane"))[0])):
-        send = added(*high)
-        if place == 0:
-            send = after(send, *first_after)
-        arrived.append(swap_link(send, place))
-        terms = [*low, arrived[-1]]
-        half = terms[0].shape[0] // 2
-        low, high = [term[:half] for term in terms], [term[half:] for term in terms]
-    return added(*[term[0] for term in terms]), arrived
+        parts.append(swap_link(added(*high), place))
+        low = [*low, parts[-1]]
+        half = low[0].shape[0] // 2
+        low, high = [term[:half] for term in low], [term[half:] for term in low]
+    return parts, parts[-len(bit_orders(lax.axis_size("plane"))[0]) :]
 
 
 def gather(value, cross=True):
@@ -200,7 +197,7 @@
     )
 
 
-def leaf_forward_call(mask, leaves, couple, sep_rhs, slots, layers):
+def leaf_forward_call(mask, leaves, couple, sep_rhs, slots, layers, apart):
     first = len(leaves) == 2
     blocks, levels, sep_rows, block_rows = couple.shape
     own_rows, rhs_cols = sep_rhs.shape[1:]
@@ -243,13 +240,50 @@
                 total = nt(scaled[level], weights).astype(BF16)
                 half = len(slots) // 2
                 for at in range(len(slots)):
-                    parts[at // half][at % half, level, :, lanes] = total[at * cols : (at + 1) * cols]
+                    value = total[at * cols : (at + 1) * cols]
+                    if at < half:
+                        parts[0][at, level, :, lanes] = value
+                    elif apart:
+                        parts[1 + level][at - half, :, lanes] = value
+                    else:
+                        parts[1][at - half, level, :, lanes] = value
 
     part = jax.ShapeDtypeStruct((len(slots) // 2, levels, cols, sep_rows), BF16)
     y_shape = [jax.ShapeDtypeStruct((rhs_cols, width), BF16)] if first else []
     scratch = [pltpu.VMEM((levels, here, width + own_rows), BF16), pltpu.VMEM((rhs_cols, own_rows), BF16)]
     arrays = [mask, *leaves, couple, sep_rhs]
-    return vmem_call(kernel, arrays, y_shape + [part] * 2, scratch, "leaf_forward")
+    one = jax.ShapeDtypeStruct((len(slots) // 2, cols, sep_rows), BF16)
+    sent = [one] * levels if apart else [part]
+    return vmem_call(kernel, arrays, [*y_shape, part, *sent], scratch, "leaf_forward")
+
+
+def joined_call(kept, others):
+    def kernel(kept, *refs):
+        for level, other in enumerate(refs[:-1]):
+            refs[-1][:, level] = (kept[:, level].astype(F32) + other[...].astype(F32)).astype(BF16)
+
+    return vmem_call(kernel, [kept, *others], [jax.ShapeDtypeStruct(kept.shape, BF16)], [], "joined")[0]
+
+
+def first_call(parts, seen):
+    def kernel(*refs):
+        total = refs[0][0].astype(F32)
+        for ref in refs[1 : len(parts)]:
+            total = total + ref[0].astype(F32)
+        refs[-1][...] = total.astype(BF16)
+
+    shapes = [jax.ShapeDtypeStruct(parts[0].shape[1:], BF16)]
+    return vmem_call(kernel, [*parts, *seen], shapes, [], "first")[0]
+
+
+def seen_call(value, flops):
+    rows, lanes = min(DIAG_ROWS, value.shape[0]), min(LANES, value.shape[1])
+
+    def kernel(value, out):
+        out[...] = value[:rows, :lanes]
+
+    shapes = [jax.ShapeDtypeStruct((rows, lanes), BF16)]
+    return kernel_call(kernel, [value], [pltpu.VMEM], shapes, [], "seen", flops)[0]
 
 
 def added_call(ours, theirs, flops):
@@ -469,14 +503,14 @@
     quarter = planes // 4
     highs = [slot for slot in range(planes) if slot // quarter % 2 == 1]
     lows = [slot for slot in range(planes) if slot // quarter % 2 == 0]
-    leaf_y, keep, send = leaf_forward_call(
-        mask, [leaf_rhs, leaf_inverse], leaf_couple, sep_rhs, highs, layers
+    leaf_y, keep, *send = leaf_forward_call(
+        mask, [leaf_rhs, leaf_inverse], leaf_couple, sep_rhs, highs, layers, True
     )
-    high = [after(keep, near), swap_core(send)]
-    keep, send = leaf_forward_call(mask, [leaf_y], leaf_couple, sep_rhs, lows, layers)
-    own_crossed = [swap_core(own[0]), swap_core(own[-1])] if four else []
-    low = [after(keep, *own_crossed), swap_core(send)]
-    sums, arrived = scatter_sum(low, high, [])
+    high = [joined_call(keep, [swap_core(part) for part in send])]
+    keep, send = leaf_forward_call(mask, [leaf_y], leaf_couple, sep_rhs, lows, layers, False)
+    low = [keep, swap_core(send)]
+    parts, arrived = scatter_sum(low, high)
+    seen = []
 
     def fitted(pieces, level):
         if own_rows == LANES:
@@ -487,15 +521,18 @@
         return repacked(pieces, jnp.argsort(slots).astype(jnp.int32), 1 + levels - level, own_rows)
 
     if four:
-        near_crossed = swap_core(after(near, keep))
+        own_crossed = swap_core(after(own[0], arrived[0]))
+        near_crossed = swap_core(after(near, arrived[0]))
         side = swap_layer(near, 0)
         far = swap_link(after(near, arrived[0]), 0)
         last_own = after(own[-1], arrived[0])
         last_near = swap_link(last_own, 1)
-        sums = after(sums, near_crossed, side)
+        parts[0] = after(parts[0], own_crossed, near_crossed)
+        seen = [seen_call(side, 3_000_000_000)]
         last = [own[-1], last_near, swap_link(after(last_own, arrived[1]), 0)]
     else:
         first = gather(own[0])
+    sums = first_call(parts, seen)
     groups, solved = [], []
     for level in range(1, levels + 1):
         theirs = swap_layer(sums, level - 1)
@@ -504,7 +541,7 @@
         sums = added_call(sums, theirs, 4_000_000_000) if level == 1 else added(sums, theirs)
         if level == 1:
             if four:
-                first = [own[0], near, side, far, own_crossed[0], near_crossed, swap_core(side), swap_core(far)]
+                first = [own[0], near, side, far, own_crossed, near_crossed, swap_core(side), swap_core(far)]
             groups.append(fitted(first, 1))
         elif four and level == levels:
             groups.append(fitted(last + [swap_core(piece) for piece in last[2:4]], level))
@@ -515,7 +552,7 @@
             solved.append(y)
         if level == 1 and four:
             last_near = after(last_near, y)
-            last = last + [swap_link(last_near, 0), own_crossed[1], swap_core(last_near)]
+            last = last + [swap_link(last_near, 0), *[swap_core(piece) for piece in after_all([last[0], last_near], y)]]
             sums = after(sums, last[2])
     answers = backward_call(planes, sums, solved, groups)
     leaves = [mask, leaf_y, leaf_inverse, leaf_couple, leaf_diag]

time: 72 us -> 70.6 us (0.981)
  waiting for transfers between devices: 29.2 us -> 27.1 us
  starting transfers between devices: 25.4 us -> 26.2 us
    ppermute x10, waiting for transfers between devices: 20.5 us -> 13.2 us  [swap_link(): return lax.ppermute(value, ('layer', 'plane'), pairs)]
    ppermute x3, waiting for transfers between devices: 5.61 us -> 11 us  [swap_layer(): lax.ppermute(value, 'layer', [(i, i ^ 1 << stride) for i in range(layers)])]
    ppermute x10, starting transfers between devices: 16.4 us -> 17.4 us  [swap_link(): return lax.ppermute(value, ('layer', 'plane'), pairs)]
    ppermute x14 -> x15, starting transfers between devices: 2.63 us -> 2.19 us  [swap_core(): return lax.ppermute(value, 'plane', [(i, i ^ 1) for i in range(planes)])]
    pallas_call x8 -> x11, Pallas kernels: 15.8 us -> 16 us  [kernel_call(): pl.pallas_call(kernel, in_specs=[pl.BlockSpec(memory_space=space) for spa...]
    ppermute x14 -> x15, waiting for transfers between devices: 3.1 us -> 2.96 us  [swap_core(): return lax.ppermute(value, 'plane', [(i, i ^ 1) for i in range(planes)])]
  transfers between devices with their start and end apart: 27 -> 28, of which waited for: 11 -> 13; matrix products, arithmetic and copies ran while one was open for 1% -> 0% of each run, Pallas kernels for 14% -> 14%
where the time goes in v5:
time: 70.6 us; the launch traced here: 70.5 us
  waiting for transfers between devices  27.1 us (38%)
  starting transfers between devices  26.2 us (37%)
  Pallas kernels  16 us (23%)
  between operations  0.86 us (1%)
    ppermute x10, starting transfers between devices, swap_link(): return lax.ppermute(value, ('layer', 'plane'), pairs)  17.4 us
    pallas_call x11, Pallas kernels, kernel_call(): pl.pallas_call(kernel, in_specs=[pl.BlockSpec(memory_space=space) for spa...  16 us
    ppermute x10, waiting for transfers between devices, swap_link(): return lax.ppermute(value, ('layer', 'plane'), pairs)  13.2 us
    ppermute x3, waiting for transfers between devices, swap_layer(): lax.ppermute(value, 'layer', [(i, i ^ 1 << stride) for i in range(layers)])  11 us
    ppermute x3, starting transfers between devices, swap_layer(): lax.ppermute(value, 'layer', [(i, i ^ 1 << stride) for i in range(layers)])  6.64 us
    ppermute x15, waiting for transfers between devices, swap_core(): return lax.ppermute(value, 'plane', [(i, i ^ 1) for i in range(planes)])  2.96 us
    ppermute x15, starting transfers between devices, swap_core(): return lax.ppermute(value, 'plane', [(i, i ^ 1) for i in range(planes)])  2.19 us
  transfers between devices with their start and end apart: 28, of which 13 were waited for; matrix products, arithmetic and copies ran while one was open for 0% of the time, Pallas kernels for 14%

profile of v5, /device:TPU:0, one launch (start us, length us, event | category | flops | bytes accessed | tf_op | source)
XLA Modules:
  0.0 70.5 jit_solution(16617124181437876085)
XLA Ops:
  2.1 3.0 %collective-permute-start.4 = (bf16[272,1024]{1,0:T(8,128)(2,1)S(1)}, bf16[272,1024]{1,0:T(8,128)(2,1)S(1)}, u32[]{:S(2)}, u32[]{:S(2)}) collective-permute-start(bf16[272,1024]{1,0:T(8,128)(2,1)S(1)} %get-tuple-element.33.refs_0_.refs_1_), channel_id=1, source_target_pairs={{0,4},{1,3},{2,6},{3,1},{4,0},{5,7},{6,2},{7,5},{8,10},{9,13},{10,... | collective-permute-start | bytes 1671176 | tf_op jit(solution)/shard_map/ppermute | solution.py:50
  5.2 2.2 %leaf_forward.2 = (bf16[512,1024]{1,0:T(8,128)(2,1)S(1)}, bf16[2,2,64,1024]{3,2,1,0:T(8,128)(2,1)S(1)}, bf16[2,64,1024]{2,1,0:T(8,128)(2,1)S(1)}, bf16[2,64,1024]{2,1,0:T(8,128)(2,1)S(1)}) custom-call(s32[2,8]{1,0:T(2,128)S(1)} %bitcast.1, bf16[8,128,512]{2,1,0:T(8,128)(2,1)S(1)} %copy-done.3, bf16[8,128,128]{2,1,0:T(8,128)(2,1)S(1)} %copy-done.1, ...), custom_call_target="tpu_custom_call" | custom-call | flops 1 | bytes 1 | tf_op jit(solution)/shard_map/leaf_forward/pallas_call | solution.py:131
  9.5 1.6 %collective-permute-start.2 = (bf16[2,2,64,1024]{3,2,1,0:T(8,128)(2,1)S(1)}, bf16[2,2,64,1024]{3,2,1,0:T(8,128)(2,1)S(1)}, u32[]{:S(2)}, u32[]{:S(2)}) collective-permute-start(bf16[2,2,64,1024]{3,2,1,0:T(8,128)(2,1)S(1)} %joined.1), channel_id=1, source_target_pairs={{0,2},{1,5},{2,0},{3,7},{4,6},{5,1},{6,4},{7,3},{8,12},{9,11},{10,... | collective-permute-start | bytes 1572872 | tf_op jit(solution)/shard_map/ppermute | solution.py:50
  11.1 1.8 %leaf_forward.3 = (bf16[2,2,64,1024]{3,2,1,0:T(8,128)(2,1)S(1)}, bf16[2,2,64,1024]{3,2,1,0:T(8,128)(2,1)S(1)}) custom-call(s32[2,8]{1,0:T(2,128)S(1)} %bitcast.2, bf16[512,1024]{1,0:T(8,128)(2,1)S(1)} %get-tuple-element.28.refs_0_.y, bf16[8,2,1024,128]{3,2,1,0:T(8,128)(2,1)S(1)} %copy-done, bf16[3,128,512]{2,1,0:T(8,128)(2,1)S(1)} %copy-done.2), custom_call_target="tpu_custom_call" | custom-call | flops 1 | bytes 1 | tf_op jit(solution)/shard_map/leaf_forward/pallas_call | solution.py:131
  13.2 2.4 %collective-permute-start.8 = (bf16[272,1024]{1,0:T(8,128)(2,1)S(1)}, bf16[272,1024]{1,0:T(8,128)(2,1)S(1)}, u32[]{:S(2)}, u32[]{:S(2)}) collective-permute-start(bf16[272,1024]{1,0:T(8,128)(2,1)S(1)} %collective-permute-done.4.refs_1_.refs_2_), channel_id=1, source_target_pairs={{0,8},{8,0},{16,24},{24,16},{1,9},{9,1},{17,25},{25,17},{2,10},{10... | collective-permute-start | bytes 1671176 | tf_op jit(solution)/shard_map/ppermute | solution.py:55
  15.6 3.2 %collective-permute-done.2.refs_2_ = bf16[2,2,64,1024]{3,2,1,0:T(8,128)(2,1)S(1)} collective-permute-done((bf16[2,2,64,1024]{3,2,1,0:T(8,128)(2,1)S(1)}, bf16[2,2,64,1024]{3,2,1,0:T(8,128)(2,1)S(1)}, u32[]{:S(2)}, u32[]{:S(2)}) %collective-permute-start.2) | collective-permute-done | bytes 524320 | tf_op jit(solution)/shard_map/ppermute | solution.py:50
  19.3 1.5 %collective-permute-start.11 = (bf16[272,1024]{1,0:T(8,128)(2,1)S(1)}, bf16[272,1024]{1,0:T(8,128)(2,1)S(1)}, u32[]{:S(2)}, u32[]{:S(2)}) collective-permute-start(bf16[272,1024]{1,0:T(8,128)(2,1)S(1)} %collective-permute-done.4.refs_1_.refs_2_), channel_id=1, source_target_pairs={{0,2},{1,5},{2,0},{3,7},{4,6},{5,1},{6,4},{7,3},{8,12},{9,11},{10,... | collective-permute-start | bytes 1671176 | tf_op jit(solution)/shard_map/ppermute | solution.py:50
  22.3 5.6 %collective-permute-done.8.value.refs_2_.refs_3_ = bf16[272,1024]{1,0:T(8,128)(2,1)S(1)} collective-permute-done((bf16[272,1024]{1,0:T(8,128)(2,1)S(1)}, bf16[272,1024]{1,0:T(8,128)(2,1)S(1)}, u32[]{:S(2)}, u32[]{:S(2)}) %collective-permute-start.8) | collective-permute-done | bytes 557088 | tf_op jit(solution)/shard_map/ppermute | solution.py:55
  30.3 1.6 %collective-permute-start.9 = (bf16[2,64,1024]{2,1,0:T(8,128)(2,1)S(1)}, bf16[2,64,1024]{2,1,0:T(8,128)(2,1)S(1)}, u32[]{:S(2)}, u32[]{:S(2)}) collective-permute-start(bf16[2,64,1024]{2,1,0:T(8,128)(2,1)S(1)} %first.1.ours), channel_id=1, source_target_pairs={{0,8},{8,0},{16,24},{24,16},{1,9},{9,1},{17,25},{25,17},{2,10},{10... | collective-permute-start | bytes 786440 | tf_op jit(solution)/shard_map/ppermute | solution.py:55
  32.0 1.6 %collective-permute-done.11.refs_3_.refs_4_ = bf16[272,1024]{1,0:T(8,128)(2,1)S(1)} collective-permute-done((bf16[272,1024]{1,0:T(8,128)(2,1)S(1)}, bf16[272,1024]{1,0:T(8,128)(2,1)S(1)}, u32[]{:S(2)}, u32[]{:S(2)}) %collective-permute-start.11) | collective-permute-done | bytes 557088 | tf_op jit(solution)/shard_map/ppermute | solution.py:50
  33.6 2.1 %collective-permute-start.14 = (bf16[128,1024]{1,0:T(8,128)(2,1)S(1)}, bf16[128,1024]{1,0:T(8,128)(2,1)S(1)}, u32[]{:S(2)}, u32[]{:S(2)}) collective-permute-start(bf16[128,1024]{1,0:T(8,128)(2,1)S(1)} %get-tuple-element.45.refs_9_), channel_id=1, source_target_pairs={{0,2},{1,5},{2,0},{3,7},{4,6},{5,1},{6,4},{7,3},{8,12},{9,11},{10,... | collective-permute-start | bytes 786440 | tf_op jit(solution)/shard_map/ppermute | solution.py:50
  35.7 1.9 %collective-permute-done.9.theirs = bf16[2,64,1024]{2,1,0:T(8,128)(2,1)S(1)} collective-permute-done((bf16[2,64,1024]{2,1,0:T(8,128)(2,1)S(1)}, bf16[2,64,1024]{2,1,0:T(8,128)(2,1)S(1)}, u32[]{:S(2)}, u32[]{:S(2)}) %collective-permute-start.9) | collective-permute-done | bytes 262176 | tf_op jit(solution)/shard_map/ppermute | solution.py:55
  37.6 1.5 %level_forward.1 = (bf16[64,1024]{1,0:T(8,128)(2,1)S(1)}, bf16[1,64,1024]{2,1,0:T(8,128)(2,1)S(1)}) custom-call(bf16[2,64,1024]{2,1,0:T(8,128)(2,1)S(1)} %added.1.sums, bf16[272,1024]{1,0:T(8,128)(2,1)S(1)} %get-tuple-element.33.refs_0_.refs_1_, bf16[272,1024]{1,0:T(8,128)(2,1)S(1)} %collective-permute-done.4.refs_1_.refs_2_, ...), custom_call_target="tpu_custom_call" | custom-call | flops 1 | bytes 1 | tf_op jit(solution)/shard_map/level_forward/pallas_call | solution.py:131
  39.2 1.6 %collective-permute-start.16 = (bf16[128,1024]{1,0:T(8,128)(2,1)S(1)}, bf16[128,1024]{1,0:T(8,128)(2,1)S(1)}, u32[]{:S(2)}, u32[]{:S(2)}) collective-permute-start(bf16[128,1024]{1,0:T(8,128)(2,1)S(1)} %collective-permute-done.10.refs_10_), channel_id=1, source_target_pairs={{0,2},{1,5},{2,0},{3,7},{4,6},{5,1},{6,4},{7,3},{8,12},{9,11},{10,... | collective-permute-start | bytes 786440 | tf_op jit(solution)/shard_map/ppermute | solution.py:50
  40.7 2.6 %collective-permute-start.15 = (bf16[1,64,1024]{2,1,0:T(8,128)(2,1)S(1)}, bf16[1,64,1024]{2,1,0:T(8,128)(2,1)S(1)}, u32[]{:S(2)}, u32[]{:S(2)}) collective-permute-start(bf16[1,64,1024]{2,1,0:T(8,128)(2,1)S(1)} %get-tuple-element.42), channel_id=1, source_target_pairs={{0,16},{8,24},{16,0},{24,8},{1,17},{9,25},{17,1},{25,9},{2,18},{10... | collective-permute-start | bytes 393224 | tf_op jit(solution)/shard_map/ppermute | solution.py:55
  43.8 1.8 %collective-permute-done.16.refs_12_ = bf16[128,1024]{1,0:T(8,128)(2,1)S(1)} collective-permute-done((bf16[128,1024]{1,0:T(8,128)(2,1)S(1)}, bf16[128,1024]{1,0:T(8,128)(2,1)S(1)}, u32[]{:S(2)}, u32[]{:S(2)}) %collective-permute-start.16) | collective-permute-done | bytes 262176 | tf_op jit(solution)/shard_map/ppermute | solution.py:50
  45.6 3.5 %collective-permute-done.15 = bf16[1,64,1024]{2,1,0:T(8,128)(2,1)S(1)} collective-permute-done((bf16[1,64,1024]{2,1,0:T(8,128)(2,1)S(1)}, bf16[1,64,1024]{2,1,0:T(8,128)(2,1)S(1)}, u32[]{:S(2)}, u32[]{:S(2)}) %collective-permute-start.15) | collective-permute-done | bytes 131104 | tf_op jit(solution)/shard_map/ppermute | solution.py:55
  49.2 2.2 %backward.1.refs_0_ = bf16[2,64,1024]{2,1,0:T(8,128)(2,1)S(1)} custom-call(bf16[1,64,1024]{2,1,0:T(8,128)(2,1)S(1)} %add_convert_fusion.1.sums, bf16[64,1024]{1,0:T(8,128)(2,1)S(1)} %get-tuple-element.43.refs_0_, bf16[272,1024]{1,0:T(8,128)(2,1)S(1)} %get-tuple-element.33.refs_0_.refs_1_, bf16[272,1024]{1,0:T(8,128)(2,1)S(1)} %collective-permute-done.4.refs_1_.refs_2_, ...), custom_call_target="tpu_custom_call" | custom-call | flops 1 | bytes 1 | tf_op jit(solution)/shard_map/backward/pallas_call | solution.py:131
  51.4 1.8 %collective-permute-start.24 = (bf16[2,64,1024]{2,1,0:T(8,128)(2,1)S(1)}, bf16[2,64,1024]{2,1,0:T(8,128)(2,1)S(1)}, u32[]{:S(2)}, u32[]{:S(2)}) collective-permute-start(bf16[2,64,1024]{2,1,0:T(8,128)(2,1)S(1)} %backward.1.refs_0_), channel_id=1, source_target_pairs={{0,2},{1,5},{2,0},{3,7},{4,6},{5,1},{6,4},{7,3},{8,12},{9,11},{10,... | collective-permute-start | bytes 786440 | tf_op jit(solution)/shard_map/ppermute | solution.py:50
  54.5 5.1 %collective-permute-done.24.refs_4_ = bf16[2,64,1024]{2,1,0:T(8,128)(2,1)S(1)} collective-permute-done((bf16[2,64,1024]{2,1,0:T(8,128)(2,1)S(1)}, bf16[2,64,1024]{2,1,0:T(8,128)(2,1)S(1)}, u32[]{:S(2)}, u32[]{:S(2)}) %collective-permute-start.24) | collective-permute-done | bytes 262176 | tf_op jit(solution)/shard_map/ppermute | solution.py:50
  60.2 1.7 %collective-permute-start.22 = (bf16[2,64,1024]{2,1,0:T(8,128)(2,1)S(1)}, bf16[2,64,1024]{2,1,0:T(8,128)(2,1)S(1)}, u32[]{:S(2)}, u32[]{:S(2)}) collective-permute-start(bf16[2,64,1024]{2,1,0:T(8,128)(2,1)S(1)} %collective-permute-done.21.refs_2_), channel_id=1, source_target_pairs={{0,2},{1,5},{2,0},{3,7},{4,6},{5,1},{6,4},{7,3},{8,12},{9,11},{10,... | collective-permute-start | bytes 786440 | tf_op jit(solution)/shard_map/ppermute | solution.py:50
  61.9 4.2 %leaf_backward.2 = (bf16[8,128,512]{2,1,0:T(8,128)(2,1)}, bf16[1,2,128,512]{3,2,1,0:T(8,128)(2,1)}) custom-call(s32[2,8]{1,0:T(2,128)S(1)} %bitcast.3, bf16[512,1024]{1,0:T(8,128)(2,1)S(1)} %get-tuple-element.28.refs_0_.y, bf16[8,128,128]{2,1,0:T(8,128)(2,1)S(1)} %copy-done.1, bf16[8,2,1024,128]{3,2,1,0:T(8,128)(2,1)S(1)} %copy-done, ...), custom_call_target="tpu_custom_call" | custom-call | flops 1 | bytes 1 | tf_op jit(solution)/shard_map/leaf_backward/pallas_call | solution.py:131
  66.5 1.5 %collective-permute-done.27.refs_1_ = bf16[2,64,1024]{2,1,0:T(8,128)(2,1)S(1)} collective-permute-done((bf16[2,64,1024]{2,1,0:T(8,128)(2,1)S(1)}, bf16[2,64,1024]{2,1,0:T(8,128)(2,1)S(1)}, u32[]{:S(2)}, u32[]{:S(2)}) %collective-permute-start.27) | collective-permute-done | bytes 262176 | tf_op jit(solution)/shard_map/ppermute | solution.py:39
  68.1 2.4 %leaf_backward.3 = (bf16[8,128,512]{2,1,0:T(8,128)(2,1)}, bf16[1,2,128,512]{3,2,1,0:T(8,128)(2,1)}) custom-call(s32[2,8]{1,0:T(2,128)S(1)} %bitcast.4, bf16[512,1024]{1,0:T(8,128)(2,1)S(1)} %get-tuple-element.28.refs_0_.y, bf16[8,128,128]{2,1,0:T(8,128)(2,1)S(1)} %copy-done.1, ...), custom_call_target="tpu_custom_call", output_to_operand_aliasing={{0}: (7, {}), {1}: (8, {})} | custom-call | flops 1 | bytes 1 | tf_op jit(solution)/shard_map/leaf_backward/pallas_call | solution.py:131
  (57 shorter events, 11.2 us)
Async XLA Ops:
  2.1 11.0 %collective-permute-start.4 = (bf16[272,1024]{1,0:T(8,128)(2,1)S(1)}, bf16[272,1024]{1,0:T(8,128)(2,1)S(1)}, u32[]{:S(2)}, u32[]{:S(2)}) collective-permute-start(bf16[272,1024]{1,0:T(8,128)(2,1)S(1)} %get-tuple-element.33.refs_0_.refs_1_), channel_id=1, source_target_pairs={{0,4},{1,3},{2,6},{3,1},{4,0},{5,7},{6,2},{7,5},{8,10},{9,13},{10,... | collective-permute-start | bytes 1671176 | tf_op jit(solution)/shard_map/ppermute | solution.py:50
  9.5 9.2 %collective-permute-start.2 = (bf16[2,2,64,1024]{3,2,1,0:T(8,128)(2,1)S(1)}, bf16[2,2,64,1024]{3,2,1,0:T(8,128)(2,1)S(1)}, u32[]{:S(2)}, u32[]{:S(2)}) collective-permute-start(bf16[2,2,64,1024]{3,2,1,0:T(8,128)(2,1)S(1)} %joined.1), channel_id=1, source_target_pairs={{0,2},{1,5},{2,0},{3,7},{4,6},{5,1},{6,4},{7,3},{8,12},{9,11},{10,... | collective-permute-start | bytes 1572872 | tf_op jit(solution)/shard_map/ppermute | solution.py:50
  12.9 7.9 %collective-permute-start.6 = (bf16[2,2,64,1024]{3,2,1,0:T(8,128)(2,1)S(1)}, bf16[2,2,64,1024]{3,2,1,0:T(8,128)(2,1)S(1)}, u32[]{:S(2)}, u32[]{:S(2)}) collective-permute-start(bf16[2,2,64,1024]{3,2,1,0:T(8,128)(2,1)S(1)} %get-tuple-element.36), channel_id=1, source_target_pairs={{0,1},{1,0},{2,3},{3,2},{4,5},{5,4},{6,7},{7,6},{8,9},{9,8},{10,11... | collective-permute-start | bytes 1572872 | tf_op jit(solution)/shard_map/ppermute | solution.py:39
  13.2 14.8 %collective-permute-start.8 = (bf16[272,1024]{1,0:T(8,128)(2,1)S(1)}, bf16[272,1024]{1,0:T(8,128)(2,1)S(1)}, u32[]{:S(2)}, u32[]{:S(2)}) collective-permute-start(bf16[272,1024]{1,0:T(8,128)(2,1)S(1)} %collective-permute-done.4.refs_1_.refs_2_), channel_id=1, source_target_pairs={{0,8},{8,0},{16,24},{24,16},{1,9},{9,1},{17,25},{25,17},{2,10},{10... | collective-permute-start | bytes 1671176 | tf_op jit(solution)/shard_map/ppermute | solution.py:55
  18.8 10.6 %collective-permute-start.5 = (bf16[272,1024]{1,0:T(8,128)(2,1)S(1)}, bf16[272,1024]{1,0:T(8,128)(2,1)S(1)}, u32[]{:S(2)}, u32[]{:S(2)}) collective-permute-start(bf16[272,1024]{1,0:T(8,128)(2,1)S(1)} %collective-permute-done.4.refs_1_.refs_2_), channel_id=1, source_target_pairs={{0,1},{1,0},{2,3},{3,2},{4,5},{5,4},{6,7},{7,6},{8,9},{9,8},{10,11... | collective-permute-start | bytes 1671176 | tf_op jit(solution)/shard_map/ppermute | solution.py:39
  18.8 10.6 %collective-permute-start.3 = (bf16[272,1024]{1,0:T(8,128)(2,1)S(1)}, bf16[272,1024]{1,0:T(8,128)(2,1)S(1)}, u32[]{:S(2)}, u32[]{:S(2)}) collective-permute-start(bf16[272,1024]{1,0:T(8,128)(2,1)S(1)} %get-tuple-element.33.refs_0_.refs_1_), channel_id=1, source_target_pairs={{0,1},{1,0},{2,3},{3,2},{4,5},{5,4},{6,7},{7,6},{8,9},{9,8},{10,11... | collective-permute-start | bytes 1671176 | tf_op jit(solution)/shard_map/ppermute | solution.py:39
  19.3 14.3 %collective-permute-start.11 = (bf16[272,1024]{1,0:T(8,128)(2,1)S(1)}, bf16[272,1024]{1,0:T(8,128)(2,1)S(1)}, u32[]{:S(2)}, u32[]{:S(2)}) collective-permute-start(bf16[272,1024]{1,0:T(8,128)(2,1)S(1)} %collective-permute-done.4.refs_1_.refs_2_), channel_id=1, source_target_pairs={{0,2},{1,5},{2,0},{3,7},{4,6},{5,1},{6,4},{7,3},{8,12},{9,11},{10,... | collective-permute-start | bytes 1671176 | tf_op jit(solution)/shard_map/ppermute | solution.py:50
  20.9 9.3 %collective-permute-start.7 = (bf16[1,2,64,1024]{3,2,1,0:T(8,128)(2,1)S(1)}, bf16[1,2,64,1024]{3,2,1,0:T(8,128)(2,1)S(1)}, u32[]{:S(2)}, u32[]{:S(2)}) collective-permute-start(bf16[1,2,64,1024]{3,2,1,0:T(8,128)(2,1)S(1)} %add_convert_fusion), channel_id=1, source_target_pairs={{0,4},{1,3},{2,6},{3,1},{4,0},{5,7},{6,2},{7,5},{8,10},{9,13},{10,... | collective-permute-start | bytes 786440 | tf_op jit(solution)/shard_map/ppermute | solution.py:50
  28.0 7.7 %collective-permute-start.10 = (bf16[128,1024]{1,0:T(8,128)(2,1)S(1)}, bf16[128,1024]{1,0:T(8,128)(2,1)S(1)}, u32[]{:S(2)}, u32[]{:S(2)}) collective-permute-start(bf16[128,1024]{1,0:T(8,128)(2,1)S(1)} %get-tuple-element.45.refs_9_), channel_id=1, source_target_pairs={{0,4},{1,3},{2,6},{3,1},{4,0},{5,7},{6,2},{7,5},{8,10},{9,13},{10,... | collective-permute-start | bytes 786440 | tf_op jit(solution)/shard_map/ppermute | solution.py:50
  30.3 7.2 %collective-permute-start.9 = (bf16[2,64,1024]{2,1,0:T(8,128)(2,1)S(1)}, bf16[2,64,1024]{2,1,0:T(8,128)(2,1)S(1)}, u32[]{:S(2)}, u32[]{:S(2)}) collective-permute-start(bf16[2,64,1024]{2,1,0:T(8,128)(2,1)S(1)} %first.1.ours), channel_id=1, source_target_pairs={{0,8},{8,0},{16,24},{24,16},{1,9},{9,1},{17,25},{25,17},{2,10},{10... | collective-permute-start | bytes 786440 | tf_op jit(solution)/shard_map/ppermute | solution.py:55
  32.0 5.6 %collective-permute-start.12 = (bf16[272,1024]{1,0:T(8,128)(2,1)S(1)}, bf16[272,1024]{1,0:T(8,128)(2,1)S(1)}, u32[]{:S(2)}, u32[]{:S(2)}) collective-permute-start(bf16[272,1024]{1,0:T(8,128)(2,1)S(1)} %collective-permute-done.8.value.refs_2_.refs_3_), channel_id=1, source_target_pairs={{0,1},{1,0},{2,3},{3,2},{4,5},{5,4},{6,7},{7,6},{8,9},{9,8},{10,11... | collective-permute-start | bytes 1671176 | tf_op jit(solution)/shard_map/ppermute | solution.py:39
  33.6 4.0 %collective-permute-start.13 = (bf16[272,1024]{1,0:T(8,128)(2,1)S(1)}, bf16[272,1024]{1,0:T(8,128)(2,1)S(1)}, u32[]{:S(2)}, u32[]{:S(2)}) collective-permute-start(bf16[272,1024]{1,0:T(8,128)(2,1)S(1)} %collective-permute-done.11.refs_3_.refs_4_), channel_id=1, source_target_pairs={{0,1},{1,0},{2,3},{3,2},{4,5},{5,4},{6,7},{7,6},{8,9},{9,8},{10,11... | collective-permute-start | bytes 1671176 | tf_op jit(solution)/shard_map/ppermute | solution.py:39
  33.6 7.1 %collective-permute-start.14 = (bf16[128,1024]{1,0:T(8,128)(2,1)S(1)}, bf16[128,1024]{1,0:T(8,128)(2,1)S(1)}, u32[]{:S(2)}, u32[]{:S(2)}) collective-permute-start(bf16[128,1024]{1,0:T(8,128)(2,1)S(1)} %get-tuple-element.45.refs_9_), channel_id=1, source_target_pairs={{0,2},{1,5},{2,0},{3,7},{4,6},{5,1},{6,4},{7,3},{8,12},{9,11},{10,... | collective-permute-start | bytes 786440 | tf_op jit(solution)/shard_map/ppermute | solution.py:50
  39.2 6.4 %collective-permute-start.16 = (bf16[128,1024]{1,0:T(8,128)(2,1)S(1)}, bf16[128,1024]{1,0:T(8,128)(2,1)S(1)}, u32[]{:S(2)}, u32[]{:S(2)}) collective-permute-start(bf16[128,1024]{1,0:T(8,128)(2,1)S(1)} %collective-permute-done.10.refs_10_), channel_id=1, source_target_pairs={{0,2},{1,5},{2,0},{3,7},{4,6},{5,1},{6,4},{7,3},{8,12},{9,11},{10,... | collective-permute-start | bytes 786440 | tf_op jit(solution)/shard_map/ppermute | solution.py:50
  40.7 8.4 %collective-permute-start.15 = (bf16[1,64,1024]{2,1,0:T(8,128)(2,1)S(1)}, bf16[1,64,1024]{2,1,0:T(8,128)(2,1)S(1)}, u32[]{:S(2)}, u32[]{:S(2)}) collective-permute-start(bf16[1,64,1024]{2,1,0:T(8,128)(2,1)S(1)} %get-tuple-element.42), channel_id=1, source_target_pairs={{0,16},{8,24},{16,0},{24,8},{1,17},{9,25},{17,1},{25,9},{2,18},{10... | collective-permute-start | bytes 393224 | tf_op jit(solution)/shard_map/ppermute | solution.py:55
  43.3 5.9 %collective-permute-start.19 = (bf16[128,1024]{1,0:T(8,128)(2,1)S(1)}, bf16[128,1024]{1,0:T(8,128)(2,1)S(1)}, u32[]{:S(2)}, u32[]{:S(2)}) collective-permute-start(bf16[128,1024]{1,0:T(8,128)(2,1)S(1)} %collective-permute-done.14.refs_11_), channel_id=1, source_target_pairs={{0,1},{1,0},{2,3},{3,2},{4,5},{5,4},{6,7},{7,6},{8,9},{9,8},{10,11... | collective-permute-start | bytes 786440 | tf_op jit(solution)/shard_map/ppermute | solution.py:39
  43.3 5.9 %collective-permute-start.17 = (bf16[128,1024]{1,0:T(8,128)(2,1)S(1)}, bf16[128,1024]{1,0:T(8,128)(2,1)S(1)}, u32[]{:S(2)}, u32[]{:S(2)}) collective-permute-start(bf16[128,1024]{1,0:T(8,128)(2,1)S(1)} %get-tuple-element.45.refs_9_), channel_id=1, source_target_pairs={{0,1},{1,0},{2,3},{3,2},{4,5},{5,4},{6,7},{7,6},{8,9},{9,8},{10,11... | collective-permute-start | bytes 786440 | tf_op jit(solution)/shard_map/ppermute | solution.py:39
  43.8 5.4 %collective-permute-start.18 = (bf16[128,1024]{1,0:T(8,128)(2,1)S(1)}, bf16[128,1024]{1,0:T(8,128)(2,1)S(1)}, u32[]{:S(2)}, u32[]{:S(2)}) collective-permute-start(bf16[128,1024]{1,0:T(8,128)(2,1)S(1)} %collective-permute-done.10.refs_10_), channel_id=1, source_target_pairs={{0,1},{1,0},{2,3},{3,2},{4,5},{5,4},{6,7},{7,6},{8,9},{9,8},{10,11... | collective-permute-start | bytes 786440 | tf_op jit(solution)/shard_map/ppermute | solution.py:39
  45.6 3.6 %collective-permute-start.20 = (bf16[128,1024]{1,0:T(8,128)(2,1)S(1)}, bf16[128,1024]{1,0:T(8,128)(2,1)S(1)}, u32[]{:S(2)}, u32[]{:S(2)}) collective-permute-start(bf16[128,1024]{1,0:T(8,128)(2,1)S(1)} %collective-permute-done.16.refs_12_), channel_id=1, source_target_pairs={{0,1},{1,0},{2,3},{3,2},{4,5},{5,4},{6,7},{7,6},{8,9},{9,8},{10,11... | collective-permute-start | bytes 786440 | tf_op jit(solution)/shard_map/ppermute | solution.py:39
  51.4 8.2 %collective-permute-start.24 = (bf16[2,64,1024]{2,1,0:T(8,128)(2,1)S(1)}, bf16[2,64,1024]{2,1,0:T(8,128)(2,1)S(1)}, u32[]{:S(2)}, u32[]{:S(2)}) collective-permute-start(bf16[2,64,1024]{2,1,0:T(8,128)(2,1)S(1)} %backward.1.refs_0_), channel_id=1, source_target_pairs={{0,2},{1,5},{2,0},{3,7},{4,6},{5,1},{6,4},{7,3},{8,12},{9,11},{10,... | collective-permute-start | bytes 786440 | tf_op jit(solution)/shard_map/ppermute | solution.py:50
  53.2 6.5 %collective-permute-start.21 = (bf16[2,64,1024]{2,1,0:T(8,128)(2,1)S(1)}, bf16[2,64,1024]{2,1,0:T(8,128)(2,1)S(1)}, u32[]{:S(2)}, u32[]{:S(2)}) collective-permute-start(bf16[2,64,1024]{2,1,0:T(8,128)(2,1)S(1)} %backward.1.refs_0_), channel_id=1, source_target_pairs={{0,4},{1,3},{2,6},{3,1},{4,0},{5,7},{6,2},{7,5},{8,10},{9,13},{10,... | collective-permute-start | bytes 786440 | tf_op jit(solution)/shard_map/ppermute | solution.py:50
  54.5 7.4 %collective-permute-start.23 = (bf16[2,64,1024]{2,1,0:T(8,128)(2,1)S(1)}, bf16[2,64,1024]{2,1,0:T(8,128)(2,1)S(1)}, u32[]{:S(2)}, u32[]{:S(2)}) collective-permute-start(bf16[2,64,1024]{2,1,0:T(8,128)(2,1)S(1)} %backward.1.refs_0_), channel_id=1, source_target_pairs={{0,1},{1,0},{2,3},{3,2},{4,5},{5,4},{6,7},{7,6},{8,9},{9,8},{10,11... | collective-permute-start | bytes 786440 | tf_op jit(solution)/shard_map/ppermute | solution.py:39
  59.6 2.3 %collective-permute-start.25 = (bf16[2,64,1024]{2,1,0:T(8,128)(2,1)S(1)}, bf16[2,64,1024]{2,1,0:T(8,128)(2,1)S(1)}, u32[]{:S(2)}, u32[]{:S(2)}) collective-permute-start(bf16[2,64,1024]{2,1,0:T(8,128)(2,1)S(1)} %collective-permute-done.24.refs_4_), channel_id=1, source_target_pairs={{0,1},{1,0},{2,3},{3,2},{4,5},{5,4},{6,7},{7,6},{8,9},{9,8},{10,11... | collective-permute-start | bytes 786440 | tf_op jit(solution)/shard_map/ppermute | solution.py:39
  60.2 6.4 %collective-permute-start.22 = (bf16[2,64,1024]{2,1,0:T(8,128)(2,1)S(1)}, bf16[2,64,1024]{2,1,0:T(8,128)(2,1)S(1)}, u32[]{:S(2)}, u32[]{:S(2)}) collective-permute-start(bf16[2,64,1024]{2,1,0:T(8,128)(2,1)S(1)} %collective-permute-done.21.refs_2_), channel_id=1, source_target_pairs={{0,2},{1,5},{2,0},{3,7},{4,6},{5,1},{6,4},{7,3},{8,12},{9,11},{10,... | collective-permute-start | bytes 786440 | tf_op jit(solution)/shard_map/ppermute | solution.py:50
  (10 other events, 52.7 us)

commit v6 on v5

--- a/solution.py
+++ b/solution.py
@@ -257,15 +257,15 @@
     return vmem_call(kernel, arrays, [*y_shape, part, *sent], scratch, "leaf_forward")
 
 
-def joined_call(kept, others):
+def joined_call(kept, others, seen):
     def kernel(kept, *refs):
-        for level, other in enumerate(refs[:-1]):
+        for level, other in enumerate(refs[: len(others)]):
             refs[-1][:, level] = (kept[:, level].astype(F32) + other[...].astype(F32)).astype(BF16)
 
-    return vmem_call(kernel, [kept, *others], [jax.ShapeDtypeStruct(kept.shape, BF16)], [], "joined")[0]
-
-
-def first_call(parts, seen):
+    return vmem_call(kernel, [kept, *others, *seen], [jax.ShapeDtypeStruct(kept.shape, BF16)], [], "joined")[0]
+
+
+def first_call(parts, seen, flops):
     def kernel(*refs):
         total = refs[0][0].astype(F32)
         for ref in refs[1 : len(parts)]:
@@ -273,7 +273,8 @@
         refs[-1][...] = total.astype(BF16)
 
     shapes = [jax.ShapeDtypeStruct(parts[0].shape[1:], BF16)]
-    return vmem_call(kernel, [*parts, *seen], shapes, [], "first")[0]
+    arrays = [*parts, *seen]
+    return kernel_call(kernel, arrays, [pltpu.VMEM] * len(arrays), shapes, [], "first", flops)[0]
 
 
 def seen_call(value, flops):
@@ -506,7 +507,8 @@
     leaf_y, keep, *send = leaf_forward_call(
         mask, [leaf_rhs, leaf_inverse], leaf_couple, sep_rhs, highs, layers, True
     )
-    high = [joined_call(keep, [swap_core(part) for part in send])]
+    own_crossed = [swap_core(own[0])] if four else []
+    high = [joined_call(keep, [swap_core(part) for part in send], own_crossed)]
     keep, send = leaf_forward_call(mask, [leaf_y], leaf_couple, sep_rhs, lows, layers, False)
     low = [keep, swap_core(send)]
     parts, arrived = scatter_sum(low, high)
@@ -521,18 +523,17 @@
         return repacked(pieces, jnp.argsort(slots).astype(jnp.int32), 1 + levels - level, own_rows)
 
     if four:
-        own_crossed = swap_core(after(own[0], arrived[0]))
         near_crossed = swap_core(after(near, arrived[0]))
         side = swap_layer(near, 0)
         far = swap_link(after(near, arrived[0]), 0)
         last_own = after(own[-1], arrived[0])
         last_near = swap_link(last_own, 1)
-        parts[0] = after(parts[0], own_crossed, near_crossed)
+        parts[0] = after(parts[0], near_crossed)
         seen = [seen_call(side, 3_000_000_000)]
         last = [own[-1], last_near, swap_link(after(last_own, arrived[1]), 0)]
     else:
         first = gather(own[0])
-    sums = first_call(parts, seen)
+    sums = first_call(parts, seen, 1)
     groups, solved = [], []
     for level in range(1, levels + 1):
         theirs = swap_layer(sums, level - 1)
@@ -541,7 +542,7 @@
         sums = added_call(sums, theirs, 4_000_000_000) if level == 1 else added(sums, theirs)
         if level == 1:
             if four:
-                first = [own[0], near, side, far, own_crossed, near_crossed, swap_core(side), swap_core(far)]
+                first = [own[0], near, side, far, own_crossed[0], near_crossed, swap_core(side), swap_core(far)]
             groups.append(fitted(first, 1))
         elif four and level == levels:
             groups.append(fitted(last + [swap_core(piece) for piece in last[2:4]], level))
@@ -551,9 +552,7 @@
             y, sums = level_forward_call(planes, sums, groups[level - 1])
             solved.append(y)
         if level == 1 and four:
-            last_near = after(last_near, y)
             last = last + [swap_link(last_near, 0), *[swap_core(piece) for piece in after_all([last[0], last_near], y)]]
-            sums = after(sums, last[2])
     answers = backward_call(planes, sums, solved, groups)
     leaves = [mask, leaf_y, leaf_inverse, leaf_couple, leaf_diag]
     if not four or 2 * answers.shape[1] != LANES:

time: 70.6 us -> 68.2 us (0.966)
  starting transfers between devices: 26.2 us -> 23.8 us
    ppermute x10, starting transfers between devices: 17.4 us -> 14.7 us  [swap_link(): return lax.ppermute(value, ('layer', 'plane'), pairs)]
    ppermute x10, waiting for transfers between devices: 13.2 us -> 14 us  [swap_link(): return lax.ppermute(value, ('layer', 'plane'), pairs)]
  transfers between devices with their start and end apart: 28 -> 28, of which waited for: 13 -> 13; matrix products, arithmetic and copies ran while one was open for 0% -> 0% of each run, Pallas kernels for 14% -> 15%
where the time goes in v6:
time: 68.2 us; the launch traced here: 68.1 us
  waiting for transfers between devices  27.2 us (40%)
  starting transfers between devices  23.8 us (35%)
  Pallas kernels  16.1 us (24%)
  between operations  0.85 us (1%)
    pallas_call x11, Pallas kernels, kernel_call(): pl.pallas_call(kernel, in_specs=[pl.BlockSpec(memory_space=space) for spa...  16.1 us
    ppermute x10, starting transfers between devices, swap_link(): return lax.ppermute(value, ('layer', 'plane'), pairs)  14.7 us
    ppermute x10, waiting for transfers between devices, swap_link(): return lax.ppermute(value, ('layer', 'plane'), pairs)  14 us
    ppermute x3, waiting for transfers between devices, swap_layer(): lax.ppermute(value, 'layer', [(i, i ^ 1 << stride) for i in range(layers)])  10.3 us
    ppermute x3, starting transfers between devices, swap_layer(): lax.ppermute(value, 'layer', [(i, i ^ 1 << stride) for i in range(layers)])  6.81 us
    ppermute x15, waiting for transfers between devices, swap_core(): return lax.ppermute(value, 'plane', [(i, i ^ 1) for i in range(planes)])  2.96 us
    ppermute x15, starting transfers between devices, swap_core(): return lax.ppermute(value, 'plane', [(i, i ^ 1) for i in range(planes)])  2.2 us
  transfers between devices with their start and end apart: 28, of which 13 were waited for; matrix products, arithmetic and copies ran while one was open for 0% of the time, Pallas kernels for 15%

profile of v6, /device:TPU:0, one launch (start us, length us, event | category | flops | bytes accessed | tf_op | source)
XLA Modules:
  0.0 68.1 jit_solution(11577026722096167296)
XLA Ops:
  2.7 2.6 %collective-permute-start = (bf16[272,1024]{1,0:T(8,128)(2,1)S(1)}, bf16[272,1024]{1,0:T(8,128)(2,1)S(1)}, u32[]{:S(2)}, u32[]{:S(2)}) collective-permute-start(bf16[272,1024]{1,0:T(8,128)(2,1)S(1)} %get-tuple-element.23.refs_0_.refs_1_), channel_id=1, source_target_pairs={{0,4},{1,3},{2,6},{3,1},{4,0},{5,7},{6,2},{7,5},{8,10},{9,13},{10,... | collective-permute-start | bytes 1671176 | tf_op jit(solution)/shard_map/ppermute | solution.py:50
  5.3 2.2 %leaf_forward.2 = (bf16[512,1024]{1,0:T(8,128)(2,1)S(1)}, bf16[2,2,64,1024]{3,2,1,0:T(8,128)(2,1)S(1)}, bf16[2,64,1024]{2,1,0:T(8,128)(2,1)S(1)}, bf16[2,64,1024]{2,1,0:T(8,128)(2,1)S(1)}) custom-call(s32[2,8]{1,0:T(2,128)S(1)} %bitcast.1, bf16[8,128,512]{2,1,0:T(8,128)(2,1)S(1)} %copy-done.3, bf16[8,128,128]{2,1,0:T(8,128)(2,1)S(1)} %copy-done.1, ...), custom_call_target="tpu_custom_call" | custom-call | flops 1 | bytes 1 | tf_op jit(solution)/shard_map/leaf_forward/pallas_call | solution.py:131
  9.6 1.6 %collective-permute-start.4 = (bf16[2,2,64,1024]{3,2,1,0:T(8,128)(2,1)S(1)}, bf16[2,2,64,1024]{3,2,1,0:T(8,128)(2,1)S(1)}, u32[]{:S(2)}, u32[]{:S(2)}) collective-permute-start(bf16[2,2,64,1024]{3,2,1,0:T(8,128)(2,1)S(1)} %joined.1), channel_id=1, source_target_pairs={{0,2},{1,5},{2,0},{3,7},{4,6},{5,1},{6,4},{7,3},{8,12},{9,11},{10,... | collective-permute-start | bytes 1572872 | tf_op jit(solution)/shard_map/ppermute | solution.py:50
  11.1 1.8 %leaf_forward.3 = (bf16[2,2,64,1024]{3,2,1,0:T(8,128)(2,1)S(1)}, bf16[2,2,64,1024]{3,2,1,0:T(8,128)(2,1)S(1)}) custom-call(s32[2,8]{1,0:T(2,128)S(1)} %bitcast.2, bf16[512,1024]{1,0:T(8,128)(2,1)S(1)} %get-tuple-element.25.refs_0_.y, bf16[8,2,1024,128]{3,2,1,0:T(8,128)(2,1)S(1)} %copy-done, bf16[3,128,512]{2,1,0:T(8,128)(2,1)S(1)} %copy-done.2), custom_call_target="tpu_custom_call" | custom-call | flops 1 | bytes 1 | tf_op jit(solution)/shard_map/leaf_forward/pallas_call | solution.py:131
  13.1 2.5 %collective-permute-start.8 = (bf16[272,1024]{1,0:T(8,128)(2,1)S(1)}, bf16[272,1024]{1,0:T(8,128)(2,1)S(1)}, u32[]{:S(2)}, u32[]{:S(2)}) collective-permute-start(bf16[272,1024]{1,0:T(8,128)(2,1)S(1)} %collective-permute-done.refs_1_.refs_2_), channel_id=1, source_target_pairs={{0,8},{8,0},{16,24},{24,16},{1,9},{9,1},{17,25},{25,17},{2,10},{10... | collective-permute-start | bytes 1671176 | tf_op jit(solution)/shard_map/ppermute | solution.py:55
  15.6 3.2 %collective-permute-done.4.refs_2_ = bf16[2,2,64,1024]{3,2,1,0:T(8,128)(2,1)S(1)} collective-permute-done((bf16[2,2,64,1024]{3,2,1,0:T(8,128)(2,1)S(1)}, bf16[2,2,64,1024]{3,2,1,0:T(8,128)(2,1)S(1)}, u32[]{:S(2)}, u32[]{:S(2)}) %collective-permute-start.4) | collective-permute-done | bytes 524320 | tf_op jit(solution)/shard_map/ppermute | solution.py:50
  18.8 1.6 %collective-permute-start.11 = (bf16[272,1024]{1,0:T(8,128)(2,1)S(1)}, bf16[272,1024]{1,0:T(8,128)(2,1)S(1)}, u32[]{:S(2)}, u32[]{:S(2)}) collective-permute-start(bf16[272,1024]{1,0:T(8,128)(2,1)S(1)} %collective-permute-done.refs_1_.refs_2_), channel_id=1, source_target_pairs={{0,2},{1,5},{2,0},{3,7},{4,6},{5,1},{6,4},{7,3},{8,12},{9,11},{10,... | collective-permute-start | bytes 1671176 | tf_op jit(solution)/shard_map/ppermute | solution.py:50
  20.6 1.6 %collective-permute-start.7 = (bf16[1,2,64,1024]{3,2,1,0:T(8,128)(2,1)S(1)}, bf16[1,2,64,1024]{3,2,1,0:T(8,128)(2,1)S(1)}, u32[]{:S(2)}, u32[]{:S(2)}) collective-permute-start(bf16[1,2,64,1024]{3,2,1,0:T(8,128)(2,1)S(1)} %add_convert_fusion), channel_id=1, source_target_pairs={{0,4},{1,3},{2,6},{3,1},{4,0},{5,7},{6,2},{7,5},{8,10},{9,13},{10,... | collective-permute-start | bytes 786440 | tf_op jit(solution)/shard_map/ppermute | solution.py:50
  22.7 5.4 %collective-permute-done.8.value.refs_2_.refs_3_ = bf16[272,1024]{1,0:T(8,128)(2,1)S(1)} collective-permute-done((bf16[272,1024]{1,0:T(8,128)(2,1)S(1)}, bf16[272,1024]{1,0:T(8,128)(2,1)S(1)}, u32[]{:S(2)}, u32[]{:S(2)}) %collective-permute-start.8) | collective-permute-done | bytes 557088 | tf_op jit(solution)/shard_map/ppermute | solution.py:55
  28.1 1.8 %collective-permute-done.7.refs_3_ = bf16[1,2,64,1024]{3,2,1,0:T(8,128)(2,1)S(1)} collective-permute-done((bf16[1,2,64,1024]{3,2,1,0:T(8,128)(2,1)S(1)}, bf16[1,2,64,1024]{3,2,1,0:T(8,128)(2,1)S(1)}, u32[]{:S(2)}, u32[]{:S(2)}) %collective-permute-start.7) | collective-permute-done | bytes 262176 | tf_op jit(solution)/shard_map/ppermute | solution.py:50
  30.1 1.7 %collective-permute-start.9 = (bf16[2,64,1024]{2,1,0:T(8,128)(2,1)S(1)}, bf16[2,64,1024]{2,1,0:T(8,128)(2,1)S(1)}, u32[]{:S(2)}, u32[]{:S(2)}) collective-permute-start(bf16[2,64,1024]{2,1,0:T(8,128)(2,1)S(1)} %first.1.ours), channel_id=1, source_target_pairs={{0,8},{8,0},{16,24},{24,16},{1,9},{9,1},{17,25},{25,17},{2,10},{10... | collective-permute-start | bytes 786440 | tf_op jit(solution)/shard_map/ppermute | solution.py:55
  31.7 1.9 %collective-permute-done.11.refs_3_.refs_4_ = bf16[272,1024]{1,0:T(8,128)(2,1)S(1)} collective-permute-done((bf16[272,1024]{1,0:T(8,128)(2,1)S(1)}, bf16[272,1024]{1,0:T(8,128)(2,1)S(1)}, u32[]{:S(2)}, u32[]{:S(2)}) %collective-permute-start.11) | collective-permute-done | bytes 557088 | tf_op jit(solution)/shard_map/ppermute | solution.py:50
  33.6 1.8 %collective-permute-start.15 = (bf16[128,1024]{1,0:T(8,128)(2,1)S(1)}, bf16[128,1024]{1,0:T(8,128)(2,1)S(1)}, u32[]{:S(2)}, u32[]{:S(2)}) collective-permute-start(bf16[128,1024]{1,0:T(8,128)(2,1)S(1)} %get-tuple-element.39.refs_9_), channel_id=1, source_target_pairs={{0,2},{1,5},{2,0},{3,7},{4,6},{5,1},{6,4},{7,3},{8,12},{9,11},{10,... | collective-permute-start | bytes 786440 | tf_op jit(solution)/shard_map/ppermute | solution.py:50
  35.7 1.6 %collective-permute-done.9.theirs = bf16[2,64,1024]{2,1,0:T(8,128)(2,1)S(1)} collective-permute-done((bf16[2,64,1024]{2,1,0:T(8,128)(2,1)S(1)}, bf16[2,64,1024]{2,1,0:T(8,128)(2,1)S(1)}, u32[]{:S(2)}, u32[]{:S(2)}) %collective-permute-start.9) | collective-permute-done | bytes 262176 | tf_op jit(solution)/shard_map/ppermute | solution.py:55
  38.9 2.6 %collective-permute-start.14 = (bf16[1,64,1024]{2,1,0:T(8,128)(2,1)S(1)}, bf16[1,64,1024]{2,1,0:T(8,128)(2,1)S(1)}, u32[]{:S(2)}, u32[]{:S(2)}) collective-permute-start(bf16[1,64,1024]{2,1,0:T(8,128)(2,1)S(1)} %get-tuple-element.36), channel_id=1, source_target_pairs={{0,16},{8,24},{16,0},{24,8},{1,17},{9,25},{17,1},{25,9},{2,18},{10... | collective-permute-start | bytes 393224 | tf_op jit(solution)/shard_map/ppermute | solution.py:55
  43.3 3.4 %collective-permute-done.14 = bf16[1,64,1024]{2,1,0:T(8,128)(2,1)S(1)} collective-permute-done((bf16[1,64,1024]{2,1,0:T(8,128)(2,1)S(1)}, bf16[1,64,1024]{2,1,0:T(8,128)(2,1)S(1)}, u32[]{:S(2)}, u32[]{:S(2)}) %collective-permute-start.14) | collective-permute-done | bytes 131104 | tf_op jit(solution)/shard_map/ppermute | solution.py:55
  46.8 2.2 %backward.1.refs_0_ = bf16[2,64,1024]{2,1,0:T(8,128)(2,1)S(1)} custom-call(bf16[1,64,1024]{2,1,0:T(8,128)(2,1)S(1)} %add_convert_fusion.1.sums, bf16[64,1024]{1,0:T(8,128)(2,1)S(1)} %get-tuple-element.37.refs_0_, bf16[272,1024]{1,0:T(8,128)(2,1)S(1)} %get-tuple-element.23.refs_0_.refs_1_, bf16[272,1024]{1,0:T(8,128)(2,1)S(1)} %collective-permute-done.refs_1_.refs_2_, ...), custom_call_target="tpu_custom_call" | custom-call | flops 1 | bytes 1 | tf_op jit(solution)/shard_map/backward/pallas_call | solution.py:131
  49.0 1.6 %collective-permute-start.24 = (bf16[2,64,1024]{2,1,0:T(8,128)(2,1)S(1)}, bf16[2,64,1024]{2,1,0:T(8,128)(2,1)S(1)}, u32[]{:S(2)}, u32[]{:S(2)}) collective-permute-start(bf16[2,64,1024]{2,1,0:T(8,128)(2,1)S(1)} %backward.1.refs_0_), channel_id=1, source_target_pairs={{0,2},{1,5},{2,0},{3,7},{4,6},{5,1},{6,4},{7,3},{8,12},{9,11},{10,... | collective-permute-start | bytes 786440 | tf_op jit(solution)/shard_map/ppermute | solution.py:50
  50.6 1.5 %collective-permute-start.21 = (bf16[2,64,1024]{2,1,0:T(8,128)(2,1)S(1)}, bf16[2,64,1024]{2,1,0:T(8,128)(2,1)S(1)}, u32[]{:S(2)}, u32[]{:S(2)}) collective-permute-start(bf16[2,64,1024]{2,1,0:T(8,128)(2,1)S(1)} %backward.1.refs_0_), channel_id=1, source_target_pairs={{0,4},{1,3},{2,6},{3,1},{4,0},{5,7},{6,2},{7,5},{8,10},{9,13},{10,... | collective-permute-start | bytes 786440 | tf_op jit(solution)/shard_map/ppermute | solution.py:50
  52.1 5.2 %collective-permute-done.24.refs_4_ = bf16[2,64,1024]{2,1,0:T(8,128)(2,1)S(1)} collective-permute-done((bf16[2,64,1024]{2,1,0:T(8,128)(2,1)S(1)}, bf16[2,64,1024]{2,1,0:T(8,128)(2,1)S(1)}, u32[]{:S(2)}, u32[]{:S(2)}) %collective-permute-start.24) | collective-permute-done | bytes 262176 | tf_op jit(solution)/shard_map/ppermute | solution.py:50
  57.8 1.7 %collective-permute-start.22 = (bf16[2,64,1024]{2,1,0:T(8,128)(2,1)S(1)}, bf16[2,64,1024]{2,1,0:T(8,128)(2,1)S(1)}, u32[]{:S(2)}, u32[]{:S(2)}) collective-permute-start(bf16[2,64,1024]{2,1,0:T(8,128)(2,1)S(1)} %collective-permute-done.21.refs_2_), channel_id=1, source_target_pairs={{0,2},{1,5},{2,0},{3,7},{4,6},{5,1},{6,4},{7,3},{8,12},{9,11},{10,... | collective-permute-start | bytes 786440 | tf_op jit(solution)/shard_map/ppermute | solution.py:50
  59.5 4.2 %leaf_backward.2 = (bf16[8,128,512]{2,1,0:T(8,128)(2,1)}, bf16[1,2,128,512]{3,2,1,0:T(8,128)(2,1)}) custom-call(s32[2,8]{1,0:T(2,128)S(1)} %bitcast.3, bf16[512,1024]{1,0:T(8,128)(2,1)S(1)} %get-tuple-element.25.refs_0_.y, bf16[8,128,128]{2,1,0:T(8,128)(2,1)S(1)} %copy-done.1, bf16[8,2,1024,128]{3,2,1,0:T(8,128)(2,1)S(1)} %copy-done, ...), custom_call_target="tpu_custom_call" | custom-call | flops 1 | bytes 1 | tf_op jit(solution)/shard_map/leaf_backward/pallas_call | solution.py:131
  64.1 1.5 %collective-permute-done.27.refs_1_ = bf16[2,64,1024]{2,1,0:T(8,128)(2,1)S(1)} collective-permute-done((bf16[2,64,1024]{2,1,0:T(8,128)(2,1)S(1)}, bf16[2,64,1024]{2,1,0:T(8,128)(2,1)S(1)}, u32[]{:S(2)}, u32[]{:S(2)}) %collective-permute-start.27) | collective-permute-done | bytes 262176 | tf_op jit(solution)/shard_map/ppermute | solution.py:39
  65.7 2.4 %leaf_backward.3 = (bf16[8,128,512]{2,1,0:T(8,128)(2,1)}, bf16[1,2,128,512]{3,2,1,0:T(8,128)(2,1)}) custom-call(s32[2,8]{1,0:T(2,128)S(1)} %bitcast.4, bf16[512,1024]{1,0:T(8,128)(2,1)S(1)} %get-tuple-element.25.refs_0_.y, bf16[8,128,128]{2,1,0:T(8,128)(2,1)S(1)} %copy-done.1, ...), custom_call_target="tpu_custom_call", output_to_operand_aliasing={{0}: (7, {}), {1}: (8, {})} | custom-call | flops 1 | bytes 1 | tf_op jit(solution)/shard_map/leaf_backward/pallas_call | solution.py:131
  (57 shorter events, 9.7 us)
Async XLA Ops:
  2.1 7.3 %collective-permute-start.3 = (bf16[272,1024]{1,0:T(8,128)(2,1)S(1)}, bf16[272,1024]{1,0:T(8,128)(2,1)S(1)}, u32[]{:S(2)}, u32[]{:S(2)}) collective-permute-start(bf16[272,1024]{1,0:T(8,128)(2,1)S(1)} %get-tuple-element.23.refs_0_.refs_1_), channel_id=1, source_target_pairs={{0,1},{1,0},{2,3},{3,2},{4,5},{5,4},{6,7},{7,6},{8,9},{9,8},{10,11... | collective-permute-start | bytes 1671176 | tf_op jit(solution)/shard_map/ppermute | solution.py:39
  2.7 10.5 %collective-permute-start = (bf16[272,1024]{1,0:T(8,128)(2,1)S(1)}, bf16[272,1024]{1,0:T(8,128)(2,1)S(1)}, u32[]{:S(2)}, u32[]{:S(2)}) collective-permute-start(bf16[272,1024]{1,0:T(8,128)(2,1)S(1)} %get-tuple-element.23.refs_0_.refs_1_), channel_id=1, source_target_pairs={{0,4},{1,3},{2,6},{3,1},{4,0},{5,7},{6,2},{7,5},{8,10},{9,13},{10,... | collective-permute-start | bytes 1671176 | tf_op jit(solution)/shard_map/ppermute | solution.py:50
  9.6 9.2 %collective-permute-start.4 = (bf16[2,2,64,1024]{3,2,1,0:T(8,128)(2,1)S(1)}, bf16[2,2,64,1024]{3,2,1,0:T(8,128)(2,1)S(1)}, u32[]{:S(2)}, u32[]{:S(2)}) collective-permute-start(bf16[2,2,64,1024]{3,2,1,0:T(8,128)(2,1)S(1)} %joined.1), channel_id=1, source_target_pairs={{0,2},{1,5},{2,0},{3,7},{4,6},{5,1},{6,4},{7,3},{8,12},{9,11},{10,... | collective-permute-start | bytes 1572872 | tf_op jit(solution)/shard_map/ppermute | solution.py:50
  12.9 7.5 %collective-permute-start.6 = (bf16[2,2,64,1024]{3,2,1,0:T(8,128)(2,1)S(1)}, bf16[2,2,64,1024]{3,2,1,0:T(8,128)(2,1)S(1)}, u32[]{:S(2)}, u32[]{:S(2)}) collective-permute-start(bf16[2,2,64,1024]{3,2,1,0:T(8,128)(2,1)S(1)} %get-tuple-element.32), channel_id=1, source_target_pairs={{0,1},{1,0},{2,3},{3,2},{4,5},{5,4},{6,7},{7,6},{8,9},{9,8},{10,11... | collective-permute-start | bytes 1572872 | tf_op jit(solution)/shard_map/ppermute | solution.py:39
  13.1 15.0 %collective-permute-start.8 = (bf16[272,1024]{1,0:T(8,128)(2,1)S(1)}, bf16[272,1024]{1,0:T(8,128)(2,1)S(1)}, u32[]{:S(2)}, u32[]{:S(2)}) collective-permute-start(bf16[272,1024]{1,0:T(8,128)(2,1)S(1)} %collective-permute-done.refs_1_.refs_2_), channel_id=1, source_target_pairs={{0,8},{8,0},{16,24},{24,16},{1,9},{9,1},{17,25},{25,17},{2,10},{10... | collective-permute-start | bytes 1671176 | tf_op jit(solution)/shard_map/ppermute | solution.py:55
  18.8 9.3 %collective-permute-start.5 = (bf16[272,1024]{1,0:T(8,128)(2,1)S(1)}, bf16[272,1024]{1,0:T(8,128)(2,1)S(1)}, u32[]{:S(2)}, u32[]{:S(2)}) collective-permute-start(bf16[272,1024]{1,0:T(8,128)(2,1)S(1)} %collective-permute-done.refs_1_.refs_2_), channel_id=1, source_target_pairs={{0,1},{1,0},{2,3},{3,2},{4,5},{5,4},{6,7},{7,6},{8,9},{9,8},{10,11... | collective-permute-start | bytes 1671176 | tf_op jit(solution)/shard_map/ppermute | solution.py:39
  18.8 14.8 %collective-permute-start.11 = (bf16[272,1024]{1,0:T(8,128)(2,1)S(1)}, bf16[272,1024]{1,0:T(8,128)(2,1)S(1)}, u32[]{:S(2)}, u32[]{:S(2)}) collective-permute-start(bf16[272,1024]{1,0:T(8,128)(2,1)S(1)} %collective-permute-done.refs_1_.refs_2_), channel_id=1, source_target_pairs={{0,2},{1,5},{2,0},{3,7},{4,6},{5,1},{6,4},{7,3},{8,12},{9,11},{10,... | collective-permute-start | bytes 1671176 | tf_op jit(solution)/shard_map/ppermute | solution.py:50
  20.6 9.3 %collective-permute-start.7 = (bf16[1,2,64,1024]{3,2,1,0:T(8,128)(2,1)S(1)}, bf16[1,2,64,1024]{3,2,1,0:T(8,128)(2,1)S(1)}, u32[]{:S(2)}, u32[]{:S(2)}) collective-permute-start(bf16[1,2,64,1024]{3,2,1,0:T(8,128)(2,1)S(1)} %add_convert_fusion), channel_id=1, source_target_pairs={{0,4},{1,3},{2,6},{3,1},{4,0},{5,7},{6,2},{7,5},{8,10},{9,13},{10,... | collective-permute-start | bytes 786440 | tf_op jit(solution)/shard_map/ppermute | solution.py:50
  22.2 13.3 %collective-permute-start.10 = (bf16[128,1024]{1,0:T(8,128)(2,1)S(1)}, bf16[128,1024]{1,0:T(8,128)(2,1)S(1)}, u32[]{:S(2)}, u32[]{:S(2)}) collective-permute-start(bf16[128,1024]{1,0:T(8,128)(2,1)S(1)} %get-tuple-element.39.refs_9_), channel_id=1, source_target_pairs={{0,4},{1,3},{2,6},{3,1},{4,0},{5,7},{6,2},{7,5},{8,10},{9,13},{10,... | collective-permute-start | bytes 786440 | tf_op jit(solution)/shard_map/ppermute | solution.py:50
  30.1 7.2 %collective-permute-start.9 = (bf16[2,64,1024]{2,1,0:T(8,128)(2,1)S(1)}, bf16[2,64,1024]{2,1,0:T(8,128)(2,1)S(1)}, u32[]{:S(2)}, u32[]{:S(2)}) collective-permute-start(bf16[2,64,1024]{2,1,0:T(8,128)(2,1)S(1)} %first.1.ours), channel_id=1, source_target_pairs={{0,8},{8,0},{16,24},{24,16},{1,9},{9,1},{17,25},{25,17},{2,10},{10... | collective-permute-start | bytes 786440 | tf_op jit(solution)/shard_map/ppermute | solution.py:55
  31.7 5.6 %collective-permute-start.12 = (bf16[272,1024]{1,0:T(8,128)(2,1)S(1)}, bf16[272,1024]{1,0:T(8,128)(2,1)S(1)}, u32[]{:S(2)}, u32[]{:S(2)}) collective-permute-start(bf16[272,1024]{1,0:T(8,128)(2,1)S(1)} %collective-permute-done.8.value.refs_2_.refs_3_), channel_id=1, source_target_pairs={{0,1},{1,0},{2,3},{3,2},{4,5},{5,4},{6,7},{7,6},{8,9},{9,8},{10,11... | collective-permute-start | bytes 1671176 | tf_op jit(solution)/shard_map/ppermute | solution.py:39
  33.6 3.7 %collective-permute-start.13 = (bf16[272,1024]{1,0:T(8,128)(2,1)S(1)}, bf16[272,1024]{1,0:T(8,128)(2,1)S(1)}, u32[]{:S(2)}, u32[]{:S(2)}) collective-permute-start(bf16[272,1024]{1,0:T(8,128)(2,1)S(1)} %collective-permute-done.11.refs_3_.refs_4_), channel_id=1, source_target_pairs={{0,1},{1,0},{2,3},{3,2},{4,5},{5,4},{6,7},{7,6},{8,9},{9,8},{10,11... | collective-permute-start | bytes 1671176 | tf_op jit(solution)/shard_map/ppermute | solution.py:39
  33.6 7.9 %collective-permute-start.15 = (bf16[128,1024]{1,0:T(8,128)(2,1)S(1)}, bf16[128,1024]{1,0:T(8,128)(2,1)S(1)}, u32[]{:S(2)}, u32[]{:S(2)}) collective-permute-start(bf16[128,1024]{1,0:T(8,128)(2,1)S(1)} %get-tuple-element.39.refs_9_), channel_id=1, source_target_pairs={{0,2},{1,5},{2,0},{3,7},{4,6},{5,1},{6,4},{7,3},{8,12},{9,11},{10,... | collective-permute-start | bytes 786440 | tf_op jit(solution)/shard_map/ppermute | solution.py:50
  35.5 7.4 %collective-permute-start.16 = (bf16[128,1024]{1,0:T(8,128)(2,1)S(1)}, bf16[128,1024]{1,0:T(8,128)(2,1)S(1)}, u32[]{:S(2)}, u32[]{:S(2)}) collective-permute-start(bf16[128,1024]{1,0:T(8,128)(2,1)S(1)} %collective-permute-done.10.refs_10_), channel_id=1, source_target_pairs={{0,2},{1,5},{2,0},{3,7},{4,6},{5,1},{6,4},{7,3},{8,12},{9,11},{10,... | collective-permute-start | bytes 786440 | tf_op jit(solution)/shard_map/ppermute | solution.py:50
  38.9 7.8 %collective-permute-start.14 = (bf16[1,64,1024]{2,1,0:T(8,128)(2,1)S(1)}, bf16[1,64,1024]{2,1,0:T(8,128)(2,1)S(1)}, u32[]{:S(2)}, u32[]{:S(2)}) collective-permute-start(bf16[1,64,1024]{2,1,0:T(8,128)(2,1)S(1)} %get-tuple-element.36), channel_id=1, source_target_pairs={{0,16},{8,24},{16,0},{24,8},{1,17},{9,25},{17,1},{25,9},{2,18},{10... | collective-permute-start | bytes 393224 | tf_op jit(solution)/shard_map/ppermute | solution.py:55
  41.5 5.3 %collective-permute-start.19 = (bf16[128,1024]{1,0:T(8,128)(2,1)S(1)}, bf16[128,1024]{1,0:T(8,128)(2,1)S(1)}, u32[]{:S(2)}, u32[]{:S(2)}) collective-permute-start(bf16[128,1024]{1,0:T(8,128)(2,1)S(1)} %collective-permute-done.15.refs_11_), channel_id=1, source_target_pairs={{0,1},{1,0},{2,3},{3,2},{4,5},{5,4},{6,7},{7,6},{8,9},{9,8},{10,11... | collective-permute-start | bytes 786440 | tf_op jit(solution)/shard_map/ppermute | solution.py:39
  42.8 3.9 %collective-permute-start.20 = (bf16[128,1024]{1,0:T(8,128)(2,1)S(1)}, bf16[128,1024]{1,0:T(8,128)(2,1)S(1)}, u32[]{:S(2)}, u32[]{:S(2)}) collective-permute-start(bf16[128,1024]{1,0:T(8,128)(2,1)S(1)} %collective-permute-done.16.refs_12_), channel_id=1, source_target_pairs={{0,1},{1,0},{2,3},{3,2},{4,5},{5,4},{6,7},{7,6},{8,9},{9,8},{10,11... | collective-permute-start | bytes 786440 | tf_op jit(solution)/shard_map/ppermute | solution.py:39
  42.8 3.9 %collective-permute-start.17 = (bf16[128,1024]{1,0:T(8,128)(2,1)S(1)}, bf16[128,1024]{1,0:T(8,128)(2,1)S(1)}, u32[]{:S(2)}, u32[]{:S(2)}) collective-permute-start(bf16[128,1024]{1,0:T(8,128)(2,1)S(1)} %get-tuple-element.39.refs_9_), channel_id=1, source_target_pairs={{0,1},{1,0},{2,3},{3,2},{4,5},{5,4},{6,7},{7,6},{8,9},{9,8},{10,11... | collective-permute-start | bytes 786440 | tf_op jit(solution)/shard_map/ppermute | solution.py:39
  43.3 3.5 %collective-permute-start.18 = (bf16[128,1024]{1,0:T(8,128)(2,1)S(1)}, bf16[128,1024]{1,0:T(8,128)(2,1)S(1)}, u32[]{:S(2)}, u32[]{:S(2)}) collective-permute-start(bf16[128,1024]{1,0:T(8,128)(2,1)S(1)} %collective-permute-done.10.refs_10_), channel_id=1, source_target_pairs={{0,1},{1,0},{2,3},{3,2},{4,5},{5,4},{6,7},{7,6},{8,9},{9,8},{10,11... | collective-permute-start | bytes 786440 | tf_op jit(solution)/shard_map/ppermute | solution.py:39
  49.0 8.3 %collective-permute-start.24 = (bf16[2,64,1024]{2,1,0:T(8,128)(2,1)S(1)}, bf16[2,64,1024]{2,1,0:T(8,128)(2,1)S(1)}, u32[]{:S(2)}, u32[]{:S(2)}) collective-permute-start(bf16[2,64,1024]{2,1,0:T(8,128)(2,1)S(1)} %backward.1.refs_0_), channel_id=1, source_target_pairs={{0,2},{1,5},{2,0},{3,7},{4,6},{5,1},{6,4},{7,3},{8,12},{9,11},{10,... | collective-permute-start | bytes 786440 | tf_op jit(solution)/shard_map/ppermute | solution.py:50
  50.6 6.7 %collective-permute-start.21 = (bf16[2,64,1024]{2,1,0:T(8,128)(2,1)S(1)}, bf16[2,64,1024]{2,1,0:T(8,128)(2,1)S(1)}, u32[]{:S(2)}, u32[]{:S(2)}) collective-permute-start(bf16[2,64,1024]{2,1,0:T(8,128)(2,1)S(1)} %backward.1.refs_0_), channel_id=1, source_target_pairs={{0,4},{1,3},{2,6},{3,1},{4,0},{5,7},{6,2},{7,5},{8,10},{9,13},{10,... | collective-permute-start | bytes 786440 | tf_op jit(solution)/shard_map/ppermute | solution.py:50
  52.1 7.4 %collective-permute-start.23 = (bf16[2,64,1024]{2,1,0:T(8,128)(2,1)S(1)}, bf16[2,64,1024]{2,1,0:T(8,128)(2,1)S(1)}, u32[]{:S(2)}, u32[]{:S(2)}) collective-permute-start(bf16[2,64,1024]{2,1,0:T(8,128)(2,1)S(1)} %backward.1.refs_0_), channel_id=1, source_target_pairs={{0,1},{1,0},{2,3},{3,2},{4,5},{5,4},{6,7},{7,6},{8,9},{9,8},{10,11... | collective-permute-start | bytes 786440 | tf_op jit(solution)/shard_map/ppermute | solution.py:39
  57.3 2.2 %collective-permute-start.25 = (bf16[2,64,1024]{2,1,0:T(8,128)(2,1)S(1)}, bf16[2,64,1024]{2,1,0:T(8,128)(2,1)S(1)}, u32[]{:S(2)}, u32[]{:S(2)}) collective-permute-start(bf16[2,64,1024]{2,1,0:T(8,128)(2,1)S(1)} %collective-permute-done.24.refs_4_), channel_id=1, source_target_pairs={{0,1},{1,0},{2,3},{3,2},{4,5},{5,4},{6,7},{7,6},{8,9},{9,8},{10,11... | collective-permute-start | bytes 786440 | tf_op jit(solution)/shard_map/ppermute | solution.py:39
  57.8 6.4 %collective-permute-start.22 = (bf16[2,64,1024]{2,1,0:T(8,128)(2,1)S(1)}, bf16[2,64,1024]{2,1,0:T(8,128)(2,1)S(1)}, u32[]{:S(2)}, u32[]{:S(2)}) collective-permute-start(bf16[2,64,1024]{2,1,0:T(8,128)(2,1)S(1)} %collective-permute-done.21.refs_2_), channel_id=1, source_target_pairs={{0,2},{1,5},{2,0},{3,7},{4,6},{5,1},{6,4},{7,3},{8,12},{9,11},{10,... | collective-permute-start | bytes 786440 | tf_op jit(solution)/shard_map/ppermute | solution.py:50
  (10 other events, 50.9 us)

commit v7 on v6

--- a/solution.py
+++ b/solution.py
@@ -169,9 +169,8 @@
             high = value.astype(BF16).astype(F32)
             rows += [high, value - high]
         rows.append(jnp.zeros((DIAG_ROWS - len(rows), own_rows), F32))
-        below = levels * own_rows
-        outs[0][below:] = jnp.zeros((DIAG_ROWS, sep_rows), BF16)
-        outs[0][below:, :own_rows] = jnp.concatenate(rows, axis=0).astype(BF16)
+        outs[-1][own_rows:] = jnp.zeros((DIAG_ROWS, sep_rows), BF16)
+        outs[-1][own_rows:, :own_rows] = jnp.concatenate(rows, axis=0).astype(BF16)
         for level in range(1, levels + 1):
             loads[level - 1].wait()
             lower = lower_unit(held[level - 1].astype(F32), me * own_rows)
@@ -180,7 +179,7 @@
             move.wait()
 
     shapes = [((1 + levels - level) * own_rows, sep_rows) for level in range(1, levels + 1)]
-    shapes[0] = (levels * own_rows + DIAG_ROWS, sep_rows)
+    shapes[-1] = (own_rows + DIAG_ROWS, sep_rows)
     return kernel_call(
         kernel,
         [sep_inverse, sep_couple, sep_diag],
@@ -287,13 +286,13 @@
     return kernel_call(kernel, [value], [pltpu.VMEM], shapes, [], "seen", flops)[0]
 
 
-def added_call(ours, theirs, flops):
-    def kernel(ours, theirs, out):
-        out[...] = (ours[...].astype(F32) + theirs[...].astype(F32)).astype(BF16)
-
-    spaces = [pltpu.VMEM] * 2
+def added_call(ours, theirs, seen, flops):
+    def kernel(ours, theirs, *refs):
+        refs[-1][...] = (ours[...].astype(F32) + theirs[...].astype(F32)).astype(BF16)
+
+    arrays = [ours, theirs, *seen]
     shapes = [jax.ShapeDtypeStruct(ours.shape, BF16)]
-    return kernel_call(kernel, [ours, theirs], spaces, shapes, [], "added", flops)[0]
+    return kernel_call(kernel, arrays, [pltpu.VMEM] * len(arrays), shapes, [], "added", flops)[0]
 
 
 def paired(count):
@@ -361,7 +360,7 @@
         solved, refs = refs[:lower], refs[lower:]
         pieces, (out, diag, work) = [refs[i * count : (i + 1) * count] for i in range(levels)], refs[-3:]
         for i in range(count):
-            split = pieces[0][i][levels * LANES : levels * LANES + DIAG_ROWS, :LANES].astype(F32)
+            split = pieces[-1][i][LANES : LANES + DIAG_ROWS, :LANES].astype(F32)
             for level in range(levels):
                 value = split[2 * level : 2 * level + 1] + split[2 * level + 1 : 2 * level + 2]
                 diag[level : level + 1, at_multiple(order[i], LANES)] = value
@@ -525,7 +524,7 @@
     if four:
         near_crossed = swap_core(after(near, arrived[0]))
         side = swap_layer(near, 0)
-        far = swap_link(after(near, arrived[0]), 0)
+        far = swap_link(near, 0)
         last_own = after(own[-1], arrived[0])
         last_near = swap_link(last_own, 1)
         parts[0] = after(parts[0], near_crossed)
@@ -533,13 +532,14 @@
         last = [own[-1], last_near, swap_link(after(last_own, arrived[1]), 0)]
     else:
         first = gather(own[0])
+    far_seen = [seen_call(far, 6_000_000_000)] if four else []
     sums = first_call(parts, seen, 1)
     groups, solved = [], []
     for level in range(1, levels + 1):
         theirs = swap_layer(sums, level - 1)
         if four and level == 1:
             theirs = after(theirs, last_near)
-        sums = added_call(sums, theirs, 4_000_000_000) if level == 1 else added(sums, theirs)
+        sums = added_call(sums, theirs, far_seen, 4_000_000_000) if level == 1 else added(sums, theirs)
         if level == 1:
             if four:
                 first = [own[0], near, side, far, own_crossed[0], near_crossed, swap_core(side), swap_core(far)]

time: 68.2 us -> 67.8 us (level)
    ppermute x10, waiting for transfers between devices: 14 us -> 8.31 us  [swap_link(): return lax.ppermute(value, ('layer', 'plane'), pairs)]
    ppermute x3, waiting for transfers between devices: 10.3 us -> 15.6 us  [swap_layer(): lax.ppermute(value, 'layer', [(i, i ^ 1 << stride) for i in range(layers)])]
    ppermute x15, starting transfers between devices: 2.2 us -> 3.21 us  [swap_core(): return lax.ppermute(value, 'plane', [(i, i ^ 1) for i in range(planes)])]
    pallas_call x11 -> x12, Pallas kernels: 16.1 us -> 16 us  [kernel_call(): pl.pallas_call(kernel, in_specs=[pl.BlockSpec(memory_space=space) for spa...]
  transfers between devices with their start and end apart: 28 -> 28, of which waited for: 13 -> 9; matrix products, arithmetic and copies ran while one was open for 0% -> 0% of each run, Pallas kernels for 15% -> 15%
where the time goes in v7:
time: 67.8 us; the launch traced here: 67.6 us
  waiting for transfers between devices  26.9 us (40%)
  starting transfers between devices  23.7 us (35%)
  Pallas kernels  16 us (24%)
  between operations  0.87 us (1%)
    pallas_call x12, Pallas kernels, kernel_call(): pl.pallas_call(kernel, in_specs=[pl.BlockSpec(memory_space=space) for spa...  16 us
    ppermute x3, waiting for transfers between devices, swap_layer(): lax.ppermute(value, 'layer', [(i, i ^ 1 << stride) for i in range(layers)])  15.6 us
    ppermute x10, starting transfers between devices, swap_link(): return lax.ppermute(value, ('layer', 'plane'), pairs)  14.3 us
    ppermute x10, waiting for transfers between devices, swap_link(): return lax.ppermute(value, ('layer', 'plane'), pairs)  8.31 us
    ppermute x3, starting transfers between devices, swap_layer(): lax.ppermute(value, 'layer', [(i, i ^ 1 << stride) for i in range(layers)])  6.19 us
    ppermute x15, starting transfers between devices, swap_core(): return lax.ppermute(value, 'plane', [(i, i ^ 1) for i in range(planes)])  3.21 us
    ppermute x15, waiting for transfers between devices, swap_core(): return lax.ppermute(value, 'plane', [(i, i ^ 1) for i in range(planes)])  2.96 us
  transfers between devices with their start and end apart: 28, of which 9 were waited for; matrix products, arithmetic and copies ran while one was open for 0% of the time, Pallas kernels for 15%

profile of v7, /device:TPU:0, one launch (start us, length us, event | category | flops | bytes accessed | tf_op | source)
XLA Modules:
  0.0 67.6 jit_solution(12460238727077019842)
XLA Ops:
  0.7 1.5 %collect.1 = (bf16[256,1024]{1,0:T(8,128)(2,1)S(1)}, bf16[144,1024]{1,0:T(8,128)(2,1)S(1)}) custom-call(bf16[3,128,1024]{2,1,0:T(8,128)(2,1)} %inverse.3, bf16[3,1,128,1024]{3,2,1,0:T(8,128)(2,1)} %couple.3, f32[3,128]{1,0:T(4,128)} %diag_in.1), custom_call_target="tpu_custom_call" | custom-call | flops 20000000000 | bytes 1 | tf_op jit(solution)/shard_map/collect/pallas_call | solution.py:131
  2.7 2.6 %collective-permute-start = (bf16[256,1024]{1,0:T(8,128)(2,1)S(1)}, bf16[256,1024]{1,0:T(8,128)(2,1)S(1)}, u32[]{:S(2)}, u32[]{:S(2)}) collective-permute-start(bf16[256,1024]{1,0:T(8,128)(2,1)S(1)} %get-tuple-element.23.refs_0_.refs_1_), channel_id=1, source_target_pairs={{0,4},{1,3},{2,6},{3,1},{4,0},{5,7},{6,2},{7,5},{8,10},{9,13},{10,... | collective-permute-start | bytes 1572872 | tf_op jit(solution)/shard_map/ppermute | solution.py:50
  5.3 2.2 %leaf_forward.2 = (bf16[512,1024]{1,0:T(8,128)(2,1)S(1)}, bf16[2,2,64,1024]{3,2,1,0:T(8,128)(2,1)S(1)}, bf16[2,64,1024]{2,1,0:T(8,128)(2,1)S(1)}, bf16[2,64,1024]{2,1,0:T(8,128)(2,1)S(1)}) custom-call(s32[2,8]{1,0:T(2,128)S(1)} %bitcast.1, bf16[8,128,512]{2,1,0:T(8,128)(2,1)S(1)} %copy-done.3, bf16[8,128,128]{2,1,0:T(8,128)(2,1)S(1)} %copy-done.1, ...), custom_call_target="tpu_custom_call" | custom-call | flops 1 | bytes 1 | tf_op jit(solution)/shard_map/leaf_forward/pallas_call | solution.py:131
  9.6 1.6 %collective-permute-start.4 = (bf16[2,2,64,1024]{3,2,1,0:T(8,128)(2,1)S(1)}, bf16[2,2,64,1024]{3,2,1,0:T(8,128)(2,1)S(1)}, u32[]{:S(2)}, u32[]{:S(2)}) collective-permute-start(bf16[2,2,64,1024]{3,2,1,0:T(8,128)(2,1)S(1)} %joined.1), channel_id=1, source_target_pairs={{0,2},{1,5},{2,0},{3,7},{4,6},{5,1},{6,4},{7,3},{8,12},{9,11},{10,... | collective-permute-start | bytes 1572872 | tf_op jit(solution)/shard_map/ppermute | solution.py:50
  11.1 1.8 %leaf_forward.3 = (bf16[2,2,64,1024]{3,2,1,0:T(8,128)(2,1)S(1)}, bf16[2,2,64,1024]{3,2,1,0:T(8,128)(2,1)S(1)}) custom-call(s32[2,8]{1,0:T(2,128)S(1)} %bitcast.2, bf16[512,1024]{1,0:T(8,128)(2,1)S(1)} %get-tuple-element.25.refs_0_.y, bf16[8,2,1024,128]{3,2,1,0:T(8,128)(2,1)S(1)} %copy-done, bf16[3,128,512]{2,1,0:T(8,128)(2,1)S(1)} %copy-done.2), custom_call_target="tpu_custom_call" | custom-call | flops 1 | bytes 1 | tf_op jit(solution)/shard_map/leaf_forward/pallas_call | solution.py:131
  13.0 1.9 %collective-permute-start.8 = (bf16[256,1024]{1,0:T(8,128)(2,1)S(1)}, bf16[256,1024]{1,0:T(8,128)(2,1)S(1)}, u32[]{:S(2)}, u32[]{:S(2)}) collective-permute-start(bf16[256,1024]{1,0:T(8,128)(2,1)S(1)} %collective-permute-done.refs_1_.refs_2_), channel_id=1, source_target_pairs={{0,8},{8,0},{16,24},{24,16},{1,9},{9,1},{17,25},{25,17},{2,10},{10... | collective-permute-start | bytes 1572872 | tf_op jit(solution)/shard_map/ppermute | solution.py:55
  14.9 1.5 %collective-permute-start.11 = (bf16[256,1024]{1,0:T(8,128)(2,1)S(1)}, bf16[256,1024]{1,0:T(8,128)(2,1)S(1)}, u32[]{:S(2)}, u32[]{:S(2)}) collective-permute-start(bf16[256,1024]{1,0:T(8,128)(2,1)S(1)} %collective-permute-done.refs_1_.refs_2_), channel_id=1, source_target_pairs={{0,2},{1,5},{2,0},{3,7},{4,6},{5,1},{6,4},{7,3},{8,12},{9,11},{10,... | collective-permute-start | bytes 1572872 | tf_op jit(solution)/shard_map/ppermute | solution.py:50
  16.4 2.4 %collective-permute-done.4.refs_2_ = bf16[2,2,64,1024]{3,2,1,0:T(8,128)(2,1)S(1)} collective-permute-done((bf16[2,2,64,1024]{3,2,1,0:T(8,128)(2,1)S(1)}, bf16[2,2,64,1024]{3,2,1,0:T(8,128)(2,1)S(1)}, u32[]{:S(2)}, u32[]{:S(2)}) %collective-permute-start.4) | collective-permute-done | bytes 524320 | tf_op jit(solution)/shard_map/ppermute | solution.py:50
  19.0 1.4 %collective-permute-start.7 = (bf16[1,2,64,1024]{3,2,1,0:T(8,128)(2,1)S(1)}, bf16[1,2,64,1024]{3,2,1,0:T(8,128)(2,1)S(1)}, u32[]{:S(2)}, u32[]{:S(2)}) collective-permute-start(bf16[1,2,64,1024]{3,2,1,0:T(8,128)(2,1)S(1)} %add_convert_fusion), channel_id=1, source_target_pairs={{0,4},{1,3},{2,6},{3,1},{4,0},{5,7},{6,2},{7,5},{8,10},{9,13},{10,... | collective-permute-start | bytes 786440 | tf_op jit(solution)/shard_map/ppermute | solution.py:50
  21.1 6.3 %collective-permute-done.8.value.refs_2_.refs_3_ = bf16[256,1024]{1,0:T(8,128)(2,1)S(1)} collective-permute-done((bf16[256,1024]{1,0:T(8,128)(2,1)S(1)}, bf16[256,1024]{1,0:T(8,128)(2,1)S(1)}, u32[]{:S(2)}, u32[]{:S(2)}) %collective-permute-start.8) | collective-permute-done | bytes 524320 | tf_op jit(solution)/shard_map/ppermute | solution.py:55
  28.0 1.6 %collective-permute-start.9 = (bf16[2,64,1024]{2,1,0:T(8,128)(2,1)S(1)}, bf16[2,64,1024]{2,1,0:T(8,128)(2,1)S(1)}, u32[]{:S(2)}, u32[]{:S(2)}) collective-permute-start(bf16[2,64,1024]{2,1,0:T(8,128)(2,1)S(1)} %first.1.ours), channel_id=1, source_target_pairs={{0,8},{8,0},{16,24},{24,16},{1,9},{9,1},{17,25},{25,17},{2,10},{10... | collective-permute-start | bytes 786440 | tf_op jit(solution)/shard_map/ppermute | solution.py:55
  29.7 1.3 %collective-permute-start.15 = (bf16[144,1024]{1,0:T(8,128)(2,1)S(1)}, bf16[144,1024]{1,0:T(8,128)(2,1)S(1)}, u32[]{:S(2)}, u32[]{:S(2)}) collective-permute-start(bf16[144,1024]{1,0:T(8,128)(2,1)S(1)} %get-tuple-element.39.refs_9_), channel_id=1, source_target_pairs={{0,2},{1,5},{2,0},{3,7},{4,6},{5,1},{6,4},{7,3},{8,12},{9,11},{10,... | collective-permute-start | bytes 884744 | tf_op jit(solution)/shard_map/ppermute | solution.py:50
  31.7 4.6 %collective-permute-done.9.theirs = bf16[2,64,1024]{2,1,0:T(8,128)(2,1)S(1)} collective-permute-done((bf16[2,64,1024]{2,1,0:T(8,128)(2,1)S(1)}, bf16[2,64,1024]{2,1,0:T(8,128)(2,1)S(1)}, u32[]{:S(2)}, u32[]{:S(2)}) %collective-permute-start.9) | collective-permute-done | bytes 262176 | tf_op jit(solution)/shard_map/ppermute | solution.py:55
  36.4 1.5 %level_forward.1 = (bf16[64,1024]{1,0:T(8,128)(2,1)S(1)}, bf16[1,64,1024]{2,1,0:T(8,128)(2,1)S(1)}) custom-call(bf16[2,64,1024]{2,1,0:T(8,128)(2,1)S(1)} %added.1.sums, bf16[256,1024]{1,0:T(8,128)(2,1)S(1)} %get-tuple-element.23.refs_0_.refs_1_, bf16[256,1024]{1,0:T(8,128)(2,1)S(1)} %collective-permute-done.refs_1_.refs_2_, ...), custom_call_target="tpu_custom_call" | custom-call | flops 1 | bytes 1 | tf_op jit(solution)/shard_map/level_forward/pallas_call | solution.py:131
  37.9 2.7 %collective-permute-start.14 = (bf16[1,64,1024]{2,1,0:T(8,128)(2,1)S(1)}, bf16[1,64,1024]{2,1,0:T(8,128)(2,1)S(1)}, u32[]{:S(2)}, u32[]{:S(2)}) collective-permute-start(bf16[1,64,1024]{2,1,0:T(8,128)(2,1)S(1)} %get-tuple-element.36), channel_id=1, source_target_pairs={{0,16},{8,24},{16,0},{24,8},{1,17},{9,25},{17,1},{25,9},{2,18},{10... | collective-permute-start | bytes 393224 | tf_op jit(solution)/shard_map/ppermute | solution.py:55
  41.6 4.7 %collective-permute-done.14 = bf16[1,64,1024]{2,1,0:T(8,128)(2,1)S(1)} collective-permute-done((bf16[1,64,1024]{2,1,0:T(8,128)(2,1)S(1)}, bf16[1,64,1024]{2,1,0:T(8,128)(2,1)S(1)}, u32[]{:S(2)}, u32[]{:S(2)}) %collective-permute-start.14) | collective-permute-done | bytes 131104 | tf_op jit(solution)/shard_map/ppermute | solution.py:55
  46.4 2.2 %backward.1.refs_0_ = bf16[2,64,1024]{2,1,0:T(8,128)(2,1)S(1)} custom-call(bf16[1,64,1024]{2,1,0:T(8,128)(2,1)S(1)} %add_convert_fusion.1.sums, bf16[64,1024]{1,0:T(8,128)(2,1)S(1)} %get-tuple-element.37.refs_0_, bf16[256,1024]{1,0:T(8,128)(2,1)S(1)} %get-tuple-element.23.refs_0_.refs_1_, bf16[256,1024]{1,0:T(8,128)(2,1)S(1)} %collective-permute-done.refs_1_.refs_2_, ...), custom_call_target="tpu_custom_call" | custom-call | flops 1 | bytes 1 | tf_op jit(solution)/shard_map/backward/pallas_call | solution.py:131
  48.6 1.2 %collective-permute-start.24 = (bf16[2,64,1024]{2,1,0:T(8,128)(2,1)S(1)}, bf16[2,64,1024]{2,1,0:T(8,128)(2,1)S(1)}, u32[]{:S(2)}, u32[]{:S(2)}) collective-permute-start(bf16[2,64,1024]{2,1,0:T(8,128)(2,1)S(1)} %backward.1.refs_0_), channel_id=1, source_target_pairs={{0,2},{1,5},{2,0},{3,7},{4,6},{5,1},{6,4},{7,3},{8,12},{9,11},{10,... | collective-permute-start | bytes 786440 | tf_op jit(solution)/shard_map/ppermute | solution.py:50
  49.7 1.6 %collective-permute-start.21 = (bf16[2,64,1024]{2,1,0:T(8,128)(2,1)S(1)}, bf16[2,64,1024]{2,1,0:T(8,128)(2,1)S(1)}, u32[]{:S(2)}, u32[]{:S(2)}) collective-permute-start(bf16[2,64,1024]{2,1,0:T(8,128)(2,1)S(1)} %backward.1.refs_0_), channel_id=1, source_target_pairs={{0,4},{1,3},{2,6},{3,1},{4,0},{5,7},{6,2},{7,5},{8,10},{9,13},{10,... | collective-permute-start | bytes 786440 | tf_op jit(solution)/shard_map/ppermute | solution.py:50
  51.4 5.4 %collective-permute-done.24.refs_4_ = bf16[2,64,1024]{2,1,0:T(8,128)(2,1)S(1)} collective-permute-done((bf16[2,64,1024]{2,1,0:T(8,128)(2,1)S(1)}, bf16[2,64,1024]{2,1,0:T(8,128)(2,1)S(1)}, u32[]{:S(2)}, u32[]{:S(2)}) %collective-permute-start.24) | collective-permute-done | bytes 262176 | tf_op jit(solution)/shard_map/ppermute | solution.py:50
  57.3 1.7 %collective-permute-start.22 = (bf16[2,64,1024]{2,1,0:T(8,128)(2,1)S(1)}, bf16[2,64,1024]{2,1,0:T(8,128)(2,1)S(1)}, u32[]{:S(2)}, u32[]{:S(2)}) collective-permute-start(bf16[2,64,1024]{2,1,0:T(8,128)(2,1)S(1)} %collective-permute-done.21.refs_2_), channel_id=1, source_target_pairs={{0,2},{1,5},{2,0},{3,7},{4,6},{5,1},{6,4},{7,3},{8,12},{9,11},{10,... | collective-permute-start | bytes 786440 | tf_op jit(solution)/shard_map/ppermute | solution.py:50
  59.1 4.2 %leaf_backward.2 = (bf16[8,128,512]{2,1,0:T(8,128)(2,1)}, bf16[1,2,128,512]{3,2,1,0:T(8,128)(2,1)}) custom-call(s32[2,8]{1,0:T(2,128)S(1)} %bitcast.3, bf16[512,1024]{1,0:T(8,128)(2,1)S(1)} %get-tuple-element.25.refs_0_.y, bf16[8,128,128]{2,1,0:T(8,128)(2,1)S(1)} %copy-done.1, bf16[8,2,1024,128]{3,2,1,0:T(8,128)(2,1)S(1)} %copy-done, ...), custom_call_target="tpu_custom_call" | custom-call | flops 1 | bytes 1 | tf_op jit(solution)/shard_map/leaf_backward/pallas_call | solution.py:131
  63.7 1.5 %collective-permute-done.27.refs_1_ = bf16[2,64,1024]{2,1,0:T(8,128)(2,1)S(1)} collective-permute-done((bf16[2,64,1024]{2,1,0:T(8,128)(2,1)S(1)}, bf16[2,64,1024]{2,1,0:T(8,128)(2,1)S(1)}, u32[]{:S(2)}, u32[]{:S(2)}) %collective-permute-start.27) | collective-permute-done | bytes 262176 | tf_op jit(solution)/shard_map/ppermute | solution.py:39
  65.2 2.4 %leaf_backward.3 = (bf16[8,128,512]{2,1,0:T(8,128)(2,1)}, bf16[1,2,128,512]{3,2,1,0:T(8,128)(2,1)}) custom-call(s32[2,8]{1,0:T(2,128)S(1)} %bitcast.4, bf16[512,1024]{1,0:T(8,128)(2,1)S(1)} %get-tuple-element.25.refs_0_.y, bf16[8,128,128]{2,1,0:T(8,128)(2,1)S(1)} %copy-done.1, ...), custom_call_target="tpu_custom_call", output_to_operand_aliasing={{0}: (7, {}), {1}: (8, {})} | custom-call | flops 1 | bytes 1 | tf_op jit(solution)/shard_map/leaf_backward/pallas_call | solution.py:131
  (58 shorter events, 7.1 us)
Async XLA Ops:
  2.1 7.3 %collective-permute-start.3 = (bf16[256,1024]{1,0:T(8,128)(2,1)S(1)}, bf16[256,1024]{1,0:T(8,128)(2,1)S(1)}, u32[]{:S(2)}, u32[]{:S(2)}) collective-permute-start(bf16[256,1024]{1,0:T(8,128)(2,1)S(1)} %get-tuple-element.23.refs_0_.refs_1_), channel_id=1, source_target_pairs={{0,1},{1,0},{2,3},{3,2},{4,5},{5,4},{6,7},{7,6},{8,9},{9,8},{10,11... | collective-permute-start | bytes 1572872 | tf_op jit(solution)/shard_map/ppermute | solution.py:39
  2.7 10.4 %collective-permute-start = (bf16[256,1024]{1,0:T(8,128)(2,1)S(1)}, bf16[256,1024]{1,0:T(8,128)(2,1)S(1)}, u32[]{:S(2)}, u32[]{:S(2)}) collective-permute-start(bf16[256,1024]{1,0:T(8,128)(2,1)S(1)} %get-tuple-element.23.refs_0_.refs_1_), channel_id=1, source_target_pairs={{0,4},{1,3},{2,6},{3,1},{4,0},{5,7},{6,2},{7,5},{8,10},{9,13},{10,... | collective-permute-start | bytes 1572872 | tf_op jit(solution)/shard_map/ppermute | solution.py:50
  9.6 9.2 %collective-permute-start.4 = (bf16[2,2,64,1024]{3,2,1,0:T(8,128)(2,1)S(1)}, bf16[2,2,64,1024]{3,2,1,0:T(8,128)(2,1)S(1)}, u32[]{:S(2)}, u32[]{:S(2)}) collective-permute-start(bf16[2,2,64,1024]{3,2,1,0:T(8,128)(2,1)S(1)} %joined.1), channel_id=1, source_target_pairs={{0,2},{1,5},{2,0},{3,7},{4,6},{5,1},{6,4},{7,3},{8,12},{9,11},{10,... | collective-permute-start | bytes 1572872 | tf_op jit(solution)/shard_map/ppermute | solution.py:50
  12.9 5.9 %collective-permute-start.6 = (bf16[2,2,64,1024]{3,2,1,0:T(8,128)(2,1)S(1)}, bf16[2,2,64,1024]{3,2,1,0:T(8,128)(2,1)S(1)}, u32[]{:S(2)}, u32[]{:S(2)}) collective-permute-start(bf16[2,2,64,1024]{3,2,1,0:T(8,128)(2,1)S(1)} %get-tuple-element.32), channel_id=1, source_target_pairs={{0,1},{1,0},{2,3},{3,2},{4,5},{5,4},{6,7},{7,6},{8,9},{9,8},{10,11... | collective-permute-start | bytes 1572872 | tf_op jit(solution)/shard_map/ppermute | solution.py:39
  13.0 14.3 %collective-permute-start.8 = (bf16[256,1024]{1,0:T(8,128)(2,1)S(1)}, bf16[256,1024]{1,0:T(8,128)(2,1)S(1)}, u32[]{:S(2)}, u32[]{:S(2)}) collective-permute-start(bf16[256,1024]{1,0:T(8,128)(2,1)S(1)} %collective-permute-done.refs_1_.refs_2_), channel_id=1, source_target_pairs={{0,8},{8,0},{16,24},{24,16},{1,9},{9,1},{17,25},{25,17},{2,10},{10... | collective-permute-start | bytes 1572872 | tf_op jit(solution)/shard_map/ppermute | solution.py:55
  14.9 12.4 %collective-permute-start.11 = (bf16[256,1024]{1,0:T(8,128)(2,1)S(1)}, bf16[256,1024]{1,0:T(8,128)(2,1)S(1)}, u32[]{:S(2)}, u32[]{:S(2)}) collective-permute-start(bf16[256,1024]{1,0:T(8,128)(2,1)S(1)} %collective-permute-done.refs_1_.refs_2_), channel_id=1, source_target_pairs={{0,2},{1,5},{2,0},{3,7},{4,6},{5,1},{6,4},{7,3},{8,12},{9,11},{10,... | collective-permute-start | bytes 1572872 | tf_op jit(solution)/shard_map/ppermute | solution.py:50
  18.8 9.0 %collective-permute-start.5 = (bf16[256,1024]{1,0:T(8,128)(2,1)S(1)}, bf16[256,1024]{1,0:T(8,128)(2,1)S(1)}, u32[]{:S(2)}, u32[]{:S(2)}) collective-permute-start(bf16[256,1024]{1,0:T(8,128)(2,1)S(1)} %collective-permute-done.refs_1_.refs_2_), channel_id=1, source_target_pairs={{0,1},{1,0},{2,3},{3,2},{4,5},{5,4},{6,7},{7,6},{8,9},{9,8},{10,11... | collective-permute-start | bytes 1572872 | tf_op jit(solution)/shard_map/ppermute | solution.py:39
  19.0 8.9 %collective-permute-start.7 = (bf16[1,2,64,1024]{3,2,1,0:T(8,128)(2,1)S(1)}, bf16[1,2,64,1024]{3,2,1,0:T(8,128)(2,1)S(1)}, u32[]{:S(2)}, u32[]{:S(2)}) collective-permute-start(bf16[1,2,64,1024]{3,2,1,0:T(8,128)(2,1)S(1)} %add_convert_fusion), channel_id=1, source_target_pairs={{0,4},{1,3},{2,6},{3,1},{4,0},{5,7},{6,2},{7,5},{8,10},{9,13},{10,... | collective-permute-start | bytes 786440 | tf_op jit(solution)/shard_map/ppermute | solution.py:50
  20.4 10.6 %collective-permute-start.10 = (bf16[144,1024]{1,0:T(8,128)(2,1)S(1)}, bf16[144,1024]{1,0:T(8,128)(2,1)S(1)}, u32[]{:S(2)}, u32[]{:S(2)}) collective-permute-start(bf16[144,1024]{1,0:T(8,128)(2,1)S(1)} %get-tuple-element.39.refs_9_), channel_id=1, source_target_pairs={{0,4},{1,3},{2,6},{3,1},{4,0},{5,7},{6,2},{7,5},{8,10},{9,13},{10,... | collective-permute-start | bytes 884744 | tf_op jit(solution)/shard_map/ppermute | solution.py:50
  27.4 9.0 %collective-permute-start.12 = (bf16[256,1024]{1,0:T(8,128)(2,1)S(1)}, bf16[256,1024]{1,0:T(8,128)(2,1)S(1)}, u32[]{:S(2)}, u32[]{:S(2)}) collective-permute-start(bf16[256,1024]{1,0:T(8,128)(2,1)S(1)} %collective-permute-done.8.value.refs_2_.refs_3_), channel_id=1, source_target_pairs={{0,1},{1,0},{2,3},{3,2},{4,5},{5,4},{6,7},{7,6},{8,9},{9,8},{10,11... | collective-permute-start | bytes 1572872 | tf_op jit(solution)/shard_map/ppermute | solution.py:39
  27.4 9.0 %collective-permute-start.13 = (bf16[256,1024]{1,0:T(8,128)(2,1)S(1)}, bf16[256,1024]{1,0:T(8,128)(2,1)S(1)}, u32[]{:S(2)}, u32[]{:S(2)}) collective-permute-start(bf16[256,1024]{1,0:T(8,128)(2,1)S(1)} %collective-permute-done.11.value.refs_3_.refs_4_), channel_id=1, source_target_pairs={{0,1},{1,0},{2,3},{3,2},{4,5},{5,4},{6,7},{7,6},{8,9},{9,8},{10,11... | collective-permute-start | bytes 1572872 | tf_op jit(solution)/shard_map/ppermute | solution.py:39
  28.0 8.3 %collective-permute-start.9 = (bf16[2,64,1024]{2,1,0:T(8,128)(2,1)S(1)}, bf16[2,64,1024]{2,1,0:T(8,128)(2,1)S(1)}, u32[]{:S(2)}, u32[]{:S(2)}) collective-permute-start(bf16[2,64,1024]{2,1,0:T(8,128)(2,1)S(1)} %first.1.ours), channel_id=1, source_target_pairs={{0,8},{8,0},{16,24},{24,16},{1,9},{9,1},{17,25},{25,17},{2,10},{10... | collective-permute-start | bytes 786440 | tf_op jit(solution)/shard_map/ppermute | solution.py:55
  29.7 10.9 %collective-permute-start.15 = (bf16[144,1024]{1,0:T(8,128)(2,1)S(1)}, bf16[144,1024]{1,0:T(8,128)(2,1)S(1)}, u32[]{:S(2)}, u32[]{:S(2)}) collective-permute-start(bf16[144,1024]{1,0:T(8,128)(2,1)S(1)} %get-tuple-element.39.refs_9_), channel_id=1, source_target_pairs={{0,2},{1,5},{2,0},{3,7},{4,6},{5,1},{6,4},{7,3},{8,12},{9,11},{10,... | collective-permute-start | bytes 884744 | tf_op jit(solution)/shard_map/ppermute | solution.py:50
  31.0 9.6 %collective-permute-start.16 = (bf16[144,1024]{1,0:T(8,128)(2,1)S(1)}, bf16[144,1024]{1,0:T(8,128)(2,1)S(1)}, u32[]{:S(2)}, u32[]{:S(2)}) collective-permute-start(bf16[144,1024]{1,0:T(8,128)(2,1)S(1)} %collective-permute-done.10.refs_10_), channel_id=1, source_target_pairs={{0,2},{1,5},{2,0},{3,7},{4,6},{5,1},{6,4},{7,3},{8,12},{9,11},{10,... | collective-permute-start | bytes 884744 | tf_op jit(solution)/shard_map/ppermute | solution.py:50
  37.9 8.3 %collective-permute-start.14 = (bf16[1,64,1024]{2,1,0:T(8,128)(2,1)S(1)}, bf16[1,64,1024]{2,1,0:T(8,128)(2,1)S(1)}, u32[]{:S(2)}, u32[]{:S(2)}) collective-permute-start(bf16[1,64,1024]{2,1,0:T(8,128)(2,1)S(1)} %get-tuple-element.36), channel_id=1, source_target_pairs={{0,16},{8,24},{16,0},{24,8},{1,17},{9,25},{17,1},{25,9},{2,18},{10... | collective-permute-start | bytes 393224 | tf_op jit(solution)/shard_map/ppermute | solution.py:55
  40.6 5.7 %collective-permute-start.19 = (bf16[144,1024]{1,0:T(8,128)(2,1)S(1)}, bf16[144,1024]{1,0:T(8,128)(2,1)S(1)}, u32[]{:S(2)}, u32[]{:S(2)}) collective-permute-start(bf16[144,1024]{1,0:T(8,128)(2,1)S(1)} %collective-permute-done.15.refs_11_), channel_id=1, source_target_pairs={{0,1},{1,0},{2,3},{3,2},{4,5},{5,4},{6,7},{7,6},{8,9},{9,8},{10,11... | collective-permute-start | bytes 884744 | tf_op jit(solution)/shard_map/ppermute | solution.py:39
  40.6 5.7 %collective-permute-start.20 = (bf16[144,1024]{1,0:T(8,128)(2,1)S(1)}, bf16[144,1024]{1,0:T(8,128)(2,1)S(1)}, u32[]{:S(2)}, u32[]{:S(2)}) collective-permute-start(bf16[144,1024]{1,0:T(8,128)(2,1)S(1)} %collective-permute-done.16.refs_12_), channel_id=1, source_target_pairs={{0,1},{1,0},{2,3},{3,2},{4,5},{5,4},{6,7},{7,6},{8,9},{9,8},{10,11... | collective-permute-start | bytes 884744 | tf_op jit(solution)/shard_map/ppermute | solution.py:39
  41.1 5.2 %collective-permute-start.17 = (bf16[144,1024]{1,0:T(8,128)(2,1)S(1)}, bf16[144,1024]{1,0:T(8,128)(2,1)S(1)}, u32[]{:S(2)}, u32[]{:S(2)}) collective-permute-start(bf16[144,1024]{1,0:T(8,128)(2,1)S(1)} %get-tuple-element.39.refs_9_), channel_id=1, source_target_pairs={{0,1},{1,0},{2,3},{3,2},{4,5},{5,4},{6,7},{7,6},{8,9},{9,8},{10,11... | collective-permute-start | bytes 884744 | tf_op jit(solution)/shard_map/ppermute | solution.py:39
  41.2 5.2 %collective-permute-start.18 = (bf16[144,1024]{1,0:T(8,128)(2,1)S(1)}, bf16[144,1024]{1,0:T(8,128)(2,1)S(1)}, u32[]{:S(2)}, u32[]{:S(2)}) collective-permute-start(bf16[144,1024]{1,0:T(8,128)(2,1)S(1)} %collective-permute-done.10.refs_10_), channel_id=1, source_target_pairs={{0,1},{1,0},{2,3},{3,2},{4,5},{5,4},{6,7},{7,6},{8,9},{9,8},{10,11... | collective-permute-start | bytes 884744 | tf_op jit(solution)/shard_map/ppermute | solution.py:39
  48.6 8.3 %collective-permute-start.24 = (bf16[2,64,1024]{2,1,0:T(8,128)(2,1)S(1)}, bf16[2,64,1024]{2,1,0:T(8,128)(2,1)S(1)}, u32[]{:S(2)}, u32[]{:S(2)}) collective-permute-start(bf16[2,64,1024]{2,1,0:T(8,128)(2,1)S(1)} %backward.1.refs_0_), channel_id=1, source_target_pairs={{0,2},{1,5},{2,0},{3,7},{4,6},{5,1},{6,4},{7,3},{8,12},{9,11},{10,... | collective-permute-start | bytes 786440 | tf_op jit(solution)/shard_map/ppermute | solution.py:50
  49.7 7.1 %collective-permute-start.21 = (bf16[2,64,1024]{2,1,0:T(8,128)(2,1)S(1)}, bf16[2,64,1024]{2,1,0:T(8,128)(2,1)S(1)}, u32[]{:S(2)}, u32[]{:S(2)}) collective-permute-start(bf16[2,64,1024]{2,1,0:T(8,128)(2,1)S(1)} %backward.1.refs_0_), channel_id=1, source_target_pairs={{0,4},{1,3},{2,6},{3,1},{4,0},{5,7},{6,2},{7,5},{8,10},{9,13},{10,... | collective-permute-start | bytes 786440 | tf_op jit(solution)/shard_map/ppermute | solution.py:50
  51.4 7.7 %collective-permute-start.23 = (bf16[2,64,1024]{2,1,0:T(8,128)(2,1)S(1)}, bf16[2,64,1024]{2,1,0:T(8,128)(2,1)S(1)}, u32[]{:S(2)}, u32[]{:S(2)}) collective-permute-start(bf16[2,64,1024]{2,1,0:T(8,128)(2,1)S(1)} %backward.1.refs_0_), channel_id=1, source_target_pairs={{0,1},{1,0},{2,3},{3,2},{4,5},{5,4},{6,7},{7,6},{8,9},{9,8},{10,11... | collective-permute-start | bytes 786440 | tf_op jit(solution)/shard_map/ppermute | solution.py:39
  56.8 2.3 %collective-permute-start.25 = (bf16[2,64,1024]{2,1,0:T(8,128)(2,1)S(1)}, bf16[2,64,1024]{2,1,0:T(8,128)(2,1)S(1)}, u32[]{:S(2)}, u32[]{:S(2)}) collective-permute-start(bf16[2,64,1024]{2,1,0:T(8,128)(2,1)S(1)} %collective-permute-done.24.refs_4_), channel_id=1, source_target_pairs={{0,1},{1,0},{2,3},{3,2},{4,5},{5,4},{6,7},{7,6},{8,9},{9,8},{10,11... | collective-permute-start | bytes 786440 | tf_op jit(solution)/shard_map/ppermute | solution.py:39
  57.3 6.4 %collective-permute-start.22 = (bf16[2,64,1024]{2,1,0:T(8,128)(2,1)S(1)}, bf16[2,64,1024]{2,1,0:T(8,128)(2,1)S(1)}, u32[]{:S(2)}, u32[]{:S(2)}) collective-permute-start(bf16[2,64,1024]{2,1,0:T(8,128)(2,1)S(1)} %collective-permute-done.21.refs_2_), channel_id=1, source_target_pairs={{0,2},{1,5},{2,0},{3,7},{4,6},{5,1},{6,4},{7,3},{8,12},{9,11},{10,... | collective-permute-start | bytes 786440 | tf_op jit(solution)/shard_map/ppermute | solution.py:50
  (10 other events, 51.4 us)

commit v8 on v7

--- a/solution.py
+++ b/solution.py
@@ -197,7 +197,7 @@
 
 
 def leaf_forward_call(mask, leaves, couple, sep_rhs, slots, layers, apart):
-    first = len(leaves) == 2
+    first = apart
     blocks, levels, sep_rows, block_rows = couple.shape
     own_rows, rhs_cols = sep_rhs.shape[1:]
     planes = sep_rows // own_rows
@@ -211,7 +211,9 @@
         if first:
             rhs, inverse, couple, own_rhs, y, *parts, scaled, turned = refs
         else:
-            y, couple, own_rhs, *parts, scaled, turned = refs
+            y, inverse, couple, own_rhs, lower_turned, *parts, scaled, turned = refs
+            for b in range(blocks):
+                lower_turned[b] = lower_unit(inverse[b].astype(F32), 0).T.astype(BF16)
         me, layer_id = places()
         order = slot_blocks(planes)
         if first:
@@ -248,7 +250,7 @@
                         parts[1][at - half, level, :, lanes] = value
 
     part = jax.ShapeDtypeStruct((len(slots) // 2, levels, cols, sep_rows), BF16)
-    y_shape = [jax.ShapeDtypeStruct((rhs_cols, width), BF16)] if first else []
+    y_shape = [jax.ShapeDtypeStruct((rhs_cols, width) if first else leaves[1].shape, BF16)]
     scratch = [pltpu.VMEM((levels, here, width + own_rows), BF16), pltpu.VMEM((rhs_cols, own_rows), BF16)]
     arrays = [mask, *leaves, couple, sep_rhs]
     one = jax.ShapeDtypeStruct((len(slots) // 2, cols, sep_rows), BF16)
@@ -381,7 +383,7 @@
     return vmem_call(kernel, arrays, shapes, scratch, "backward")[0]
 
 
-def leaf_backward_call(mask, y, inverse, couple, diag, above, groups, before, own_rows):
+def leaf_backward_call(mask, y, turned, couple, diag, above, groups, before, own_rows):
     blocks, levels, sep_rows, block_rows = couple.shape
     rhs_cols, width = y.shape
     planes = sep_rows // own_rows
@@ -393,7 +395,7 @@
     steps = blocks // pair
     kept = len(before)
 
-    def kernel(mask, y, inverse, couple, diag, *refs):
+    def kernel(mask, y, turned, couple, diag, *refs):
         pieces, refs = dict(zip(slots, refs)), refs[len(slots) + kept :]
         leaf_to, sep_to, whole, ys, leaf_out, sep_out, sems = refs
         me = places()[0]
@@ -435,15 +437,14 @@
                 place = slice(at * block_rows, (at + 1) * block_rows)
                 scale = 1.0 / diag[at : at + 1]
                 target = (ys[:, place].astype(F32) * scale - terms[b]).astype(BF16)
-                lower = lower_unit(inverse[at].astype(F32), 0).T.astype(BF16)
-                leaf_out[at] = nt(lower, target).astype(BF16)
+                leaf_out[at] = nt(turned[at], target).astype(BF16)
             at = slice(step * pair, (step + 1) * pair)
             for j in range(len(groups)):
                 store(leaf_out.at[at, :, j * size : (j + 1) * size], leaf_to.at[at, :, lanes[j]])
         for copy in stores:
             copy.wait()
 
-    arrays = [mask, y, inverse, couple, diag, *[above[slot] for slot in slots], *before]
+    arrays = [mask, y, turned, couple, diag, *[above[slot] for slot in slots], *before]
     shapes = [
         jax.ShapeDtypeStruct((blocks, block_rows, rhs_cols), BF16),
         jax.ShapeDtypeStruct((1, levels, own_rows, rhs_cols), BF16),
@@ -508,7 +509,7 @@
     )
     own_crossed = [swap_core(own[0])] if four else []
     high = [joined_call(keep, [swap_core(part) for part in send], own_crossed)]
-    keep, send = leaf_forward_call(mask, [leaf_y], leaf_couple, sep_rhs, lows, layers, False)
+    turned, keep, send = leaf_forward_call(mask, [leaf_y, leaf_inverse], leaf_couple, sep_rhs, lows, layers, False)
     low = [keep, swap_core(send)]
     parts, arrived = scatter_sum(low, high)
     seen = []
@@ -554,7 +555,7 @@
         if level == 1 and four:
             last = last + [swap_link(last_near, 0), *[swap_core(piece) for piece in after_all([last[0], last_near], y)]]
     answers = backward_call(planes, sums, solved, groups)
-    leaves = [mask, leaf_y, leaf_inverse, leaf_couple, leaf_diag]
+    leaves = [mask, leaf_y, turned, leaf_couple, leaf_diag]
     if not four or 2 * answers.shape[1] != LANES:
         above = dict(enumerate(gather(answers)))
         return tuple(leaf_backward_call(*leaves, above, [list(range(planes))], [], own_rows))

time: 67.8 us -> 68.8 us (1.015)
  waiting for transfers between devices: 26.9 us -> 28.8 us
  starting transfers between devices: 23.7 us -> 22.8 us
    ppermute x15, waiting for transfers between devices: 2.96 us -> 3.96 us  [swap_core(): return lax.ppermute(value, 'plane', [(i, i ^ 1) for i in range(planes)])]
    ppermute x10, waiting for transfers between devices: 8.31 us -> 9.27 us  [swap_link(): return lax.ppermute(value, ('layer', 'plane'), pairs)]
    ppermute x10, starting transfers between devices: 14.3 us -> 13.4 us  [swap_link(): return lax.ppermute(value, ('layer', 'plane'), pairs)]
  transfers between devices with their start and end apart: 28 -> 28, of which waited for: 9 -> 11; matrix products, arithmetic and copies ran while one was open for 0% -> 0% of each run, Pallas kernels for 15% -> 15%
where the time goes in v8:
time: 68.8 us; the launch traced here: 68.6 us
  waiting for transfers between devices  28.8 us (42%)
  starting transfers between devices  22.8 us (33%)
  Pallas kernels  16 us (23%)
  between operations  0.86 us (1%)
    pallas_call x12, Pallas kernels, kernel_call(): pl.pallas_call(kernel, in_specs=[pl.BlockSpec(memory_space=space) for spa...  16 us
    ppermute x3, waiting for transfers between devices, swap_layer(): lax.ppermute(value, 'layer', [(i, i ^ 1 << stride) for i in range(layers)])  15.6 us
    ppermute x10, starting transfers between devices, swap_link(): return lax.ppermute(value, ('layer', 'plane'), pairs)  13.4 us
    ppermute x10, waiting for transfers between devices, swap_link(): return lax.ppermute(value, ('layer', 'plane'), pairs)  9.27 us
    ppermute x3, starting transfers between devices, swap_layer(): lax.ppermute(value, 'layer', [(i, i ^ 1 << stride) for i in range(layers)])  6.19 us
    ppermute x15, waiting for transfers between devices, swap_core(): return lax.ppermute(value, 'plane', [(i, i ^ 1) for i in range(planes)])  3.96 us
    ppermute x15, starting transfers between devices, swap_core(): return lax.ppermute(value, 'plane', [(i, i ^ 1) for i in range(planes)])  3.21 us
  transfers between devices with their start and end apart: 28, of which 11 were waited for; matrix products, arithmetic and copies ran while one was open for 0% of the time, Pallas kernels for 15%

profile of v8, /device:TPU:0, one launch (start us, length us, event | category | flops | bytes accessed | tf_op | source)
XLA Modules:
  0.0 68.6 jit_solution(1932666156363238909)
XLA Ops:
  0.7 1.5 %collect.1 = (bf16[256,1024]{1,0:T(8,128)(2,1)S(1)}, bf16[144,1024]{1,0:T(8,128)(2,1)S(1)}) custom-call(bf16[3,128,1024]{2,1,0:T(8,128)(2,1)} %inverse.1, bf16[3,1,128,1024]{3,2,1,0:T(8,128)(2,1)} %couple.3, f32[3,128]{1,0:T(4,128)} %diag_in.1), custom_call_target="tpu_custom_call" | custom-call | flops 20000000000 | bytes 1 | tf_op jit(solution)/shard_map/collect/pallas_call | solution.py:131
  2.7 2.6 %collective-permute-start = (bf16[256,1024]{1,0:T(8,128)(2,1)S(1)}, bf16[256,1024]{1,0:T(8,128)(2,1)S(1)}, u32[]{:S(2)}, u32[]{:S(2)}) collective-permute-start(bf16[256,1024]{1,0:T(8,128)(2,1)S(1)} %get-tuple-element.24.refs_0_.refs_1_), channel_id=1, source_target_pairs={{0,4},{1,3},{2,6},{3,1},{4,0},{5,7},{6,2},{7,5},{8,10},{9,13},{10,... | collective-permute-start | bytes 1572872 | tf_op jit(solution)/shard_map/ppermute | solution.py:50
  5.3 2.2 %leaf_forward.2 = (bf16[512,1024]{1,0:T(8,128)(2,1)S(1)}, bf16[2,2,64,1024]{3,2,1,0:T(8,128)(2,1)S(1)}, bf16[2,64,1024]{2,1,0:T(8,128)(2,1)S(1)}, bf16[2,64,1024]{2,1,0:T(8,128)(2,1)S(1)}) custom-call(s32[2,8]{1,0:T(2,128)S(1)} %bitcast.1, bf16[8,128,512]{2,1,0:T(8,128)(2,1)S(1)} %copy-done.2, bf16[8,128,128]{2,1,0:T(8,128)(2,1)S(1)} %copy-done.3, ...), custom_call_target="tpu_custom_call" | custom-call | flops 1 | bytes 1 | tf_op jit(solution)/shard_map/leaf_forward/pallas_call | solution.py:131
  8.1 1.0 %collective-permute-done.1.refs_0_ = bf16[2,64,1024]{2,1,0:T(8,128)(2,1)S(1)} collective-permute-done((bf16[2,64,1024]{2,1,0:T(8,128)(2,1)S(1)}, bf16[2,64,1024]{2,1,0:T(8,128)(2,1)S(1)}, u32[]{:S(2)}, u32[]{:S(2)}) %collective-permute-start.1) | collective-permute-done | bytes 262176 | tf_op jit(solution)/shard_map/ppermute | solution.py:39
  9.6 1.6 %collective-permute-start.4 = (bf16[2,2,64,1024]{3,2,1,0:T(8,128)(2,1)S(1)}, bf16[2,2,64,1024]{3,2,1,0:T(8,128)(2,1)S(1)}, u32[]{:S(2)}, u32[]{:S(2)}) collective-permute-start(bf16[2,2,64,1024]{3,2,1,0:T(8,128)(2,1)S(1)} %joined.1), channel_id=1, source_target_pairs={{0,2},{1,5},{2,0},{3,7},{4,6},{5,1},{6,4},{7,3},{8,12},{9,11},{10,... | collective-permute-start | bytes 1572872 | tf_op jit(solution)/shard_map/ppermute | solution.py:50
  11.1 1.8 %leaf_forward.3 = (bf16[8,128,128]{2,1,0:T(8,128)(2,1)S(1)}, bf16[2,2,64,1024]{3,2,1,0:T(8,128)(2,1)S(1)}, bf16[2,2,64,1024]{3,2,1,0:T(8,128)(2,1)S(1)}) custom-call(s32[2,8]{1,0:T(2,128)S(1)} %bitcast.2, bf16[512,1024]{1,0:T(8,128)(2,1)S(1)} %get-tuple-element.26.refs_0_.y, bf16[8,128,128]{2,1,0:T(8,128)(2,1)S(1)} %copy-done.3, ...), custom_call_target="tpu_custom_call" | custom-call | flops 1 | bytes 1 | tf_op jit(solution)/shard_map/leaf_forward/pallas_call | solution.py:131
  13.0 1.9 %collective-permute-start.8 = (bf16[256,1024]{1,0:T(8,128)(2,1)S(1)}, bf16[256,1024]{1,0:T(8,128)(2,1)S(1)}, u32[]{:S(2)}, u32[]{:S(2)}) collective-permute-start(bf16[256,1024]{1,0:T(8,128)(2,1)S(1)} %collective-permute-done.refs_1_.refs_2_), channel_id=1, source_target_pairs={{0,8},{8,0},{16,24},{24,16},{1,9},{9,1},{17,25},{25,17},{2,10},{10... | collective-permute-start | bytes 1572872 | tf_op jit(solution)/shard_map/ppermute | solution.py:55
  14.9 1.5 %collective-permute-start.11 = (bf16[256,1024]{1,0:T(8,128)(2,1)S(1)}, bf16[256,1024]{1,0:T(8,128)(2,1)S(1)}, u32[]{:S(2)}, u32[]{:S(2)}) collective-permute-start(bf16[256,1024]{1,0:T(8,128)(2,1)S(1)} %collective-permute-done.refs_1_.refs_2_), channel_id=1, source_target_pairs={{0,2},{1,5},{2,0},{3,7},{4,6},{5,1},{6,4},{7,3},{8,12},{9,11},{10,... | collective-permute-start | bytes 1572872 | tf_op jit(solution)/shard_map/ppermute | solution.py:50
  16.4 2.4 %collective-permute-done.4.refs_2_ = bf16[2,2,64,1024]{3,2,1,0:T(8,128)(2,1)S(1)} collective-permute-done((bf16[2,2,64,1024]{3,2,1,0:T(8,128)(2,1)S(1)}, bf16[2,2,64,1024]{3,2,1,0:T(8,128)(2,1)S(1)}, u32[]{:S(2)}, u32[]{:S(2)}) %collective-permute-start.4) | collective-permute-done | bytes 524320 | tf_op jit(solution)/shard_map/ppermute | solution.py:50
  19.0 1.4 %collective-permute-start.7 = (bf16[1,2,64,1024]{3,2,1,0:T(8,128)(2,1)S(1)}, bf16[1,2,64,1024]{3,2,1,0:T(8,128)(2,1)S(1)}, u32[]{:S(2)}, u32[]{:S(2)}) collective-permute-start(bf16[1,2,64,1024]{3,2,1,0:T(8,128)(2,1)S(1)} %add_convert_fusion), channel_id=1, source_target_pairs={{0,4},{1,3},{2,6},{3,1},{4,0},{5,7},{6,2},{7,5},{8,10},{9,13},{10,... | collective-permute-start | bytes 786440 | tf_op jit(solution)/shard_map/ppermute | solution.py:50
  21.1 6.3 %collective-permute-done.8.value.refs_2_.refs_3_ = bf16[256,1024]{1,0:T(8,128)(2,1)S(1)} collective-permute-done((bf16[256,1024]{1,0:T(8,128)(2,1)S(1)}, bf16[256,1024]{1,0:T(8,128)(2,1)S(1)}, u32[]{:S(2)}, u32[]{:S(2)}) %collective-permute-start.8) | collective-permute-done | bytes 524320 | tf_op jit(solution)/shard_map/ppermute | solution.py:55
  28.0 1.6 %collective-permute-start.9 = (bf16[2,64,1024]{2,1,0:T(8,128)(2,1)S(1)}, bf16[2,64,1024]{2,1,0:T(8,128)(2,1)S(1)}, u32[]{:S(2)}, u32[]{:S(2)}) collective-permute-start(bf16[2,64,1024]{2,1,0:T(8,128)(2,1)S(1)} %first.1.ours), channel_id=1, source_target_pairs={{0,8},{8,0},{16,24},{24,16},{1,9},{9,1},{17,25},{25,17},{2,10},{10... | collective-permute-start | bytes 786440 | tf_op jit(solution)/shard_map/ppermute | solution.py:55
  29.7 1.2 %collective-permute-start.15 = (bf16[144,1024]{1,0:T(8,128)(2,1)S(1)}, bf16[144,1024]{1,0:T(8,128)(2,1)S(1)}, u32[]{:S(2)}, u32[]{:S(2)}) collective-permute-start(bf16[144,1024]{1,0:T(8,128)(2,1)S(1)} %get-tuple-element.41.refs_9_), channel_id=1, source_target_pairs={{0,2},{1,5},{2,0},{3,7},{4,6},{5,1},{6,4},{7,3},{8,12},{9,11},{10,... | collective-permute-start | bytes 884744 | tf_op jit(solution)/shard_map/ppermute | solution.py:50
  31.7 4.6 %collective-permute-done.9.theirs = bf16[2,64,1024]{2,1,0:T(8,128)(2,1)S(1)} collective-permute-done((bf16[2,64,1024]{2,1,0:T(8,128)(2,1)S(1)}, bf16[2,64,1024]{2,1,0:T(8,128)(2,1)S(1)}, u32[]{:S(2)}, u32[]{:S(2)}) %collective-permute-start.9) | collective-permute-done | bytes 262176 | tf_op jit(solution)/shard_map/ppermute | solution.py:55
  36.4 1.5 %level_forward.1 = (bf16[64,1024]{1,0:T(8,128)(2,1)S(1)}, bf16[1,64,1024]{2,1,0:T(8,128)(2,1)S(1)}) custom-call(bf16[2,64,1024]{2,1,0:T(8,128)(2,1)S(1)} %added.1.sums, bf16[256,1024]{1,0:T(8,128)(2,1)S(1)} %get-tuple-element.24.refs_0_.refs_1_, bf16[256,1024]{1,0:T(8,128)(2,1)S(1)} %collective-permute-done.refs_1_.refs_2_, ...), custom_call_target="tpu_custom_call" | custom-call | flops 1 | bytes 1 | tf_op jit(solution)/shard_map/level_forward/pallas_call | solution.py:131
  37.9 2.6 %collective-permute-start.14 = (bf16[1,64,1024]{2,1,0:T(8,128)(2,1)S(1)}, bf16[1,64,1024]{2,1,0:T(8,128)(2,1)S(1)}, u32[]{:S(2)}, u32[]{:S(2)}) collective-permute-start(bf16[1,64,1024]{2,1,0:T(8,128)(2,1)S(1)} %get-tuple-element.38), channel_id=1, source_target_pairs={{0,16},{8,24},{16,0},{24,8},{1,17},{9,25},{17,1},{25,9},{2,18},{10... | collective-permute-start | bytes 393224 | tf_op jit(solution)/shard_map/ppermute | solution.py:55
  41.6 4.7 %collective-permute-done.14 = bf16[1,64,1024]{2,1,0:T(8,128)(2,1)S(1)} collective-permute-done((bf16[1,64,1024]{2,1,0:T(8,128)(2,1)S(1)}, bf16[1,64,1024]{2,1,0:T(8,128)(2,1)S(1)}, u32[]{:S(2)}, u32[]{:S(2)}) %collective-permute-start.14) | collective-permute-done | bytes 131104 | tf_op jit(solution)/shard_map/ppermute | solution.py:55
  46.4 2.2 %backward.1.refs_0_ = bf16[2,64,1024]{2,1,0:T(8,128)(2,1)S(1)} custom-call(bf16[1,64,1024]{2,1,0:T(8,128)(2,1)S(1)} %add_convert_fusion.1.sums, bf16[64,1024]{1,0:T(8,128)(2,1)S(1)} %get-tuple-element.39.refs_0_, bf16[256,1024]{1,0:T(8,128)(2,1)S(1)} %get-tuple-element.24.refs_0_.refs_1_, bf16[256,1024]{1,0:T(8,128)(2,1)S(1)} %collective-permute-done.refs_1_.refs_2_, ...), custom_call_target="tpu_custom_call" | custom-call | flops 1 | bytes 1 | tf_op jit(solution)/shard_map/backward/pallas_call | solution.py:131
  48.5 1.1 %collective-permute-start.24 = (bf16[2,64,1024]{2,1,0:T(8,128)(2,1)S(1)}, bf16[2,64,1024]{2,1,0:T(8,128)(2,1)S(1)}, u32[]{:S(2)}, u32[]{:S(2)}) collective-permute-start(bf16[2,64,1024]{2,1,0:T(8,128)(2,1)S(1)} %backward.1.refs_0_), channel_id=1, source_target_pairs={{0,2},{1,5},{2,0},{3,7},{4,6},{5,1},{6,4},{7,3},{8,12},{9,11},{10,... | collective-permute-start | bytes 786440 | tf_op jit(solution)/shard_map/ppermute | solution.py:50
  49.7 2.1 %collective-permute-start.21 = (bf16[2,64,1024]{2,1,0:T(8,128)(2,1)S(1)}, bf16[2,64,1024]{2,1,0:T(8,128)(2,1)S(1)}, u32[]{:S(2)}, u32[]{:S(2)}) collective-permute-start(bf16[2,64,1024]{2,1,0:T(8,128)(2,1)S(1)} %backward.1.refs_0_), channel_id=1, source_target_pairs={{0,4},{1,3},{2,6},{3,1},{4,0},{5,7},{6,2},{7,5},{8,10},{9,13},{10,... | collective-permute-start | bytes 786440 | tf_op jit(solution)/shard_map/ppermute | solution.py:50
  51.8 6.0 %collective-permute-done.24.refs_4_ = bf16[2,64,1024]{2,1,0:T(8,128)(2,1)S(1)} collective-permute-done((bf16[2,64,1024]{2,1,0:T(8,128)(2,1)S(1)}, bf16[2,64,1024]{2,1,0:T(8,128)(2,1)S(1)}, u32[]{:S(2)}, u32[]{:S(2)}) %collective-permute-start.24) | collective-permute-done | bytes 262176 | tf_op jit(solution)/shard_map/ppermute | solution.py:50
  59.7 4.2 %leaf_backward.2 = (bf16[8,128,512]{2,1,0:T(8,128)(2,1)}, bf16[1,2,128,512]{3,2,1,0:T(8,128)(2,1)}) custom-call(s32[2,8]{1,0:T(2,128)S(1)} %bitcast.3, bf16[512,1024]{1,0:T(8,128)(2,1)S(1)} %get-tuple-element.26.refs_0_.y, bf16[8,128,128]{2,1,0:T(8,128)(2,1)S(1)} %get-tuple-element.27.turned, bf16[8,2,1024,128]{3,2,1,0:T(8,128)(2,1)S(1)} %copy-done, ...), custom_call_target="tpu_custom_call" | custom-call | flops 1 | bytes 1 | tf_op jit(solution)/shard_map/leaf_backward/pallas_call | solution.py:131
  64.7 1.5 %collective-permute-done.27.refs_1_ = bf16[2,64,1024]{2,1,0:T(8,128)(2,1)S(1)} collective-permute-done((bf16[2,64,1024]{2,1,0:T(8,128)(2,1)S(1)}, bf16[2,64,1024]{2,1,0:T(8,128)(2,1)S(1)}, u32[]{:S(2)}, u32[]{:S(2)}) %collective-permute-start.27) | collective-permute-done | bytes 262176 | tf_op jit(solution)/shard_map/ppermute | solution.py:39
  66.2 2.4 %leaf_backward.3 = (bf16[8,128,512]{2,1,0:T(8,128)(2,1)}, bf16[1,2,128,512]{3,2,1,0:T(8,128)(2,1)}) custom-call(s32[2,8]{1,0:T(2,128)S(1)} %bitcast.4, bf16[512,1024]{1,0:T(8,128)(2,1)S(1)} %get-tuple-element.26.refs_0_.y, bf16[8,128,128]{2,1,0:T(8,128)(2,1)S(1)} %get-tuple-element.27.turned, ...), custom_call_target="tpu_custom_call", output_to_operand_aliasing={{0}: (7, {}), {1}: (8, {})} | custom-call | flops 1 | bytes 1 | tf_op jit(solution)/shard_map/leaf_backward/pallas_call | solution.py:131
  (58 shorter events, 7.9 us)
Async XLA Ops:
  2.1 7.3 %collective-permute-start.3 = (bf16[256,1024]{1,0:T(8,128)(2,1)S(1)}, bf16[256,1024]{1,0:T(8,128)(2,1)S(1)}, u32[]{:S(2)}, u32[]{:S(2)}) collective-permute-start(bf16[256,1024]{1,0:T(8,128)(2,1)S(1)} %get-tuple-element.24.refs_0_.refs_1_), channel_id=1, source_target_pairs={{0,1},{1,0},{2,3},{3,2},{4,5},{5,4},{6,7},{7,6},{8,9},{9,8},{10,11... | collective-permute-start | bytes 1572872 | tf_op jit(solution)/shard_map/ppermute | solution.py:39
  2.7 10.4 %collective-permute-start = (bf16[256,1024]{1,0:T(8,128)(2,1)S(1)}, bf16[256,1024]{1,0:T(8,128)(2,1)S(1)}, u32[]{:S(2)}, u32[]{:S(2)}) collective-permute-start(bf16[256,1024]{1,0:T(8,128)(2,1)S(1)} %get-tuple-element.24.refs_0_.refs_1_), channel_id=1, source_target_pairs={{0,4},{1,3},{2,6},{3,1},{4,0},{5,7},{6,2},{7,5},{8,10},{9,13},{10,... | collective-permute-start | bytes 1572872 | tf_op jit(solution)/shard_map/ppermute | solution.py:50
  9.6 9.2 %collective-permute-start.4 = (bf16[2,2,64,1024]{3,2,1,0:T(8,128)(2,1)S(1)}, bf16[2,2,64,1024]{3,2,1,0:T(8,128)(2,1)S(1)}, u32[]{:S(2)}, u32[]{:S(2)}) collective-permute-start(bf16[2,2,64,1024]{3,2,1,0:T(8,128)(2,1)S(1)} %joined.1), channel_id=1, source_target_pairs={{0,2},{1,5},{2,0},{3,7},{4,6},{5,1},{6,4},{7,3},{8,12},{9,11},{10,... | collective-permute-start | bytes 1572872 | tf_op jit(solution)/shard_map/ppermute | solution.py:50
  12.9 5.9 %collective-permute-start.6 = (bf16[2,2,64,1024]{3,2,1,0:T(8,128)(2,1)S(1)}, bf16[2,2,64,1024]{3,2,1,0:T(8,128)(2,1)S(1)}, u32[]{:S(2)}, u32[]{:S(2)}) collective-permute-start(bf16[2,2,64,1024]{3,2,1,0:T(8,128)(2,1)S(1)} %get-tuple-element.34), channel_id=1, source_target_pairs={{0,1},{1,0},{2,3},{3,2},{4,5},{5,4},{6,7},{7,6},{8,9},{9,8},{10,11... | collective-permute-start | bytes 1572872 | tf_op jit(solution)/shard_map/ppermute | solution.py:39
  13.0 14.3 %collective-permute-start.8 = (bf16[256,1024]{1,0:T(8,128)(2,1)S(1)}, bf16[256,1024]{1,0:T(8,128)(2,1)S(1)}, u32[]{:S(2)}, u32[]{:S(2)}) collective-permute-start(bf16[256,1024]{1,0:T(8,128)(2,1)S(1)} %collective-permute-done.refs_1_.refs_2_), channel_id=1, source_target_pairs={{0,8},{8,0},{16,24},{24,16},{1,9},{9,1},{17,25},{25,17},{2,10},{10... | collective-permute-start | bytes 1572872 | tf_op jit(solution)/shard_map/ppermute | solution.py:55
  14.9 12.4 %collective-permute-start.11 = (bf16[256,1024]{1,0:T(8,128)(2,1)S(1)}, bf16[256,1024]{1,0:T(8,128)(2,1)S(1)}, u32[]{:S(2)}, u32[]{:S(2)}) collective-permute-start(bf16[256,1024]{1,0:T(8,128)(2,1)S(1)} %collective-permute-done.refs_1_.refs_2_), channel_id=1, source_target_pairs={{0,2},{1,5},{2,0},{3,7},{4,6},{5,1},{6,4},{7,3},{8,12},{9,11},{10,... | collective-permute-start | bytes 1572872 | tf_op jit(solution)/shard_map/ppermute | solution.py:50
  18.8 9.0 %collective-permute-start.5 = (bf16[256,1024]{1,0:T(8,128)(2,1)S(1)}, bf16[256,1024]{1,0:T(8,128)(2,1)S(1)}, u32[]{:S(2)}, u32[]{:S(2)}) collective-permute-start(bf16[256,1024]{1,0:T(8,128)(2,1)S(1)} %collective-permute-done.refs_1_.refs_2_), channel_id=1, source_target_pairs={{0,1},{1,0},{2,3},{3,2},{4,5},{5,4},{6,7},{7,6},{8,9},{9,8},{10,11... | collective-permute-start | bytes 1572872 | tf_op jit(solution)/shard_map/ppermute | solution.py:39
  19.0 8.9 %collective-permute-start.7 = (bf16[1,2,64,1024]{3,2,1,0:T(8,128)(2,1)S(1)}, bf16[1,2,64,1024]{3,2,1,0:T(8,128)(2,1)S(1)}, u32[]{:S(2)}, u32[]{:S(2)}) collective-permute-start(bf16[1,2,64,1024]{3,2,1,0:T(8,128)(2,1)S(1)} %add_convert_fusion), channel_id=1, source_target_pairs={{0,4},{1,3},{2,6},{3,1},{4,0},{5,7},{6,2},{7,5},{8,10},{9,13},{10,... | collective-permute-start | bytes 786440 | tf_op jit(solution)/shard_map/ppermute | solution.py:50
  20.4 10.5 %collective-permute-start.10 = (bf16[144,1024]{1,0:T(8,128)(2,1)S(1)}, bf16[144,1024]{1,0:T(8,128)(2,1)S(1)}, u32[]{:S(2)}, u32[]{:S(2)}) collective-permute-start(bf16[144,1024]{1,0:T(8,128)(2,1)S(1)} %get-tuple-element.41.refs_9_), channel_id=1, source_target_pairs={{0,4},{1,3},{2,6},{3,1},{4,0},{5,7},{6,2},{7,5},{8,10},{9,13},{10,... | collective-permute-start | bytes 884744 | tf_op jit(solution)/shard_map/ppermute | solution.py:50
  27.4 9.0 %collective-permute-start.12 = (bf16[256,1024]{1,0:T(8,128)(2,1)S(1)}, bf16[256,1024]{1,0:T(8,128)(2,1)S(1)}, u32[]{:S(2)}, u32[]{:S(2)}) collective-permute-start(bf16[256,1024]{1,0:T(8,128)(2,1)S(1)} %collective-permute-done.8.value.refs_2_.refs_3_), channel_id=1, source_target_pairs={{0,1},{1,0},{2,3},{3,2},{4,5},{5,4},{6,7},{7,6},{8,9},{9,8},{10,11... | collective-permute-start | bytes 1572872 | tf_op jit(solution)/shard_map/ppermute | solution.py:39
  27.4 9.0 %collective-permute-start.13 = (bf16[256,1024]{1,0:T(8,128)(2,1)S(1)}, bf16[256,1024]{1,0:T(8,128)(2,1)S(1)}, u32[]{:S(2)}, u32[]{:S(2)}) collective-permute-start(bf16[256,1024]{1,0:T(8,128)(2,1)S(1)} %collective-permute-done.11.value.refs_3_.refs_4_), channel_id=1, source_target_pairs={{0,1},{1,0},{2,3},{3,2},{4,5},{5,4},{6,7},{7,6},{8,9},{9,8},{10,11... | collective-permute-start | bytes 1572872 | tf_op jit(solution)/shard_map/ppermute | solution.py:39
  28.0 8.3 %collective-permute-start.9 = (bf16[2,64,1024]{2,1,0:T(8,128)(2,1)S(1)}, bf16[2,64,1024]{2,1,0:T(8,128)(2,1)S(1)}, u32[]{:S(2)}, u32[]{:S(2)}) collective-permute-start(bf16[2,64,1024]{2,1,0:T(8,128)(2,1)S(1)} %first.1.ours), channel_id=1, source_target_pairs={{0,8},{8,0},{16,24},{24,16},{1,9},{9,1},{17,25},{25,17},{2,10},{10... | collective-permute-start | bytes 786440 | tf_op jit(solution)/shard_map/ppermute | solution.py:55
  29.7 10.9 %collective-permute-start.15 = (bf16[144,1024]{1,0:T(8,128)(2,1)S(1)}, bf16[144,1024]{1,0:T(8,128)(2,1)S(1)}, u32[]{:S(2)}, u32[]{:S(2)}) collective-permute-start(bf16[144,1024]{1,0:T(8,128)(2,1)S(1)} %get-tuple-element.41.refs_9_), channel_id=1, source_target_pairs={{0,2},{1,5},{2,0},{3,7},{4,6},{5,1},{6,4},{7,3},{8,12},{9,11},{10,... | collective-permute-start | bytes 884744 | tf_op jit(solution)/shard_map/ppermute | solution.py:50
  30.9 9.7 %collective-permute-start.16 = (bf16[144,1024]{1,0:T(8,128)(2,1)S(1)}, bf16[144,1024]{1,0:T(8,128)(2,1)S(1)}, u32[]{:S(2)}, u32[]{:S(2)}) collective-permute-start(bf16[144,1024]{1,0:T(8,128)(2,1)S(1)} %collective-permute-done.10.refs_10_), channel_id=1, source_target_pairs={{0,2},{1,5},{2,0},{3,7},{4,6},{5,1},{6,4},{7,3},{8,12},{9,11},{10,... | collective-permute-start | bytes 884744 | tf_op jit(solution)/shard_map/ppermute | solution.py:50
  37.9 8.3 %collective-permute-start.14 = (bf16[1,64,1024]{2,1,0:T(8,128)(2,1)S(1)}, bf16[1,64,1024]{2,1,0:T(8,128)(2,1)S(1)}, u32[]{:S(2)}, u32[]{:S(2)}) collective-permute-start(bf16[1,64,1024]{2,1,0:T(8,128)(2,1)S(1)} %get-tuple-element.38), channel_id=1, source_target_pairs={{0,16},{8,24},{16,0},{24,8},{1,17},{9,25},{17,1},{25,9},{2,18},{10... | collective-permute-start | bytes 393224 | tf_op jit(solution)/shard_map/ppermute | solution.py:55
  40.6 5.7 %collective-permute-start.19 = (bf16[144,1024]{1,0:T(8,128)(2,1)S(1)}, bf16[144,1024]{1,0:T(8,128)(2,1)S(1)}, u32[]{:S(2)}, u32[]{:S(2)}) collective-permute-start(bf16[144,1024]{1,0:T(8,128)(2,1)S(1)} %collective-permute-done.15.refs_11_), channel_id=1, source_target_pairs={{0,1},{1,0},{2,3},{3,2},{4,5},{5,4},{6,7},{7,6},{8,9},{9,8},{10,11... | collective-permute-start | bytes 884744 | tf_op jit(solution)/shard_map/ppermute | solution.py:39
  40.6 5.7 %collective-permute-start.20 = (bf16[144,1024]{1,0:T(8,128)(2,1)S(1)}, bf16[144,1024]{1,0:T(8,128)(2,1)S(1)}, u32[]{:S(2)}, u32[]{:S(2)}) collective-permute-start(bf16[144,1024]{1,0:T(8,128)(2,1)S(1)} %collective-permute-done.16.refs_12_), channel_id=1, source_target_pairs={{0,1},{1,0},{2,3},{3,2},{4,5},{5,4},{6,7},{7,6},{8,9},{9,8},{10,11... | collective-permute-start | bytes 884744 | tf_op jit(solution)/shard_map/ppermute | solution.py:39
  41.1 5.2 %collective-permute-start.17 = (bf16[144,1024]{1,0:T(8,128)(2,1)S(1)}, bf16[144,1024]{1,0:T(8,128)(2,1)S(1)}, u32[]{:S(2)}, u32[]{:S(2)}) collective-permute-start(bf16[144,1024]{1,0:T(8,128)(2,1)S(1)} %get-tuple-element.41.refs_9_), channel_id=1, source_target_pairs={{0,1},{1,0},{2,3},{3,2},{4,5},{5,4},{6,7},{7,6},{8,9},{9,8},{10,11... | collective-permute-start | bytes 884744 | tf_op jit(solution)/shard_map/ppermute | solution.py:39
  41.2 5.2 %collective-permute-start.18 = (bf16[144,1024]{1,0:T(8,128)(2,1)S(1)}, bf16[144,1024]{1,0:T(8,128)(2,1)S(1)}, u32[]{:S(2)}, u32[]{:S(2)}) collective-permute-start(bf16[144,1024]{1,0:T(8,128)(2,1)S(1)} %collective-permute-done.10.refs_10_), channel_id=1, source_target_pairs={{0,1},{1,0},{2,3},{3,2},{4,5},{5,4},{6,7},{7,6},{8,9},{9,8},{10,11... | collective-permute-start | bytes 884744 | tf_op jit(solution)/shard_map/ppermute | solution.py:39
  48.5 9.2 %collective-permute-start.24 = (bf16[2,64,1024]{2,1,0:T(8,128)(2,1)S(1)}, bf16[2,64,1024]{2,1,0:T(8,128)(2,1)S(1)}, u32[]{:S(2)}, u32[]{:S(2)}) collective-permute-start(bf16[2,64,1024]{2,1,0:T(8,128)(2,1)S(1)} %backward.1.refs_0_), channel_id=1, source_target_pairs={{0,2},{1,5},{2,0},{3,7},{4,6},{5,1},{6,4},{7,3},{8,12},{9,11},{10,... | collective-permute-start | bytes 786440 | tf_op jit(solution)/shard_map/ppermute | solution.py:50
  49.7 8.1 %collective-permute-start.21 = (bf16[2,64,1024]{2,1,0:T(8,128)(2,1)S(1)}, bf16[2,64,1024]{2,1,0:T(8,128)(2,1)S(1)}, u32[]{:S(2)}, u32[]{:S(2)}) collective-permute-start(bf16[2,64,1024]{2,1,0:T(8,128)(2,1)S(1)} %backward.1.refs_0_), channel_id=1, source_target_pairs={{0,4},{1,3},{2,6},{3,1},{4,0},{5,7},{6,2},{7,5},{8,10},{9,13},{10,... | collective-permute-start | bytes 786440 | tf_op jit(solution)/shard_map/ppermute | solution.py:50
  51.8 6.9 %collective-permute-start.23 = (bf16[2,64,1024]{2,1,0:T(8,128)(2,1)S(1)}, bf16[2,64,1024]{2,1,0:T(8,128)(2,1)S(1)}, u32[]{:S(2)}, u32[]{:S(2)}) collective-permute-start(bf16[2,64,1024]{2,1,0:T(8,128)(2,1)S(1)} %backward.1.refs_0_), channel_id=1, source_target_pairs={{0,1},{1,0},{2,3},{3,2},{4,5},{5,4},{6,7},{7,6},{8,9},{9,8},{10,11... | collective-permute-start | bytes 786440 | tf_op jit(solution)/shard_map/ppermute | solution.py:39
  57.8 1.9 %collective-permute-start.26 = (bf16[2,64,1024]{2,1,0:T(8,128)(2,1)S(1)}, bf16[2,64,1024]{2,1,0:T(8,128)(2,1)S(1)}, u32[]{:S(2)}, u32[]{:S(2)}) collective-permute-start(bf16[2,64,1024]{2,1,0:T(8,128)(2,1)S(1)} %collective-permute-done.21.refs_2_), channel_id=1, source_target_pairs={{0,1},{1,0},{2,3},{3,2},{4,5},{5,4},{6,7},{7,6},{8,9},{9,8},{10,11... | collective-permute-start | bytes 786440 | tf_op jit(solution)/shard_map/ppermute | solution.py:39
  58.3 6.4 %collective-permute-start.22 = (bf16[2,64,1024]{2,1,0:T(8,128)(2,1)S(1)}, bf16[2,64,1024]{2,1,0:T(8,128)(2,1)S(1)}, u32[]{:S(2)}, u32[]{:S(2)}) collective-permute-start(bf16[2,64,1024]{2,1,0:T(8,128)(2,1)S(1)} %collective-permute-done.21.refs_2_), channel_id=1, source_target_pairs={{0,2},{1,5},{2,0},{3,7},{4,6},{5,1},{6,4},{7,3},{8,12},{9,11},{10,... | collective-permute-start | bytes 786440 | tf_op jit(solution)/shard_map/ppermute | solution.py:50
  (10 other events, 51.3 us)
